TPU v7x, 512 devices: a whole 4x8x8 slice. The times are simulated.
512 devices in a mesh: member: 16 (over y, core), space: 32 (over z, x).
Axes of the slice: x: 4, y: 8, z: 8, core: 2. Of those that a mesh axis runs over, the one named last changes fastest.
Arguments:
- prior_sample: float32 [256, 1048576], P('member', 'space'), may hold values from -6 to 6
- measured_point_location: int32 [512, 128], P('space'), may hold values from 0 to 32767
- measured_data: float32 [512, 128], P('space'), may hold values from -12 to 12
- measurement_noise_sigma: float32 [512, 128], P('space'), may hold values from 2 to 64
- measured_slots_used: int32 [32], P('space'), may hold values from 512 to 2048, as said below
Outputs:
- analysis: float32 [256, 1048576], P('member', 'space')
Inputs may be any that keep to these rules, and one draw needn't show every extreme that they name: measured_slots_used gives for each space block how many of its first slots are in use; some block uses all 2048 slots. `measured_point_location`: each index is a state point of the observation's own space block.
All inputs are finite; a program needn't handle non-finite values.
Results may differ from a plain program's by a relative error of at most 0.000088.
Values sent between devices are 32-bit elements; how exact they have to be, the bound alone decides.
No kernel may reach another device: no remote copies, remote signals or barrier semaphores. Data moves between devices by JAX's collectives and lax.ppermute only.
A program may use at most 64 MiB of HBM per device.

v0:
```python
import math

import jax
import jax.numpy as jnp
from jax import lax
from jax.sharding import Mesh
from jax.sharding import PartitionSpec as P

MEMBER = ("member_0", "member_1")
SPACE = ("space_0", "space_1")


def side_by_side(arrays, axis, split_dim, concat_dim, along):
    widths = [a.shape[along] for a in arrays]
    both = jnp.concatenate(arrays, axis=along)
    result = lax.all_to_all(both, axis, split_axis=split_dim, concat_axis=concat_dim, tiled=True)
    return tuple(jnp.split(result, [sum(widths[:k]) for k in range(1, len(widths))], axis=along))


def split_up(array, dim, size):
    before, after = (array.shape[:dim], array.shape[dim + 1 :])
    return jnp.moveaxis(array.reshape(*before, size, -1, *after), dim, 0)


def sent_and_summed(array, axis, dim):
    size = lax.axis_size(axis)
    parts = lax.all_to_all(split_up(array, dim, size), axis, 0, 0, tiled=True)
    return jnp.sum(parts, axis=0)


def sum_by_axis(array, axes, dim):
    far, near = axes
    own = sent_and_summed(split_up(array, dim, lax.axis_size(far)), near, dim + 1)
    return jnp.sum(lax.all_to_all(own, far, 0, 0, tiled=True), axis=0)


def rows_for(lines, size):
    spare = -lines.shape[0] % size
    if not spare:
        return lines
    return jnp.concatenate([lines, jnp.zeros((spare, *lines.shape[1:]), lines.dtype)])


def sent_to_all(array, axis):
    size = lax.axis_size(axis)
    return lax.all_to_all(
        jnp.broadcast_to(array[None], (size, *array.shape)), axis, 0, 0, tiled=True
    )


def joined_along(parts, dim):
    parts = jnp.moveaxis(parts, 0, dim)
    lengths = parts.shape
    return parts.reshape(*lengths[:dim], lengths[dim] * lengths[dim + 1], *lengths[dim + 2 :])


def whole_of(array, axes, dim):
    far, near = axes
    parts = sent_to_all(sent_to_all(array, far), near)
    return joined_along(parts.swapaxes(0, 1).reshape(-1, *array.shape), dim)


def sum_by_parts(array, axes):
    own = sum_by_axis(rows_for(array, lax.axis_size(axes[0]) * lax.axis_size(axes[1])), axes, 0)
    whole = whole_of(own, axes, 0)
    return whole[: len(array)].reshape(array.shape)


def packed_total(arrays, axis):
    ravelled, at, done = (jnp.concatenate([a.reshape(-1) for a in arrays]), 0, [])
    subtotal = sum_by_parts(ravelled, axis)
    for a in arrays:
        done.append(subtotal[at : at + a.size].reshape(a.shape))
        at += a.size
    return tuple(done)


def solve_lower(lower_factor, target):
    return lax.linalg.triangular_solve(lower_factor, target, left_side=True, lower=True)


def body(
    prior_sample,
    measured_point_location,
    measured_data,
    measurement_noise_sigma,
    measured_slots_used,
):
    exact_arithmetic = lax.Precision.HIGHEST
    anomaly_matrix, points_in_region = prior_sample.shape
    region_batches = lax.axis_size(MEMBER)
    sample_total = anomaly_matrix * region_batches
    pointwise_spread = points_in_region // region_batches
    linear_position = measured_point_location.reshape(-1)
    obs_blk = linear_position.shape[0]
    observation_deviation = obs_blk // region_batches
    propagated_grid = jnp.take(prior_sample, linear_position, axis=1).reshape(
        anomaly_matrix, region_batches, observation_deviation
    )
    prior_regions = prior_sample.reshape(anomaly_matrix, region_batches, pointwise_spread)
    prior_sample_full, integrate_dynamics = side_by_side(
        (prior_regions, propagated_grid), MEMBER, 1, 0, 2
    )
    integrate_dynamics = integrate_dynamics.reshape(sample_total, observation_deviation)
    rank = lax.axis_index(MEMBER)
    start = rank * observation_deviation
    my_value = lax.dynamic_slice_in_dim(measured_data.reshape(-1), start, observation_deviation)
    my_sigma = lax.dynamic_slice_in_dim(
        measurement_noise_sigma.reshape(-1), start, observation_deviation
    )
    slots = start + jnp.arange(observation_deviation, dtype=jnp.int32)
    valid = slots < measured_slots_used[0]
    weight = jnp.where(valid, 1.0 / my_sigma, jnp.zeros_like(my_sigma))
    sim_mean = jnp.mean(integrate_dynamics, axis=0)
    perturbed = (integrate_dynamics - sim_mean[None, :]) * weight[None, :]
    innovation = (my_value - sim_mean) * weight
    gram_loc = jnp.dot(perturbed, perturbed.T, precision=exact_arithmetic)
    cross_loc = jnp.dot(perturbed, innovation, precision=exact_arithmetic)
    gram_all, cross = packed_total(
        (gram_loc, cross_loc), ("member_0", ("member_1", "space_0", "space_1"))
    )
    cov_matrix = gram_all + (sample_total - 1) * jnp.eye(sample_total, dtype=jnp.float32)
    lower_factor = jnp.linalg.cholesky(cov_matrix)
    inverse = solve_lower(lower_factor, jnp.eye(sample_total, dtype=jnp.float32))
    projected = jnp.dot(inverse, cross, precision=exact_arithmetic)
    mean_weight = jnp.dot(inverse.T, projected, precision=exact_arithmetic)
    weight_matrix_update = math.sqrt(sample_total - 1) * inverse + mean_weight[None, :]
    sample_vectors = prior_sample_full.reshape(sample_total, -1)
    prior_average = jnp.mean(sample_vectors, axis=0)
    updated_sample = prior_average[None, :] + jnp.dot(
        weight_matrix_update, sample_vectors - prior_average[None, :], precision=exact_arithmetic
    )
    returned = lax.all_to_all(
        updated_sample.reshape(prior_sample_full.shape),
        MEMBER,
        split_axis=0,
        concat_axis=1,
        tiled=True,
    )
    return returned.reshape(anomaly_matrix, points_in_region)


def solution(mesh):
    torus = Mesh(mesh.devices.reshape(8, 2, 8, 4), ("member_0", "member_1", "space_0", "space_1"))
    in_specs = (P(MEMBER, SPACE), P(SPACE, None), P(SPACE, None), P(SPACE, None), P(SPACE))
    out_specs = P(MEMBER, SPACE)
    return jax.shard_map(body, mesh=torus, in_specs=in_specs, out_specs=out_specs, check_vma=False)
```

profile of v0, /device:TPU:1, one launch (start us, length us, event | category | flops | bytes accessed | tf_op | source)
XLA Modules:
  0.0 291.4 jit_solution(18197405325729240451)
XLA Ops:
  0.0 9.8 %copy.39 = f32[16,32768]{0,1:T(8,128)} copy(f32[16,32768]{1,0:T(8,128)} %param.5) | data formatting | bytes 4194304 | tf_op args[0]
  9.8 11.4 %gather_fusion = f32[2048,16]{1,0:T(8,128)S(1)} fusion(f32[16,32768]{0,1:T(8,128)} %copy.39, s32[2048]{0:T(1024)S(1)} %broadcast_clamp_fusion), kind=kCustom, calls=%fused_computation | custom fusion | bytes 270336 | tf_op jit(solution)/shard_map/jit(_take)/gather | solution.py:97
  21.2 0.3 copy.40
  21.7 1.6 pad_maximum_fusion
  23.2 10.4 %all-to-all-start = ((f32[16,16,2176]{2,0,1:T(8,128)}), f32[16,16,2176]{2,0,1:T(8,128)S(1)}, u32[]{:S(2)}, u32[]{:S(2)}) async-start(f32[16,16,2176]{2,0,1:T(8,128)} %pad_maximum_fusion), calls=%async_computation | async-start | bytes 4456448 | tf_op jit(solution)/shard_map/all_to_all | solution.py:16
  34.3 0.8 compare_select_fusion.2
  35.0 50.2 %all-to-all-done = f32[16,16,2176]{2,0,1:T(8,128)S(1)} async-done(((f32[16,16,2176]{2,0,1:T(8,128)}), f32[16,16,2176]{2,0,1:T(8,128)S(1)}, u32[]{:S(2)}, u32[]{:S(2)}) %all-to-all-start) | async-done | bytes 2228256 | tf_op jit(solution)/shard_map/all_to_all | solution.py:16
  85.3 0.4 convolution_bitcast_fusion
  85.7 0.9 fusion.9
  86.6 0.2 copy.59
  86.8 0.6 reshape_reshape.6
  87.4 0.3 copy.42
  87.7 29.3 %all_to_all.58 = f32[64,8,129]{2,1,0:T(8,128)S(1)} all-to-all(f32[64,8,129]{2,1,0:T(8,128)S(1)} %copy.42), channel_id=1, replica_groups=mesh['member_0'=8,'member_1'=2,'space_0'=8,'space_1'=4] {'member_1','spa..., dimensions={0} | all-to-all | bytes 528384 | tf_op jit(solution)/shard_map/all_to_all | solution.py:27
  117.1 10.7 %all_to_all.59 = f32[8,1,129]{2,1,0:T(1,128)S(1)} all-to-all(f32[8,1,129]{2,1,0:T(1,128)S(1)} %all_to_all.45), channel_id=1, replica_groups=mesh['member_0'=8,'member_1'=2,'space_0'=8,'space_1'=4] {'member_0'}, dimensions={0} | all-to-all | bytes 8256 | tf_op jit(solution)/shard_map/all_to_all | solution.py:34
  127.9 0.6 broadcast_in_dim.41
  128.5 3.3 %all-to-all-start.3 = ((f32[8,1,129]{2,1,0:T(1,128)}), f32[8,1,129]{2,1,0:T(1,128)S(1)}, u32[]{:S(2)}, u32[]{:S(2)}) async-start(f32[8,1,129]{2,1,0:T(1,128)} %broadcast_in_dim.41), calls=%async_computation.3 | async-start | bytes 16384 | tf_op jit(solution)/shard_map/all_to_all | solution.py:46
  131.8 0.6 iota_compare_fusion
  132.5 5.9 %all-to-all-done.3 = f32[8,1,129]{2,1,0:T(1,128)S(1)} async-done(((f32[8,1,129]{2,1,0:T(1,128)}), f32[8,1,129]{2,1,0:T(1,128)S(1)}, u32[]{:S(2)}, u32[]{:S(2)}) %all-to-all-start.3) | async-done | bytes 4160 | tf_op jit(solution)/shard_map/all_to_all | solution.py:46
  138.3 0.8 broadcast_in_dim.43
  139.2 8.6 %all-to-all-start.4 = ((f32[64,8,129]{2,1,0:T(8,128)}), f32[64,8,129]{2,1,0:T(8,128)S(1)}, u32[]{:S(2)}, u32[]{:S(2)}) async-start(f32[64,8,129]{2,1,0:T(8,128)} %broadcast_in_dim.43), calls=%async_computation.4 | async-start | bytes 1048576 | tf_op jit(solution)/shard_map/all_to_all | solution.py:46
  147.9 17.2 %all-to-all-done.4 = f32[64,8,129]{2,1,0:T(8,128)S(1)} async-done(((f32[64,8,129]{2,1,0:T(8,128)}), f32[64,8,129]{2,1,0:T(8,128)S(1)}, u32[]{:S(2)}, u32[]{:S(2)}) %all-to-all-start.4) | async-done | bytes 264224 | tf_op jit(solution)/shard_map/all_to_all | solution.py:46
  165.1 0.2 copy.43
  165.3 0.5 slice.55
  166.2 11.7 %cholesky.49 = f32[128,128]{1,0:T(8,128)S(1)} custom-call(f32[128,128]{1,0:T(8,128)S(1)} %cholesky.115), custom_call_target="Cholesky" | custom-call | tf_op jit(solution)/shard_map/jit(cholesky)/cholesky | solution.py:123
  178.1 9.8 %custom-call.14 = f32[1,128,128]{1,2,0:T(8,128)S(1)} custom-call(f32[1,128,128]{2,1,0:T(8,128)S(1)} %get-tuple-element.40), custom_call_target="InvertDiagBlocksLowerTriangular" | custom-call | tf_op jit(solution)/shard_map/jit(cholesky)/cholesky | solution.py:123
  187.9 0.2 fusion.22
  188.2 0.3 convolution_subtract_fusion.1
  188.5 11.7 %cholesky.103 = f32[128,128]{1,0:T(8,128)S(1)} custom-call(f32[128,128]{1,0:T(8,128)S(1)} %convolution_subtract_fusion.1), custom_call_target="Cholesky" | custom-call | tf_op jit(solution)/shard_map/jit(cholesky)/cholesky | solution.py:123
  200.3 0.4 reshape_reshape.7
  200.8 0.7 compare_reduce_fusion
  202.9 5.4 %while.1 = (s32[]{:T(128)}, f32[256,256]{0,1:T(8,128)S(1)}, s32[2,2]{1,0:T(2,128)S(1)}, f32[2,128,128]{2,1,0:T(8,128)}, s32[]{:T(128)}) while((s32[]{:T(128)}, f32[256,256]{0,1:T(8,128)S(1)}, s32[2,2]{1,0:T(2,128)S(1)}, f32[2,128,128]{2,1,0:T(8,128)}, s32[]{:T(128)}) %tuple.25), condition=%wide.while_cond, body=%wide.while_body.sunk | while | flops 2 | bytes 393329 | solution.py:79
  202.9 0.6 fusion.45
  203.5 1.4 dynamic-slice.7
  204.9 0.6 bitcast_dynamic-update-slice_fusion.2
  205.6 0.6 fusion.45
  206.2 1.4 dynamic-slice.7
  207.6 0.6 bitcast_dynamic-update-slice_fusion.2
  208.2 20.5 %custom-call.15 = f32[2,128,128]{1,2,0:T(8,128)S(1)} custom-call(f32[2,128,128]{2,1,0:T(8,128)} %get-tuple-element.12), custom_call_target="InvertDiagBlocksLowerTriangular" | custom-call | tf_op jit(solution)/shard_map/triangular_solve | solution.py:79
  228.7 0.3 fusion.16
  229.0 0.4 convolution_subtract_fusion
  229.4 0.3 fusion.21
  229.7 0.3 convolution_bitcast_fusion.1
  230.0 0.3 fusion.3
  230.3 2.0 fusion
  232.3 2.2 copy.52
  234.4 53.2 %all_to_all.60 = f32[256,1,2048]{2,1,0:T(1,128)S(1)} all-to-all(f32[256,1,2048]{2,1,0:T(1,128)S(1)} %copy.52), channel_id=1, replica_groups=mesh['member_0'=8,'member_1'=2,'space_0'=8,'space_1'=4] {'member_0','mem..., dimensions={0} | all-to-all | bytes 4194304 | tf_op jit(solution)/shard_map/all_to_all | solution.py:133
  287.6 1.2 copy.53
  288.8 2.5 copy.60
  (44 shorter events, 1.5 us)
Async XLA Ops:
  0.0 9.8 %copy-start.2 = (s32[16,128]{1,0:T(8,128)S(1)}, s32[16,128]{1,0:T(8,128)}, u32[]{:S(2)}) copy-start(s32[16,128]{1,0:T(8,128)} %param.6) | copy-start | bytes 24580
  9.8 11.7 %copy-start = (f32[16,32768]{1,0:T(8,128)S(1)}, f32[16,32768]{1,0:T(8,128)}, u32[]{:S(2)}) copy-start(f32[16,32768]{1,0:T(8,128)} %param.5) | copy-start | bytes 6291460
  23.2 62.0 %all-to-all-start = ((f32[16,16,2176]{2,0,1:T(8,128)}), f32[16,16,2176]{2,0,1:T(8,128)S(1)}, u32[]{:S(2)}, u32[]{:S(2)}) async-start(f32[16,16,2176]{2,0,1:T(8,128)} %pad_maximum_fusion), calls=%async_computation | async-start | bytes 4456448 | tf_op jit(solution)/shard_map/all_to_all | solution.py:16
  128.5 9.9 %all-to-all-start.3 = ((f32[8,1,129]{2,1,0:T(1,128)}), f32[8,1,129]{2,1,0:T(1,128)S(1)}, u32[]{:S(2)}, u32[]{:S(2)}) async-start(f32[8,1,129]{2,1,0:T(1,128)} %broadcast_in_dim.41), calls=%async_computation.3 | async-start | bytes 16384 | tf_op jit(solution)/shard_map/all_to_all | solution.py:46
  139.2 25.9 %all-to-all-start.4 = ((f32[64,8,129]{2,1,0:T(8,128)}), f32[64,8,129]{2,1,0:T(8,128)S(1)}, u32[]{:S(2)}, u32[]{:S(2)}) async-start(f32[64,8,129]{2,1,0:T(8,128)} %broadcast_in_dim.43), calls=%async_computation.4 | async-start | bytes 1048576 | tf_op jit(solution)/shard_map/all_to_all | solution.py:46
  200.3 28.4 %copy-start.1 = (pred[256,256]{0,1:T(32,128)(4,1)S(1)}, pred[256,256]{0,1:T(32,128)(4,1)}, u32[]{:S(2)}) copy-start(pred[256,256]{0,1:T(32,128)(4,1)} %iota_compare_fusion) | copy-start | bytes 196612
where the time goes:
time: 292 us; the launch traced here: 291 us
  blocking collectives  93.2 us (32%)
  waiting for transfers between devices  73.3 us (25%)
  other arithmetic  57.9 us (20%)
  local copies, waits for them, and re-layouts  37.1 us (13%)
  starting transfers between devices  22.3 us (8%)
  matrix products  5.23 us (2%)
    all_to_all x1, blocking collectives, body(): lax.all_to_all(updated_sample.reshape(prior_sample_full.shape), MEMBER, s...  53.2 us
    all_to_all x1, waiting for transfers between devices, side_by_side(): lax.all_to_all(both, axis, split_axis=split_dim, concat_axis=concat_dim,...  50.2 us
    another operation x6, other arithmetic, body(): lower_factor = jnp.linalg.cholesky(cov_matrix)  34 us
    all_to_all x1, blocking collectives, sent_and_summed(): parts = lax.all_to_all(split_up(array, dim, size), axis, 0, 0, tiled=True)  29.3 us
    all_to_all x2, waiting for transfers between devices, sent_to_all(): lax.all_to_all(jnp.broadcast_to(array[None], (size, *array.shape)), axis,...  23.1 us
    another operation x3, other arithmetic, solve_lower(): lax.linalg.triangular_solve(lower_factor, target, left_side=True, lower=T...  20.5 us
    unnamed x11, local copies, waits for them, and re-layouts  12.6 us
    all_to_all x2, starting transfers between devices, sent_to_all(): lax.all_to_all(jnp.broadcast_to(array[None], (size, *array.shape)), axis,...  11.9 us
  transfers between devices with their start and end apart: 3, of which 3 were waited for; matrix products, arithmetic and copies ran while one was open for 1% of the time, Pallas kernels for 0%

commit v1 on v0

v1 whole, which is shorter than its diff:
```python
import math

import jax
import jax.numpy as jnp
from jax import lax
from jax.experimental import pallas as pl
from jax.experimental.pallas import tpu as pltpu
from jax.sharding import PartitionSpec as P

MEMBER = "member"
SPACE = "space"
LANES = 128


def pick_kernel(places_ref, state_ref, out_ref):
    rows = out_ref.shape[0]
    members = state_ref.shape[0]
    lane = lax.broadcasted_iota(jnp.int32, (members, LANES), 1)

    def one_row(row, carry):
        total = jnp.zeros((members, LANES), jnp.float32)
        for slot in range(LANES):
            place = places_ref[row, slot]
            tile = pl.multiple_of((place >> 7) << 7, LANES)
            cells = state_ref[:, pl.ds(tile, LANES)]
            turned = pltpu.roll(cells, (slot - place) & (LANES - 1), 1)
            total = jnp.where(lane == slot, turned, total)
        out_ref[row] = total
        return carry

    lax.fori_loop(0, rows, one_row, 0)


def pick(places, state):
    rows = places.shape[0]
    members = state.shape[0]
    return pl.pallas_call(
        pick_kernel,
        out_shape=jax.ShapeDtypeStruct((rows, members, LANES), jnp.float32),
        in_specs=[
            pl.BlockSpec(memory_space=pltpu.SMEM),
            pl.BlockSpec(memory_space=pltpu.VMEM),
        ],
        out_specs=pl.BlockSpec(memory_space=pltpu.VMEM),
        compiler_params=pltpu.CompilerParams(vmem_limit_bytes=16 * 2**20),
        cost_estimate=pl.CostEstimate(
            flops=0, bytes_accessed=state.size * 4, transcendentals=0
        ),
    )(places, state)


def sent_to_all(array, axis):
    size = lax.axis_size(axis)
    copies = jnp.broadcast_to(array[None], (size, *array.shape))
    return lax.all_to_all(copies, axis, 0, 0, tiled=True)


def summed_everywhere(array):
    parts = lax.axis_size(SPACE)
    height = array.shape[0] // parts
    pieces = array.reshape(parts, height, array.shape[1])
    pieces = jnp.sum(lax.all_to_all(pieces, SPACE, 0, 0, tiled=True), axis=0)
    pieces = jnp.sum(sent_to_all(pieces, MEMBER), axis=0)
    return sent_to_all(pieces, SPACE).reshape(array.shape)


def body(
    prior_sample,
    measured_point_location,
    measured_data,
    measurement_noise_sigma,
    measured_slots_used,
):
    exact = lax.Precision.HIGHEST
    own_members, cells = prior_sample.shape
    groups = lax.axis_size(MEMBER)
    total = own_members * groups
    own_cells = cells // groups
    obs = measured_point_location.size // groups

    picked = pick(measured_point_location, prior_sample)
    evolved = lax.all_to_all(picked, MEMBER, 0, 0, tiled=True).reshape(total, obs)

    rank = lax.axis_index(MEMBER)
    value = lax.dynamic_slice_in_dim(measured_data, rank, 1).reshape(obs)
    sigma = lax.dynamic_slice_in_dim(measurement_noise_sigma, rank, 1).reshape(obs)
    slots = rank * obs + jnp.arange(obs, dtype=jnp.int32)
    weight = jnp.where(slots < measured_slots_used[0], 1.0 / sigma, 0.0)
    sim_mean = jnp.mean(evolved, axis=0)
    perturbed = (evolved - sim_mean[None, :]) * weight[None, :]
    innovation = (value - sim_mean) * weight
    gram = jnp.dot(perturbed, perturbed.T, precision=exact)
    cross = jnp.dot(perturbed, innovation, precision=exact)

    state, gram = lax.optimization_barrier((prior_sample, gram))
    forward = state.reshape(own_members, groups, own_cells).swapaxes(0, 1)
    forward = lax.all_to_all(forward, MEMBER, 0, 0, tiled=True).reshape(total, own_cells)

    half = total // 2
    gram = gram.at[:2, half:].set(cross.reshape(2, half))
    gram = summed_everywhere(gram)
    cross = gram[:2, half:].reshape(total)
    lower = jnp.concatenate([gram[:half, :half], gram[half:, :half].T], axis=1)
    gram = jnp.concatenate([lower, gram[half:]], axis=0)
    cov_matrix = gram + (total - 1) * jnp.eye(total, dtype=jnp.float32)
    lower_factor = jnp.linalg.cholesky(cov_matrix)
    inverse = lax.linalg.triangular_solve(
        lower_factor, jnp.eye(total, dtype=jnp.float32), left_side=True, lower=True
    )
    projected = jnp.dot(inverse, cross, precision=exact)
    mean_weight = jnp.dot(inverse.T, projected, precision=exact)
    transform = math.sqrt(total - 1) * inverse + mean_weight[None, :]

    average = jnp.mean(forward, axis=0)
    updated = average[None, :] + jnp.dot(
        transform, forward - average[None, :], precision=exact
    )
    updated = updated.reshape(groups, own_members, own_cells)
    back = lax.all_to_all(updated, MEMBER, 0, 0, tiled=True)
    return back.swapaxes(0, 1).reshape(own_members, cells)


def solution(mesh):
    in_specs = (P(MEMBER, SPACE), P(SPACE, None), P(SPACE, None), P(SPACE, None), P(SPACE))
    return jax.shard_map(
        body, mesh=mesh, in_specs=in_specs, out_specs=P(MEMBER, SPACE), check_vma=False
    )
```

time: 292 us -> 217 us (0.74)
  waiting for transfers between devices: 73.3 us -> 17.8 us
  local copies, waits for them, and re-layouts: 37.1 us -> 13.2 us
  Pallas kernels: 0 us -> 7.32 us
  starting transfers between devices: 22.3 us -> 18.2 us
    all_to_all x3, waiting for transfers between devices: 73.3 us -> 17.8 us  [the longest x1 11.3 us: sent_to_all(): return lax.all_to_all(copies, axis, 0, 0, tiled=True)]
    gather x2 -> x0, local copies, waits for them, and re-layouts: 11.7 us -> none  [body(): jnp.take(prior_sample, linear_position, axis=1)]
    unnamed x11 -> x8, local copies, waits for them, and re-layouts: 12.6 us -> 2.31 us
    pallas_call x0 -> x1, Pallas kernels: none -> 7.32 us  [pick(): pl.pallas_call(pick_kernel, out_shape=jax.ShapeDtypeStruct((rows, members...]
    all_to_all x3, starting transfers between devices: 22.3 us -> 18.2 us  [the longest x1 10.3 us: body(): lax.all_to_all(picked, MEMBER, 0, 0, tiled=True).reshape(total, obs)]
    another operation x3 -> x5, other arithmetic: 20.5 us -> 22.6 us  [the longest x2 19.9 us: body(): lax.linalg.triangular_solve(lower_factor, jnp.eye(total, dtype=jnp.float3...]
    another operation x13 -> x12, local copies, waits for them, and re-layouts: 6.35 us -> 4.96 us
  transfers between devices with their start and end apart: 3 -> 3, of which waited for: 3 -> 2; matrix products, arithmetic and copies ran while one was open for 1% -> 30% of each run, Pallas kernels for 0% -> 0%
where the time goes in v1:
time: 217 us; the launch traced here: 216 us
  blocking collectives  94.6 us (44%)
  other arithmetic  58 us (27%)
  starting transfers between devices  18.2 us (8%)
  waiting for transfers between devices  17.8 us (8%)
  local copies, waits for them, and re-layouts  13.2 us (6%)
  Pallas kernels  7.32 us (3%)
  matrix products  5.16 us (2%)
  between operations  2.2 us (1%)
    all_to_all x1, blocking collectives, body(): back = lax.all_to_all(updated, MEMBER, 0, 0, tiled=True)  58.1 us
    another operation x6, other arithmetic, body(): lower_factor = jnp.linalg.cholesky(cov_matrix)  34 us
    all_to_all x1, blocking collectives, summed_everywhere(): pieces = jnp.sum(lax.all_to_all(pieces, SPACE, 0, 0, tiled=True), axis=0)  23.4 us
    another operation x2, other arithmetic, body(): lax.linalg.triangular_solve(lower_factor, jnp.eye(total, dtype=jnp.float3...  19.9 us
    all_to_all x1, blocking collectives, sent_to_all(): return lax.all_to_all(copies, axis, 0, 0, tiled=True)  13.2 us
    all_to_all x1, waiting for transfers between devices, sent_to_all(): return lax.all_to_all(copies, axis, 0, 0, tiled=True)  11.3 us
    all_to_all x1, starting transfers between devices, body(): lax.all_to_all(picked, MEMBER, 0, 0, tiled=True).reshape(total, obs)  10.3 us
    pallas_call x1, Pallas kernels, pick(): pl.pallas_call(pick_kernel, out_shape=jax.ShapeDtypeStruct((rows, members...  7.32 us
  transfers between devices with their start and end apart: 3, of which 2 were waited for; matrix products, arithmetic and copies ran while one was open for 30% of the time, Pallas kernels for 0%

profile of v1, /device:TPU:1, one launch (start us, length us, event | category | flops | bytes accessed | tf_op | source)
XLA Modules:
  0.0 216.5 jit_solution(6404896347173347378)
XLA Ops:
  0.0 1.6 copy-done
  1.6 0.7 copy-done.2
  2.3 7.3 %shard_map.55 = f32[16,16,128]{2,1,0:T(8,128)} custom-call(s32[16,128]{1,0:T(8,128)S(1)} %copy-done.2, f32[16,32768]{1,0:T(8,128)S(1)} %copy-done), custom_call_target="tpu_custom_call" | custom-call | bytes 2097152 | tf_op jit(solution)/shard_map/pallas_call | solution.py:37
  9.6 10.3 %all-to-all-start = ((f32[16,16,128]{2,1,0:T(8,128)}), f32[16,16,128]{2,1,0:T(8,128)S(1)}, u32[]{:S(2)}, u32[]{:S(2)}) async-start(f32[16,16,128]{2,1,0:T(8,128)} %shard_map.55), calls=%async_computation | async-start | bytes 262144 | tf_op jit(solution)/shard_map/all_to_all | solution.py:82
  20.6 0.7 fusion.37
  21.3 0.7 fusion.25
  22.0 0.7 and_reduce_fusion
  22.7 6.5 %all-to-all-done = f32[16,16,128]{2,1,0:T(8,128)S(1)} async-done(((f32[16,16,128]{2,1,0:T(8,128)}), f32[16,16,128]{2,1,0:T(8,128)S(1)}, u32[]{:S(2)}, u32[]{:S(2)}) %all-to-all-start) | async-done | bytes 131104 | tf_op jit(solution)/shard_map/all_to_all | solution.py:82
  29.2 0.4 fusion.26
  29.6 0.9 fusion.16
  30.5 2.0 dynamic-slice_select_fusion
  32.5 1.6 scatter.4
  34.1 23.4 %all_to_all.30 = f32[32,8,256]{2,1,0:T(8,128)S(1)} all-to-all(f32[32,8,256]{2,1,0:T(8,128)S(1)} %bitcast.93), channel_id=1, replica_groups=mesh['member'=16,'space'=32] {'space'}, dimensions={0} | all-to-all | bytes 524288 | tf_op jit(solution)/shard_map/all_to_all | solution.py:62
  57.6 13.2 %all_to_all.31 = f32[16,8,256]{2,1,0:T(8,128)S(1)} all-to-all(f32[16,8,256]{2,1,0:T(8,128)S(1)} %broadcast_in_dim.10), channel_id=1, replica_groups=mesh['member'=16,'space'=32] {'member'}, dimensions={0} | all-to-all | bytes 262144 | tf_op jit(solution)/shard_map/all_to_all | solution.py:55
  70.7 0.7 broadcast_in_dim.11
  71.5 3.9 %all-to-all-start.4 = ((f32[32,8,256]{2,1,0:T(8,128)}), f32[32,8,256]{2,1,0:T(8,128)S(1)}, u32[]{:S(2)}, u32[]{:S(2)}) async-start(f32[32,8,256]{2,1,0:T(8,128)} %broadcast_in_dim.11), calls=%async_computation.4 | async-start | bytes 524288 | tf_op jit(solution)/shard_map/all_to_all | solution.py:55
  75.4 1.5 copy.40
  76.9 11.3 %all-to-all-done.4 = f32[32,8,256]{2,1,0:T(8,128)S(1)} async-done(((f32[32,8,256]{2,1,0:T(8,128)}), f32[32,8,256]{2,1,0:T(8,128)S(1)}, u32[]{:S(2)}, u32[]{:S(2)}) %all-to-all-start.4) | async-done | bytes 262176 | tf_op jit(solution)/shard_map/all_to_all | solution.py:55
  88.2 4.0 %all-to-all-start.1 = ((f32[16,16,2048]{2,1,0:T(8,128)}), f32[16,16,2048]{2,1,0:T(8,128)S(1)}, u32[]{:S(2)}, u32[]{:S(2)}) async-start(f32[16,16,2048]{2,1,0:T(8,128)} %bitcast.87), calls=%async_computation.1 | async-start | bytes 4194304 | tf_op jit(solution)/shard_map/all_to_all | solution.py:97
  92.2 0.1 copy.26
  92.3 0.1 copy.25
  92.4 0.1 copy.27
  92.6 11.7 %cholesky.49 = f32[128,128]{1,0:T(8,128)S(1)} custom-call(f32[128,128]{1,0:T(8,128)S(1)} %cholesky.115), custom_call_target="Cholesky" | custom-call | tf_op jit(solution)/shard_map/jit(cholesky)/cholesky | solution.py:106
  104.3 0.1 copy.28
  104.5 9.8 %custom-call.14 = f32[1,128,128]{1,2,0:T(8,128)S(1)} custom-call(f32[1,128,128]{2,1,0:T(8,128)S(1)} %get-tuple-element.54), custom_call_target="InvertDiagBlocksLowerTriangular" | custom-call | tf_op jit(solution)/shard_map/jit(cholesky)/cholesky | solution.py:106
  114.3 0.2 fusion.11
  114.6 0.3 convolution_subtract_fusion.1
  114.9 11.7 %cholesky.103 = f32[128,128]{1,0:T(8,128)S(1)} custom-call(f32[128,128]{1,0:T(8,128)S(1)} %convolution_subtract_fusion.1), custom_call_target="Cholesky" | custom-call | tf_op jit(solution)/shard_map/jit(cholesky)/cholesky | solution.py:106
  126.6 0.1 copy.30
  126.8 0.7 compare_reduce_fusion
  128.9 4.3 %while.2 = (s32[]{:T(128)}, f32[256,256]{0,1:T(8,128)S(1)}, s32[2,2]{1,0:T(2,128)S(1)}, f32[2,128,128]{2,1,0:T(8,128)S(1)}, s32[]{:T(128)}) while((s32[]{:T(128)}, f32[256,256]{0,1:T(8,128)S(1)}, s32[2,2]{1,0:T(2,128)S(1)}, f32[2,128,128]{2,1,0:T(8,128)S(1)}, s32[]{:T(128)}) %tuple.32), condition=%wide.while_cond.1, body=%wide.while_body.1.sunk | while | flops 2 | bytes 393329 | solution.py:107
  128.9 0.7 fusion.39
  129.5 1.3 dynamic-slice.18
  130.9 0.1 copy.42
  131.0 0.7 fusion.39
  131.7 1.3 dynamic-slice.18
  133.0 0.1 copy.42
  133.2 19.9 %custom-call.15 = f32[2,128,128]{1,2,0:T(8,128)S(1)} custom-call(f32[2,128,128]{2,1,0:T(8,128)S(1)} %get-tuple-element.28), custom_call_target="InvertDiagBlocksLowerTriangular" | custom-call | tf_op jit(solution)/shard_map/triangular_solve | solution.py:107
  153.1 0.3 fusion.7
  153.3 0.4 convolution_subtract_fusion
  153.7 0.3 fusion.10
  154.0 0.3 convolution_bitcast_fusion
  154.3 0.3 fusion
  154.6 0.1 reduce_sum.37
  154.8 0.2 bitcast_subtract_fusion
  155.0 1.9 convolution_add_fusion
  156.9 58.1 %all_to_all.32 = f32[16,16,2048]{2,1,0:T(8,128)S(1)} all-to-all(f32[16,16,2048]{2,1,0:T(8,128)S(1)} %bitcast.86), channel_id=1, replica_groups=mesh['member'=16,'space'=32] {'member'}, dimensions={0} | all-to-all | bytes 4194304 | tf_op jit(solution)/shard_map/all_to_all | solution.py:119
  215.0 1.5 copy.38
  (35 shorter events, 0.6 us)
Async XLA Ops:
  0.0 22.0 %copy-start.3 = (s32[2]{0:T(128)S(1)}, s32[2]{0:T(128)}, u32[]{:S(2)}) copy-start(s32[2]{0:T(128)} %constant.115.clone.1) | copy-start | bytes 28
  0.0 1.6 copy-start
  1.6 0.7 copy-start.2
  9.6 65.8 %copy-start.1 = (f32[16,32768]{1,0:T(8,128)S(1)}, f32[16,32768]{1,0:T(8,128)}, u32[]{:S(2)}) copy-start(f32[16,32768]{1,0:T(8,128)} %state_ref.1) | copy-start | bytes 6291460
  9.6 19.5 %all-to-all-start = ((f32[16,16,128]{2,1,0:T(8,128)}), f32[16,16,128]{2,1,0:T(8,128)S(1)}, u32[]{:S(2)}, u32[]{:S(2)}) async-start(f32[16,16,128]{2,1,0:T(8,128)} %shard_map.55), calls=%async_computation | async-start | bytes 262144 | tf_op jit(solution)/shard_map/all_to_all | solution.py:82
  71.5 16.7 %all-to-all-start.4 = ((f32[32,8,256]{2,1,0:T(8,128)}), f32[32,8,256]{2,1,0:T(8,128)S(1)}, u32[]{:S(2)}, u32[]{:S(2)}) async-start(f32[32,8,256]{2,1,0:T(8,128)} %broadcast_in_dim.11), calls=%async_computation.4 | async-start | bytes 524288 | tf_op jit(solution)/shard_map/all_to_all | solution.py:55
  88.2 66.4 %all-to-all-start.1 = ((f32[16,16,2048]{2,1,0:T(8,128)}), f32[16,16,2048]{2,1,0:T(8,128)S(1)}, u32[]{:S(2)}, u32[]{:S(2)}) async-start(f32[16,16,2048]{2,1,0:T(8,128)} %bitcast.87), calls=%async_computation.1 | async-start | bytes 4194304 | tf_op jit(solution)/shard_map/all_to_all | solution.py:97

commit v2 on v1

v2 whole, which is shorter than its diff:
```python
import functools
import math

import jax
import jax.numpy as jnp
from jax import lax
from jax.experimental import pallas as pl
from jax.experimental.pallas import tpu as pltpu
from jax.sharding import PartitionSpec as P

MEMBER = "member"
SPACE = "space"
LANES = 128
SUBLANES = 8
IN_VMEM = pl.BlockSpec(memory_space=pltpu.VMEM)
IN_SMEM = pl.BlockSpec(memory_space=pltpu.SMEM)
KERNEL = pltpu.CompilerParams(vmem_limit_bytes=16 * 2**20)
SMALL = pl.CostEstimate(flops=1024, bytes_accessed=1024, transcendentals=0)


def product(a, b, along):
    return lax.dot_general(
        a,
        b,
        (((1,), (along,)), ((), ())),
        precision=lax.Precision.HIGHEST,
        preferred_element_type=jnp.float32,
    )


def pick_kernel(places_ref, state_ref, out_ref):
    rows, members = out_ref.shape[:2]
    lane = lax.broadcasted_iota(jnp.int32, (members, LANES), 1)

    def one_row(row, carry):
        total = jnp.zeros((members, LANES), jnp.float32)
        for slot in range(LANES):
            place = places_ref[row, slot]
            tile = pl.multiple_of((place >> 7) << 7, LANES)
            cells = state_ref[:, pl.ds(tile, LANES)]
            turned = pltpu.roll(cells, (slot - place) & (LANES - 1), 1)
            total = jnp.where(lane == slot, turned, total)
        out_ref[row] = total
        return carry

    lax.fori_loop(0, rows, one_row, 0)


def pick(places, state):
    return pl.pallas_call(
        pick_kernel,
        out_shape=jax.ShapeDtypeStruct((places.shape[0], state.shape[0], LANES), jnp.float32),
        in_specs=[IN_SMEM, IN_VMEM],
        out_specs=IN_VMEM,
        compiler_params=KERNEL,
        cost_estimate=SMALL,
    )(places, state)


def gram_kernel(rank_ref, used_ref, evolved_ref, data_ref, sigma_ref, out_ref):
    total, obs = evolved_ref.shape
    half = total // 2
    rank = rank_ref[0]
    value = data_ref[pl.ds(rank, 1), :]
    sigma = sigma_ref[pl.ds(rank, 1), :]
    slots = rank * obs + lax.broadcasted_iota(jnp.int32, (1, obs), 1)
    weight = jnp.where(slots < used_ref[0], 1.0 / sigma, 0.0)
    evolved = evolved_ref[...]
    sim_mean = jnp.sum(evolved, axis=0, keepdims=True) * (1.0 / total)
    perturbed = (evolved - sim_mean) * weight
    innovation = jnp.broadcast_to((value - sim_mean) * weight, (SUBLANES, obs))
    out_ref[...] = product(perturbed, perturbed, 1)
    cross = product(innovation, perturbed, 1)
    out_ref[0:1, half:] = cross[0:1, :half]
    out_ref[1:2, half:] = cross[0:1, half:]


def gram_of(rank, used, evolved, data, sigma):
    total = evolved.shape[0]
    return pl.pallas_call(
        gram_kernel,
        out_shape=jax.ShapeDtypeStruct((total, total), jnp.float32),
        in_specs=[IN_SMEM, IN_SMEM, IN_VMEM, IN_VMEM, IN_VMEM],
        out_specs=IN_VMEM,
        compiler_params=KERNEL,
        cost_estimate=SMALL,
    )(rank.reshape(1), used, evolved, data, sigma)


def all_lanes(a, lane):
    return jnp.broadcast_to(a[:, lane : lane + 1], a.shape)


def all_rows(a, row):
    return jnp.broadcast_to(a[row : row + 1, :], a.shape)


def inverse_factor(block):
    size, step = block.shape[0], SUBLANES
    groups = size // step
    row = lax.broadcasted_iota(jnp.int32, (step, size), 0)
    lane = lax.broadcasted_iota(jnp.int32, (step, size), 1)
    left = [block[step * g : step * (g + 1)] for g in range(groups)]
    right = [jnp.where(lane == row + step * g, 1.0, 0.0) for g in range(groups)]
    for p in range(groups):
        left_row = [all_rows(left[p], k) for k in range(step)]
        right_row = [all_rows(right[p], k) for k in range(step)]
        column = [all_lanes(left[p], step * p + j) for j in range(step)]
        a = {(i, j): all_rows(column[j], i) for i in range(step) for j in range(i + 1)}
        factor, scale = {}, []
        for k in range(step):
            scale.append(lax.rsqrt(a[k, k]))
            left_row[k] = left_row[k] * scale[k]
            right_row[k] = right_row[k] * scale[k]
            for i in range(k + 1, step):
                factor[i, k] = a[i, k] * scale[k]
            for i in range(k + 1, step):
                for j in range(k + 1, i + 1):
                    a[i, j] = a[i, j] - factor[i, k] * factor[j, k]
                left_row[i] = left_row[i] - factor[i, k] * left_row[k]
                right_row[i] = right_row[i] - factor[i, k] * right_row[k]
        right[p] = right_row[0]
        for k in range(1, step):
            right[p] = jnp.where(row == k, right_row[k], right[p])
        for g in range(p + 1, groups):
            below = [all_lanes(left[g], step * p + j) for j in range(step)]
            for k in range(step):
                for j in range(k):
                    below[k] = below[k] - below[j] * factor[k, j]
                below[k] = below[k] * scale[k]
            for k in range(step):
                left[g] = left[g] - below[k] * left_row[k]
                right[g] = right[g] - below[k] * right_row[k]
    return jnp.concatenate(right, axis=0)


def transform_kernel(gram_ref, out_ref):
    total = gram_ref.shape[0]
    half = total // 2
    row = lax.broadcasted_iota(jnp.int32, (half, half), 0)
    lane = lax.broadcasted_iota(jnp.int32, (half, half), 1)
    diagonal = jnp.where(row == lane, jnp.float32(total - 1), 0.0)
    first = inverse_factor(gram_ref[:half, :half] + diagonal)
    low = product(gram_ref[half:, :half], first, 1)
    last = inverse_factor(gram_ref[half:, half:] + diagonal - product(low, low, 1))
    corner = -product(last, product(low, first, 0), 0)
    cross_0 = jnp.broadcast_to(gram_ref[0:1, half:], (SUBLANES, half))
    cross_1 = jnp.broadcast_to(gram_ref[1:2, half:], (SUBLANES, half))
    projected_0 = product(cross_0, first, 1)
    projected_1 = product(cross_0, corner, 1) + product(cross_1, last, 1)
    mean_0 = (product(projected_0, first, 0) + product(projected_1, corner, 0))[0:1]
    mean_1 = product(projected_1, last, 0)[0:1]
    spread = math.sqrt(total - 1)
    out_ref[:half, :half] = spread * first + mean_0
    out_ref[:half, half:] = jnp.broadcast_to(mean_1, (half, half))
    out_ref[half:, :half] = spread * corner + mean_0
    out_ref[half:, half:] = spread * last + mean_1


def transform_of(gram):
    return pl.pallas_call(
        transform_kernel,
        out_shape=jax.ShapeDtypeStruct(gram.shape, jnp.float32),
        in_specs=[IN_VMEM],
        out_specs=IN_VMEM,
        compiler_params=KERNEL,
        cost_estimate=SMALL,
    )(gram)


def sent_to_all(array, axis):
    size = lax.axis_size(axis)
    copies = jnp.broadcast_to(array[None], (size, *array.shape))
    return lax.all_to_all(copies, axis, 0, 0, tiled=True)


def summed_everywhere(array):
    parts = lax.axis_size(SPACE)
    height = array.shape[0] // parts
    pieces = array.reshape(parts, height, array.shape[1])
    pieces = jnp.sum(lax.all_to_all(pieces, SPACE, 0, 0, tiled=True), axis=0)
    pieces = jnp.sum(sent_to_all(pieces, MEMBER), axis=0)
    return sent_to_all(pieces, SPACE).reshape(array.shape)


def body(
    prior_sample,
    measured_point_location,
    measured_data,
    measurement_noise_sigma,
    measured_slots_used,
):
    own_members, cells = prior_sample.shape
    groups = lax.axis_size(MEMBER)
    total = own_members * groups
    own_cells = cells // groups

    picked = pick(measured_point_location, prior_sample)
    state, picked = lax.optimization_barrier((prior_sample, picked))
    evolved = lax.all_to_all(picked, MEMBER, 0, 0, tiled=True).reshape(total, LANES)
    forward = state.reshape(own_members, groups, own_cells).swapaxes(0, 1)
    forward = lax.all_to_all(forward, MEMBER, 0, 0, tiled=True).reshape(total, own_cells)

    gram = gram_of(
        lax.axis_index(MEMBER).astype(jnp.int32),
        measured_slots_used,
        evolved,
        measured_data,
        measurement_noise_sigma,
    )
    transform = transform_of(summed_everywhere(gram))

    average = jnp.mean(forward, axis=0)
    updated = average[None, :] + product(transform, forward - average[None, :], 0)
    updated = updated.reshape(groups, own_members, own_cells)
    back = lax.all_to_all(updated, MEMBER, 0, 0, tiled=True)
    return back.swapaxes(0, 1).reshape(own_members, cells)


def solution(mesh):
    in_specs = (P(MEMBER, SPACE), P(SPACE, None), P(SPACE, None), P(SPACE, None), P(SPACE))
    return jax.shard_map(
        body, mesh=mesh, in_specs=in_specs, out_specs=P(MEMBER, SPACE), check_vma=False
    )
```

time: 217 us -> 201 us (0.926)
  other arithmetic: 58 us -> 3.59 us
  waiting for transfers between devices: 17.8 us -> 58.2 us
  Pallas kernels: 7.32 us -> 18.7 us
  local copies, waits for them, and re-layouts: 13.2 us -> 5.94 us
  matrix products: 5.16 us -> 1.93 us
  blocking collectives: 94.6 us -> 92.3 us
    another operation x11 -> x0, other arithmetic: 56.7 us -> none  [the longest x6 34 us: body(): lower_factor = jnp.linalg.cholesky(cov_matrix)]
    all_to_all x1, waiting for transfers between devices: 0.01 us -> 38.3 us  [body(): lax.all_to_all(forward, MEMBER, 0, 0, tiled=True).reshape(total, own_cells)]
    pallas_call x1 -> x3, Pallas kernels: 7.32 us -> 18.7 us  [the longest x1 10.9 us: transform_of(): pl.pallas_call(transform_kernel, out_shape=jax.ShapeDtypeStruct(gram.shap...]
    another operation x19 -> x0, local copies, waits for them, and re-layouts: 5.28 us -> none
    all_to_all x1, blocking collectives: 58.1 us -> 55.8 us  [body(): back = lax.all_to_all(updated, MEMBER, 0, 0, tiled=True)]
  transfers between devices with their start and end apart: 3 -> 3, of which waited for: 2 -> 3; matrix products, arithmetic and copies ran while one was open for 30% -> 1% of each run, Pallas kernels for 0% -> 5%
where the time goes in v2:
time: 201 us; the launch traced here: 200 us
  blocking collectives  92.3 us (46%)
  waiting for transfers between devices  58.2 us (29%)
  Pallas kernels  18.7 us (9%)
  starting transfers between devices  18.7 us (9%)
  local copies, waits for them, and re-layouts  5.94 us (3%)
  other arithmetic  3.59 us (2%)
    all_to_all x1, blocking collectives, body(): back = lax.all_to_all(updated, MEMBER, 0, 0, tiled=True)  55.8 us
    all_to_all x1, waiting for transfers between devices, body(): lax.all_to_all(forward, MEMBER, 0, 0, tiled=True).reshape(total, own_cells)  38.3 us
    all_to_all x1, blocking collectives, summed_everywhere(): pieces = jnp.sum(lax.all_to_all(pieces, SPACE, 0, 0, tiled=True), axis=0)  23.4 us
    all_to_all x1, blocking collectives, sent_to_all(): return lax.all_to_all(copies, axis, 0, 0, tiled=True)  13.2 us
    all_to_all x1, waiting for transfers between devices, sent_to_all(): return lax.all_to_all(copies, axis, 0, 0, tiled=True)  11.4 us
    pallas_call x1, Pallas kernels, transform_of(): pl.pallas_call(transform_kernel, out_shape=jax.ShapeDtypeStruct(gram.shap...  10.9 us
    all_to_all x1, starting transfers between devices, body(): lax.all_to_all(picked, MEMBER, 0, 0, tiled=True).reshape(total, LANES)  10.2 us
    all_to_all x1, waiting for transfers between devices, body(): lax.all_to_all(picked, MEMBER, 0, 0, tiled=True).reshape(total, LANES)  8.56 us
  transfers between devices with their start and end apart: 3, of which 3 were waited for; matrix products, arithmetic and copies ran while one was open for 1% of the time, Pallas kernels for 5%

profile of v2, /device:TPU:1, one launch (start us, length us, event | category | flops | bytes accessed | tf_op | source)
XLA Modules:
  0.0 200.1 jit_solution(15673047362014895305)
XLA Ops:
  0.0 0.0 copy-start
  0.0 1.6 copy-done
  1.6 0.0 copy-start.2
  1.6 0.7 copy-done.2
  2.3 0.0 copy-start.3
  2.3 0.0 copy-start.4
  2.3 0.0 copy-start.1
  2.3 7.3 %shard_map.55 = f32[16,16,128]{2,1,0:T(8,128)} custom-call(s32[16,128]{1,0:T(8,128)S(1)} %copy-done.2, f32[16,32768]{1,0:T(8,128)S(1)} %copy-done), custom_call_target="tpu_custom_call" | custom-call | flops 1024 | bytes 1024 | tf_op jit(solution)/shard_map/pallas_call | solution.py:50
  9.6 10.2 %all-to-all-start.1 = ((f32[16,16,128]{2,1,0:T(8,128)}), f32[16,16,128]{2,1,0:T(8,128)S(1)}, u32[]{:S(2)}, u32[]{:S(2)}) async-start(f32[16,16,128]{2,1,0:T(8,128)} %shard_map.55), calls=%async_computation.1 | async-start | bytes 262144 | tf_op jit(solution)/shard_map/all_to_all | solution.py:200
  20.4 8.6 %all-to-all-done.1 = f32[16,16,128]{2,1,0:T(8,128)S(1)} async-done(((f32[16,16,128]{2,1,0:T(8,128)}), f32[16,16,128]{2,1,0:T(8,128)S(1)}, u32[]{:S(2)}, u32[]{:S(2)}) %all-to-all-start.1) | async-done | bytes 131104 | tf_op jit(solution)/shard_map/all_to_all | solution.py:200
  29.0 0.0 copy-done.3
  29.0 0.0 copy-done.4
  29.0 0.5 shard_map.56
  29.5 23.4 %all_to_all.30 = f32[32,8,256]{2,1,0:T(8,128)S(1)} all-to-all(f32[32,8,256]{2,1,0:T(8,128)S(1)} %bitcast.21), channel_id=1, replica_groups=mesh['member'=16,'space'=32] {'space'}, dimensions={0} | all-to-all | bytes 524288 | tf_op jit(solution)/shard_map/all_to_all | solution.py:181
  53.0 13.2 %all_to_all.31 = f32[16,8,256]{2,1,0:T(8,128)S(1)} all-to-all(f32[16,8,256]{2,1,0:T(8,128)S(1)} %broadcast_in_dim.4), channel_id=1, replica_groups=mesh['member'=16,'space'=32] {'member'}, dimensions={0} | all-to-all | bytes 262144 | tf_op jit(solution)/shard_map/all_to_all | solution.py:174
  66.2 0.7 broadcast_in_dim.5
  66.9 3.9 %all-to-all-start.4 = ((f32[32,8,256]{2,1,0:T(8,128)}), f32[32,8,256]{2,1,0:T(8,128)S(1)}, u32[]{:S(2)}, u32[]{:S(2)}) async-start(f32[32,8,256]{2,1,0:T(8,128)} %broadcast_in_dim.5), calls=%async_computation.4 | async-start | bytes 524288 | tf_op jit(solution)/shard_map/all_to_all | solution.py:174
  70.8 0.0 copy-done.1
  70.8 1.5 copy.13
  72.2 11.4 %all-to-all-done.4 = f32[32,8,256]{2,1,0:T(8,128)S(1)} async-done(((f32[32,8,256]{2,1,0:T(8,128)}), f32[32,8,256]{2,1,0:T(8,128)S(1)}, u32[]{:S(2)}, u32[]{:S(2)}) %all-to-all-start.4) | async-done | bytes 262176 | tf_op jit(solution)/shard_map/all_to_all | solution.py:174
  83.6 4.6 %all-to-all-start = ((f32[16,16,2048]{2,1,0:T(8,128)}), f32[16,16,2048]{2,1,0:T(8,128)}, u32[]{:S(2)}, u32[]{:S(2)}) async-start(f32[16,16,2048]{2,1,0:T(8,128)} %bitcast.23), calls=%async_computation | async-start | bytes 4194304 | tf_op jit(solution)/shard_map/all_to_all | solution.py:202
  88.2 10.9 %shard_map.57 = f32[256,256]{1,0:T(8,128)S(1)} custom-call(f32[256,256]{1,0:T(8,128)S(1)} %bitcast.20), custom_call_target="tpu_custom_call" | custom-call | flops 1024 | bytes 1024 | tf_op jit(solution)/shard_map/pallas_call | solution.py:161
  99.1 38.3 %all-to-all-done = f32[16,16,2048]{2,1,0:T(8,128)} async-done(((f32[16,16,2048]{2,1,0:T(8,128)}), f32[16,16,2048]{2,1,0:T(8,128)}, u32[]{:S(2)}, u32[]{:S(2)}) %all-to-all-start) | async-done | bytes 2097184 | tf_op jit(solution)/shard_map/all_to_all | solution.py:202
  137.3 1.7 reduce_sum.27
  139.0 1.8 bitcast_subtract_fusion
  140.9 1.9 convolution_add_fusion
  142.8 55.8 %all_to_all.32 = f32[16,16,2048]{2,1,0:T(8,128)S(1)} all-to-all(f32[16,16,2048]{2,1,0:T(8,128)S(1)} %bitcast.24), channel_id=1, replica_groups=mesh['member'=16,'space'=32] {'member'}, dimensions={0} | all-to-all | bytes 4194304 | tf_op jit(solution)/shard_map/all_to_all | solution.py:216
  198.6 1.5 copy.11
  (4 shorter events, 0.1 us)
Async XLA Ops:
  0.0 1.6 copy-start
  1.6 0.7 copy-start.2
  2.3 26.7 %copy-start.3 = (f32[16,128]{1,0:T(8,128)S(1)}, f32[16,128]{1,0:T(8,128)}, u32[]{:S(2)}) copy-start(f32[16,128]{1,0:T(8,128)} %data_ref.1) | copy-start | bytes 24580
  2.3 26.7 %copy-start.4 = (f32[16,128]{1,0:T(8,128)S(1)}, f32[16,128]{1,0:T(8,128)}, u32[]{:S(2)}) copy-start(f32[16,128]{1,0:T(8,128)} %sigma_ref.1) | copy-start | bytes 24580
  2.3 68.5 %copy-start.1 = (f32[16,32768]{1,0:T(8,128)S(1)}, f32[16,32768]{1,0:T(8,128)}, u32[]{:S(2)}) copy-start(f32[16,32768]{1,0:T(8,128)} %state_ref.1) | copy-start | bytes 6291460
  9.6 19.4 %all-to-all-start.1 = ((f32[16,16,128]{2,1,0:T(8,128)}), f32[16,16,128]{2,1,0:T(8,128)S(1)}, u32[]{:S(2)}, u32[]{:S(2)}) async-start(f32[16,16,128]{2,1,0:T(8,128)} %shard_map.55), calls=%async_computation.1 | async-start | bytes 262144 | tf_op jit(solution)/shard_map/all_to_all | solution.py:200
  66.9 16.7 %all-to-all-start.4 = ((f32[32,8,256]{2,1,0:T(8,128)}), f32[32,8,256]{2,1,0:T(8,128)S(1)}, u32[]{:S(2)}, u32[]{:S(2)}) async-start(f32[32,8,256]{2,1,0:T(8,128)} %broadcast_in_dim.5), calls=%async_computation.4 | async-start | bytes 524288 | tf_op jit(solution)/shard_map/all_to_all | solution.py:174
  83.6 53.7 %all-to-all-start = ((f32[16,16,2048]{2,1,0:T(8,128)}), f32[16,16,2048]{2,1,0:T(8,128)}, u32[]{:S(2)}, u32[]{:S(2)}) async-start(f32[16,16,2048]{2,1,0:T(8,128)} %bitcast.23), calls=%async_computation | async-start | bytes 4194304 | tf_op jit(solution)/shard_map/all_to_all | solution.py:202

commit v3 on v2

--- a/solution.py
+++ b/solution.py
@@ -12,6 +12,7 @@
 SPACE = "space"
 LANES = 128
 SUBLANES = 8
+EARLY = (3, 5, 1, 7)
 IN_VMEM = pl.BlockSpec(memory_space=pltpu.VMEM)
 IN_SMEM = pl.BlockSpec(memory_space=pltpu.SMEM)
 KERNEL = pltpu.CompilerParams(vmem_limit_bytes=16 * 2**20)
@@ -168,19 +169,95 @@
     )(gram)
 
 
+def apply_kernel(chip_ref, transform_ref, *refs):
+    *parts, out_ref, state_ref = refs
+    chips = len(parts)
+    height = parts[0].shape[0]
+    for k, part in enumerate(parts):
+        chip = lax.rem(chip_ref[0] - k + chips, chips)
+        state_ref[pl.ds(pl.multiple_of(chip * height, height), height), :] = part[...]
+    state = state_ref[...]
+    average = jnp.sum(state, axis=0, keepdims=True) * (1.0 / state.shape[0])
+    out_ref[...] = average + product(transform_ref[...], state - average, 0)
+
+
+def applied(chip, transform, parts):
+    total = transform.shape[0]
+    shape = (total, parts[0].shape[1])
+    return pl.pallas_call(
+        apply_kernel,
+        out_shape=jax.ShapeDtypeStruct(shape, jnp.float32),
+        in_specs=[IN_SMEM] + [IN_VMEM] * (1 + len(parts)),
+        out_specs=IN_VMEM,
+        scratch_shapes=[pltpu.VMEM(shape, jnp.float32)],
+        compiler_params=pltpu.CompilerParams(vmem_limit_bytes=32 * 2**20),
+        cost_estimate=SMALL,
+    )(chip.reshape(1), transform, *parts)
+
+
 def sent_to_all(array, axis):
     size = lax.axis_size(axis)
     copies = jnp.broadcast_to(array[None], (size, *array.shape))
     return lax.all_to_all(copies, axis, 0, 0, tiled=True)
 
 
-def summed_everywhere(array):
-    parts = lax.axis_size(SPACE)
-    height = array.shape[0] // parts
-    pieces = array.reshape(parts, height, array.shape[1])
-    pieces = jnp.sum(lax.all_to_all(pieces, SPACE, 0, 0, tiled=True), axis=0)
-    pieces = jnp.sum(sent_to_all(pieces, MEMBER), axis=0)
-    return sent_to_all(pieces, SPACE).reshape(array.shape)
+def swapped(array):
+    groups = lax.axis_size(MEMBER)
+    return lax.ppermute(array, MEMBER, [(i, i ^ 1) for i in range(groups)])
+
+
+def shifted(array, k):
+    if k == 0:
+        return array
+    groups = lax.axis_size(MEMBER)
+    return lax.ppermute(array, MEMBER, [(i, (i + 2 * k) % groups) for i in range(groups)])
+
+
+def split_kernel(core_ref, state_ref, kept_ref, sent_ref):
+    chips, _, width = kept_ref.shape
+    core = core_ref[0]
+    for chip in range(chips):
+        own = pl.multiple_of((2 * chip + core) * width, LANES)
+        away = pl.multiple_of((2 * chip + 1 - core) * width, LANES)
+        kept_ref[chip] = state_ref[:, pl.ds(own, width)]
+        sent_ref[chip] = state_ref[:, pl.ds(away, width)]
+
+
+def split(core, state, chips):
+    members, cells = state.shape
+    half = jax.ShapeDtypeStruct((chips, members, cells // chips // 2), jnp.float32)
+    return pl.pallas_call(
+        split_kernel,
+        out_shape=(half, half),
+        in_specs=[IN_SMEM, IN_VMEM],
+        out_specs=(IN_VMEM, IN_VMEM),
+        compiler_params=KERNEL,
+        cost_estimate=SMALL,
+    )(core.reshape(1), state)
+
+
+def join_kernel(chip_ref, core_ref, kept_ref, other_ref, *out_refs):
+    chips, members, _ = kept_ref.shape
+    core = core_ref[0]
+    own = pl.ds(pl.multiple_of(core * members, members), members)
+    away = pl.ds(pl.multiple_of((1 - core) * members, members), members)
+    for k, out_ref in enumerate(out_refs):
+        target = lax.rem(chip_ref[0] + k, chips)
+        out_ref[own, :] = kept_ref[target]
+        out_ref[away, :] = other_ref[target]
+
+
+def join(chip, core, kept, other):
+    chips, members, width = kept.shape
+    pair = jax.ShapeDtypeStruct((2 * members, width), jnp.float32)
+    return pl.pallas_call(
+        join_kernel,
+        out_shape=(pair,) * chips,
+        in_specs=[IN_SMEM, IN_SMEM, IN_VMEM, IN_VMEM],
+        out_specs=(IN_VMEM,) * chips,
+        compiler_params=KERNEL,
+        cost_estimate=SMALL,
+    )(chip.reshape(1), core.reshape(1), kept, other)
 
 
 def body(
@@ -192,26 +269,37 @@
 ):
     own_members, cells = prior_sample.shape
     groups = lax.axis_size(MEMBER)
+    chips = groups // 2
     total = own_members * groups
     own_cells = cells // groups
+    rank = lax.axis_index(MEMBER).astype(jnp.int32)
+    chip, core = rank // 2, lax.rem(rank, 2)
 
     picked = pick(measured_point_location, prior_sample)
     state, picked = lax.optimization_barrier((prior_sample, picked))
     evolved = lax.all_to_all(picked, MEMBER, 0, 0, tiled=True).reshape(total, LANES)
-    forward = state.reshape(own_members, groups, own_cells).swapaxes(0, 1)
-    forward = lax.all_to_all(forward, MEMBER, 0, 0, tiled=True).reshape(total, own_cells)
+
+    kept, sent = split(core, state, chips)
+    pairs = join(chip, core, kept, swapped(sent))
+    evolved, pairs = lax.optimization_barrier((evolved, pairs))
 
     gram = gram_of(
-        lax.axis_index(MEMBER).astype(jnp.int32),
-        measured_slots_used,
-        evolved,
-        measured_data,
-        measurement_noise_sigma,
+        rank, measured_slots_used, evolved, measured_data, measurement_noise_sigma
     )
-    transform = transform_of(summed_everywhere(gram))
-
-    average = jnp.mean(forward, axis=0)
-    updated = average[None, :] + product(transform, forward - average[None, :], 0)
+    parts = {k: shifted(pairs[k], k) for k in EARLY}
+    spaces = lax.axis_size(SPACE)
+    pieces = gram.reshape(spaces, total // spaces, total)
+    pieces = jnp.sum(lax.all_to_all(pieces, SPACE, 0, 0, tiled=True), axis=0)
+    pieces, parts = lax.optimization_barrier((pieces, parts))
+    pieces = jnp.sum(sent_to_all(pieces, MEMBER), axis=0)
+    pieces, pairs = lax.optimization_barrier((pieces, pairs))
+    gram = sent_to_all(pieces, SPACE).reshape(total, total)
+    for k in range(chips):
+        if k not in parts:
+            parts[k] = shifted(pairs[k], k)
+    transform = transform_of(gram)
+
+    updated = applied(chip, transform, [parts[k] for k in range(chips)])
     updated = updated.reshape(groups, own_members, own_cells)
     back = lax.all_to_all(updated, MEMBER, 0, 0, tiled=True)
     return back.swapaxes(0, 1).reshape(own_members, cells)

time: 201 us -> 193 us (0.960)
  starting transfers between devices: 18.7 us -> 56.5 us
  blocking collectives: 92.3 us -> 68.5 us
  waiting for transfers between devices: 58.2 us -> 38.1 us
  other arithmetic: 3.59 us -> 0.06 us
  Pallas kernels: 18.7 us -> 21.8 us
    all_to_all x1, waiting for transfers between devices: 38.3 us -> 0.01 us  [body(): pieces = jnp.sum(lax.all_to_all(pieces, SPACE, 0, 0, tiled=True), axis=0)]
    ppermute x0 -> x8, starting transfers between devices: none -> 32.5 us  [the longest x7 23.7 us: shifted(): lax.ppermute(array, MEMBER, [(i, (i + 2 * k) % groups) for i in range(gro...]
    ppermute x0 -> x8, waiting for transfers between devices: none -> 29.8 us  [the longest x7 29.7 us: shifted(): lax.ppermute(array, MEMBER, [(i, (i + 2 * k) % groups) for i in range(gro...]
    all_to_all x1 -> x0, blocking collectives: 23.4 us -> none  [summed_everywhere(): pieces = jnp.sum(lax.all_to_all(pieces, SPACE, 0, 0, tiled=True), axis=0)]
    all_to_all x1, waiting for transfers between devices: 11.4 us -> 2.14 us  [sent_to_all(): return lax.all_to_all(copies, axis, 0, 0, tiled=True)]
    all_to_all x1, starting transfers between devices: 4.61 us -> 11.4 us  [body(): pieces = jnp.sum(lax.all_to_all(pieces, SPACE, 0, 0, tiled=True), axis=0)]
    all_to_all x1, starting transfers between devices: 10.2 us -> 3.42 us  [body(): lax.all_to_all(picked, MEMBER, 0, 0, tiled=True).reshape(total, LANES)]
    all_to_all x1, starting transfers between devices: 3.87 us -> 9.2 us  [sent_to_all(): return lax.all_to_all(copies, axis, 0, 0, tiled=True)]
  transfers between devices with their start and end apart: 3 -> 11, of which waited for: 3 -> 6; matrix products, arithmetic and copies ran while one was open for 1% -> 0% of each run, Pallas kernels for 5% -> 6%
where the time goes in v3:
time: 193 us; the launch traced here: 192 us
  blocking collectives  68.5 us (35%)
  starting transfers between devices  56.5 us (29%)
  waiting for transfers between devices  38.1 us (20%)
  Pallas kernels  21.8 us (11%)
  local copies, waits for them, and re-layouts  6.58 us (3%)
    all_to_all x1, blocking collectives, body(): back = lax.all_to_all(updated, MEMBER, 0, 0, tiled=True)  54.1 us
    ppermute x7, waiting for transfers between devices, shifted(): lax.ppermute(array, MEMBER, [(i, (i + 2 * k) % groups) for i in range(gro...  29.7 us
    ppermute x7, starting transfers between devices, shifted(): lax.ppermute(array, MEMBER, [(i, (i + 2 * k) % groups) for i in range(gro...  23.7 us
    all_to_all x1, blocking collectives, sent_to_all(): return lax.all_to_all(copies, axis, 0, 0, tiled=True)  14.4 us
    all_to_all x1, starting transfers between devices, body(): pieces = jnp.sum(lax.all_to_all(pieces, SPACE, 0, 0, tiled=True), axis=0)  11.4 us
    pallas_call x1, Pallas kernels, transform_of(): pl.pallas_call(transform_kernel, out_shape=jax.ShapeDtypeStruct(gram.shap...  10.9 us
    all_to_all x1, starting transfers between devices, sent_to_all(): return lax.all_to_all(copies, axis, 0, 0, tiled=True)  9.2 us
    ppermute x1, starting transfers between devices, swapped(): return lax.ppermute(array, MEMBER, [(i, i ^ 1) for i in range(groups)])  8.79 us
  transfers between devices with their start and end apart: 11, of which 6 were waited for; matrix products, arithmetic and copies ran while one was open for 0% of the time, Pallas kernels for 6%

profile of v3, /device:TPU:1, one launch (start us, length us, event | category | flops | bytes accessed | tf_op | source)
XLA Modules:
  0.0 192.3 jit_solution(16277943597244851023)
XLA Ops:
  0.0 0.0 copy-start
  0.0 1.6 copy-done
  1.6 0.0 copy-start.2
  1.6 0.7 copy-done.2
  2.3 0.0 copy-start.1
  2.3 7.3 %shard_map.55 = f32[16,16,128]{2,1,0:T(8,128)} custom-call(s32[16,128]{1,0:T(8,128)S(1)} %copy-done.2, f32[16,32768]{1,0:T(8,128)S(1)} %copy-done), custom_call_target="tpu_custom_call" | custom-call | flops 1024 | bytes 1024 | tf_op jit(solution)/shard_map/pallas_call | solution.py:51
  9.6 0.0 copy-done.1
  9.6 0.0 copy-start.3
  9.6 0.0 copy-start.4
  9.6 0.1 shard_map.56
  9.8 8.8 %collective-permute-start = (f32[8,16,2048]{2,1,0:T(8,128)S(1)}, f32[8,16,2048]{2,1,0:T(8,128)S(1)}, u32[]{:S(2)}, u32[]{:S(2)}) collective-permute-start(f32[8,16,2048]{2,1,0:T(8,128)S(1)} %get-tuple-element.39), channel_id=1, source_target_pairs={{0,32},{32,0},{64,96},{96,64},{128,160},{160,128},{192,224},{224,1... | collective-permute-start | bytes 3145736 | tf_op jit(solution)/shard_map/ppermute | solution.py:206
  18.6 3.4 %all-to-all-start = ((f32[16,16,128]{2,1,0:T(8,128)}), f32[16,16,128]{2,1,0:T(8,128)S(1)}, u32[]{:S(2)}, u32[]{:S(2)}) async-start(f32[16,16,128]{2,1,0:T(8,128)} %shard_map.55), calls=%async_computation | async-start | bytes 262144 | tf_op jit(solution)/shard_map/all_to_all | solution.py:280
  22.7 0.0 collective-permute-done.other_ref
  22.7 0.1 shard_map.57
  22.8 0.0 copy-start.5
  22.8 0.7 copy-done.5
  23.5 0.0 copy-start.6
  23.5 0.7 copy-done.6
  24.2 0.0 copy-start.7
  24.2 0.7 copy-done.7
  24.9 6.2 %all-to-all-done = f32[16,16,128]{2,1,0:T(8,128)S(1)} async-done(((f32[16,16,128]{2,1,0:T(8,128)}), f32[16,16,128]{2,1,0:T(8,128)S(1)}, u32[]{:S(2)}, u32[]{:S(2)}) %all-to-all-start) | async-done | bytes 131104 | tf_op jit(solution)/shard_map/all_to_all | solution.py:280
  31.1 0.0 copy-done.3
  31.1 0.0 copy-done.4
  31.1 1.2 shard_map.58
  32.3 11.4 %all-to-all-start.1 = ((f32[32,8,256]{2,1,0:T(8,128)}), f32[32,8,256]{2,1,0:T(8,128)S(1)}, u32[]{:S(2)}, u32[]{:S(2)}) async-start(f32[32,8,256]{2,1,0:T(8,128)} %bitcast.4), calls=%async_computation.1 | async-start | bytes 524288 | tf_op jit(solution)/shard_map/all_to_all | solution.py:292
  43.7 2.0 %collective-permute-start.1 = (f32[32,2048]{1,0:T(8,128)}, f32[32,2048]{1,0:T(8,128)S(1)}, u32[]{:S(2)}, u32[]{:S(2)}) collective-permute-start(f32[32,2048]{1,0:T(8,128)} %copy-done.7), channel_id=1, source_target_pairs={{0,64},{32,96},{64,128},{96,160},{128,192},{160,224},{192,256},{22... | collective-permute-start | bytes 786440 | tf_op jit(solution)/shard_map/ppermute | solution.py:213
  45.7 2.8 %collective-permute-start.2 = (f32[32,2048]{1,0:T(8,128)}, f32[32,2048]{1,0:T(8,128)S(1)}, u32[]{:S(2)}, u32[]{:S(2)}) collective-permute-start(f32[32,2048]{1,0:T(8,128)} %copy-done.6), channel_id=1, source_target_pairs={{0,192},{32,224},{64,256},{96,288},{128,320},{160,352},{192,384},{... | collective-permute-start | bytes 786440 | tf_op jit(solution)/shard_map/ppermute | solution.py:213
  48.5 5.5 %collective-permute-start.3 = (f32[32,2048]{1,0:T(8,128)}, f32[32,2048]{1,0:T(8,128)S(1)}, u32[]{:S(2)}, u32[]{:S(2)}) collective-permute-start(f32[32,2048]{1,0:T(8,128)} %copy-done.5), channel_id=1, source_target_pairs={{0,320},{32,352},{64,384},{96,416},{128,448},{160,480},{192,0},{22... | collective-permute-start | bytes 786440 | tf_op jit(solution)/shard_map/ppermute | solution.py:213
  54.0 3.3 %collective-permute-start.4 = (f32[32,2048]{1,0:T(8,128)S(1)}, f32[32,2048]{1,0:T(8,128)S(1)}, u32[]{:S(2)}, u32[]{:S(2)}) collective-permute-start(f32[32,2048]{1,0:T(8,128)S(1)} %get-tuple-element.52), channel_id=1, source_target_pairs={{0,448},{32,480},{64,0},{96,32},{128,64},{160,96},{192,128},{224,1... | collective-permute-start | bytes 786440 | tf_op jit(solution)/shard_map/ppermute | solution.py:213
  57.3 0.0 all-to-all-done.1
  57.4 0.3 collective-permute-done.1.refs_1_
  57.6 12.4 %collective-permute-done.2.refs_3_ = f32[32,2048]{1,0:T(8,128)S(1)} collective-permute-done((f32[32,2048]{1,0:T(8,128)}, f32[32,2048]{1,0:T(8,128)S(1)}, u32[]{:S(2)}, u32[]{:S(2)}) %collective-permute-start.2) | collective-permute-done | bytes 262176 | tf_op jit(solution)/shard_map/ppermute | solution.py:213
  70.1 0.0 collective-permute-done.3.refs_5_
  70.1 7.2 %collective-permute-done.4.refs_7_ = f32[32,2048]{1,0:T(8,128)S(1)} collective-permute-done((f32[32,2048]{1,0:T(8,128)S(1)}, f32[32,2048]{1,0:T(8,128)S(1)}, u32[]{:S(2)}, u32[]{:S(2)}) %collective-permute-start.4) | collective-permute-done | bytes 262176 | tf_op jit(solution)/shard_map/ppermute | solution.py:213
  77.3 14.4 %all_to_all.25 = f32[16,8,256]{2,1,0:T(8,128)S(1)} all-to-all(f32[16,8,256]{2,1,0:T(8,128)S(1)} %broadcast_in_dim.4), channel_id=1, replica_groups=mesh['member'=16,'space'=32] {'member'}, dimensions={0} | all-to-all | bytes 262144 | tf_op jit(solution)/shard_map/all_to_all | solution.py:201
  91.7 0.7 broadcast_in_dim.5
  92.4 9.2 %all-to-all-start.3 = ((f32[32,8,256]{2,1,0:T(8,128)}), f32[32,8,256]{2,1,0:T(8,128)S(1)}, u32[]{:S(2)}, u32[]{:S(2)}) async-start(f32[32,8,256]{2,1,0:T(8,128)} %broadcast_in_dim.5), calls=%async_computation.3 | async-start | bytes 524288 | tf_op jit(solution)/shard_map/all_to_all | solution.py:201
  101.6 2.1 %collective-permute-start.5 = (f32[32,2048]{1,0:T(8,128)S(1)}, f32[32,2048]{1,0:T(8,128)S(1)}, u32[]{:S(2)}, u32[]{:S(2)}) collective-permute-start(f32[32,2048]{1,0:T(8,128)S(1)} %get-tuple-element.61), channel_id=1, source_target_pairs={{0,128},{32,160},{64,192},{96,224},{128,256},{160,288},{192,320},{... | collective-permute-start | bytes 786440 | tf_op jit(solution)/shard_map/ppermute | solution.py:213
  103.8 4.1 %collective-permute-start.6 = (f32[32,2048]{1,0:T(8,128)S(1)}, f32[32,2048]{1,0:T(8,128)S(1)}, u32[]{:S(2)}, u32[]{:S(2)}) collective-permute-start(f32[32,2048]{1,0:T(8,128)S(1)} %get-tuple-element.63), channel_id=1, source_target_pairs={{0,256},{32,288},{64,320},{96,352},{128,384},{160,416},{192,448},{... | collective-permute-start | bytes 786440 | tf_op jit(solution)/shard_map/ppermute | solution.py:213
  107.8 4.0 %collective-permute-start.7 = (f32[32,2048]{1,0:T(8,128)S(1)}, f32[32,2048]{1,0:T(8,128)S(1)}, u32[]{:S(2)}, u32[]{:S(2)}) collective-permute-start(f32[32,2048]{1,0:T(8,128)S(1)} %get-tuple-element.65), channel_id=1, source_target_pairs={{0,384},{32,416},{64,448},{96,480},{128,0},{160,32},{192,64},{224,... | collective-permute-start | bytes 786440 | tf_op jit(solution)/shard_map/ppermute | solution.py:213
  111.8 2.1 %all-to-all-done.3 = f32[32,8,256]{2,1,0:T(8,128)S(1)} async-done(((f32[32,8,256]{2,1,0:T(8,128)}), f32[32,8,256]{2,1,0:T(8,128)S(1)}, u32[]{:S(2)}, u32[]{:S(2)}) %all-to-all-start.3) | async-done | bytes 262176 | tf_op jit(solution)/shard_map/all_to_all | solution.py:201
  113.9 10.9 %shard_map.59.transform_ref = f32[256,256]{1,0:T(8,128)S(1)} custom-call(f32[256,256]{1,0:T(8,128)S(1)} %bitcast.11), custom_call_target="tpu_custom_call" | custom-call | flops 1024 | bytes 1024 | tf_op jit(solution)/shard_map/pallas_call | solution.py:162
  124.8 0.0 collective-permute-done.5.refs_2_
  124.8 0.0 collective-permute-done.6.refs_4_
  124.8 9.8 %collective-permute-done.7.refs_6_ = f32[32,2048]{1,0:T(8,128)S(1)} collective-permute-done((f32[32,2048]{1,0:T(8,128)S(1)}, f32[32,2048]{1,0:T(8,128)S(1)}, u32[]{:S(2)}, u32[]{:S(2)}) %collective-permute-start.7) | collective-permute-done | bytes 262176 | tf_op jit(solution)/shard_map/ppermute | solution.py:213
  134.6 2.1 %shard_map.60 = f32[256,2048]{1,0:T(8,128)S(1)} custom-call(s32[1]{0:T(128)} %bitcast.chip_ref, f32[256,256]{1,0:T(8,128)S(1)} %shard_map.59.transform_ref, f32[32,2048]{1,0:T(8,128)S(1)} %get-tuple-element.59.refs_0_, f32[32,2048]{1,0:T(8,128)S(1)} %collective-permute-done.1.refs_1_, f32[32,2048]{1,0:T(8,128)S(1)} %collective-permute-done.5.refs_2_, ...), custom_call_target="tpu_custom_call" | custom-call | flops 1024 | bytes 1024 | tf_op jit(solution)/shard_map/pallas_call | solution.py:187
  136.8 54.1 %all_to_all.26 = f32[16,16,2048]{2,1,0:T(8,128)S(1)} all-to-all(f32[16,16,2048]{2,1,0:T(8,128)S(1)} %bitcast.10), channel_id=1, replica_groups=mesh['member'=16,'space'=32] {'member'}, dimensions={0} | all-to-all | bytes 4194304 | tf_op jit(solution)/shard_map/all_to_all | solution.py:304
  190.8 1.5 copy.8
  (3 shorter events, 0.1 us)
Async XLA Ops:
  0.0 1.6 copy-start
  1.6 0.7 copy-start.2
  2.3 7.3 %copy-start.1 = (f32[16,32768]{1,0:T(8,128)S(1)}, f32[16,32768]{1,0:T(8,128)}, u32[]{:S(2)}) copy-start(f32[16,32768]{1,0:T(8,128)} %state_ref.2) | copy-start | bytes 6291460
  9.6 21.5 %copy-start.3 = (f32[16,128]{1,0:T(8,128)S(1)}, f32[16,128]{1,0:T(8,128)}, u32[]{:S(2)}) copy-start(f32[16,128]{1,0:T(8,128)} %data_ref.1) | copy-start | bytes 24580
  9.6 21.5 %copy-start.4 = (f32[16,128]{1,0:T(8,128)S(1)}, f32[16,128]{1,0:T(8,128)}, u32[]{:S(2)}) copy-start(f32[16,128]{1,0:T(8,128)} %sigma_ref.1) | copy-start | bytes 24580
  9.8 12.9 %collective-permute-start = (f32[8,16,2048]{2,1,0:T(8,128)S(1)}, f32[8,16,2048]{2,1,0:T(8,128)S(1)}, u32[]{:S(2)}, u32[]{:S(2)}) collective-permute-start(f32[8,16,2048]{2,1,0:T(8,128)S(1)} %get-tuple-element.39), channel_id=1, source_target_pairs={{0,32},{32,0},{64,96},{96,64},{128,160},{160,128},{192,224},{224,1... | collective-permute-start | bytes 3145736 | tf_op jit(solution)/shard_map/ppermute | solution.py:206
  18.6 12.5 %all-to-all-start = ((f32[16,16,128]{2,1,0:T(8,128)}), f32[16,16,128]{2,1,0:T(8,128)S(1)}, u32[]{:S(2)}, u32[]{:S(2)}) async-start(f32[16,16,128]{2,1,0:T(8,128)} %shard_map.55), calls=%async_computation | async-start | bytes 262144 | tf_op jit(solution)/shard_map/all_to_all | solution.py:280
  22.8 0.7 copy-start.5
  23.5 0.7 copy-start.6
  24.2 0.7 copy-start.7
  32.3 25.0 %all-to-all-start.1 = ((f32[32,8,256]{2,1,0:T(8,128)}), f32[32,8,256]{2,1,0:T(8,128)S(1)}, u32[]{:S(2)}, u32[]{:S(2)}) async-start(f32[32,8,256]{2,1,0:T(8,128)} %bitcast.4), calls=%async_computation.1 | async-start | bytes 524288 | tf_op jit(solution)/shard_map/all_to_all | solution.py:292
  43.7 13.9 %collective-permute-start.1 = (f32[32,2048]{1,0:T(8,128)}, f32[32,2048]{1,0:T(8,128)S(1)}, u32[]{:S(2)}, u32[]{:S(2)}) collective-permute-start(f32[32,2048]{1,0:T(8,128)} %copy-done.7), channel_id=1, source_target_pairs={{0,64},{32,96},{64,128},{96,160},{128,192},{160,224},{192,256},{22... | collective-permute-start | bytes 786440 | tf_op jit(solution)/shard_map/ppermute | solution.py:213
  45.7 24.4 %collective-permute-start.2 = (f32[32,2048]{1,0:T(8,128)}, f32[32,2048]{1,0:T(8,128)S(1)}, u32[]{:S(2)}, u32[]{:S(2)}) collective-permute-start(f32[32,2048]{1,0:T(8,128)} %copy-done.6), channel_id=1, source_target_pairs={{0,192},{32,224},{64,256},{96,288},{128,320},{160,352},{192,384},{... | collective-permute-start | bytes 786440 | tf_op jit(solution)/shard_map/ppermute | solution.py:213
  48.5 21.6 %collective-permute-start.3 = (f32[32,2048]{1,0:T(8,128)}, f32[32,2048]{1,0:T(8,128)S(1)}, u32[]{:S(2)}, u32[]{:S(2)}) collective-permute-start(f32[32,2048]{1,0:T(8,128)} %copy-done.5), channel_id=1, source_target_pairs={{0,320},{32,352},{64,384},{96,416},{128,448},{160,480},{192,0},{22... | collective-permute-start | bytes 786440 | tf_op jit(solution)/shard_map/ppermute | solution.py:213
  54.0 23.3 %collective-permute-start.4 = (f32[32,2048]{1,0:T(8,128)S(1)}, f32[32,2048]{1,0:T(8,128)S(1)}, u32[]{:S(2)}, u32[]{:S(2)}) collective-permute-start(f32[32,2048]{1,0:T(8,128)S(1)} %get-tuple-element.52), channel_id=1, source_target_pairs={{0,448},{32,480},{64,0},{96,32},{128,64},{160,96},{192,128},{224,1... | collective-permute-start | bytes 786440 | tf_op jit(solution)/shard_map/ppermute | solution.py:213
  92.4 21.5 %all-to-all-start.3 = ((f32[32,8,256]{2,1,0:T(8,128)}), f32[32,8,256]{2,1,0:T(8,128)S(1)}, u32[]{:S(2)}, u32[]{:S(2)}) async-start(f32[32,8,256]{2,1,0:T(8,128)} %broadcast_in_dim.5), calls=%async_computation.3 | async-start | bytes 524288 | tf_op jit(solution)/shard_map/all_to_all | solution.py:201
  101.6 23.1 %collective-permute-start.5 = (f32[32,2048]{1,0:T(8,128)S(1)}, f32[32,2048]{1,0:T(8,128)S(1)}, u32[]{:S(2)}, u32[]{:S(2)}) collective-permute-start(f32[32,2048]{1,0:T(8,128)S(1)} %get-tuple-element.61), channel_id=1, source_target_pairs={{0,128},{32,160},{64,192},{96,224},{128,256},{160,288},{192,320},{... | collective-permute-start | bytes 786440 | tf_op jit(solution)/shard_map/ppermute | solution.py:213
  103.8 21.0 %collective-permute-start.6 = (f32[32,2048]{1,0:T(8,128)S(1)}, f32[32,2048]{1,0:T(8,128)S(1)}, u32[]{:S(2)}, u32[]{:S(2)}) collective-permute-start(f32[32,2048]{1,0:T(8,128)S(1)} %get-tuple-element.63), channel_id=1, source_target_pairs={{0,256},{32,288},{64,320},{96,352},{128,384},{160,416},{192,448},{... | collective-permute-start | bytes 786440 | tf_op jit(solution)/shard_map/ppermute | solution.py:213
  107.8 26.8 %collective-permute-start.7 = (f32[32,2048]{1,0:T(8,128)S(1)}, f32[32,2048]{1,0:T(8,128)S(1)}, u32[]{:S(2)}, u32[]{:S(2)}) collective-permute-start(f32[32,2048]{1,0:T(8,128)S(1)} %get-tuple-element.65), channel_id=1, source_target_pairs={{0,384},{32,416},{64,448},{96,480},{128,0},{160,32},{192,64},{224,... | collective-permute-start | bytes 786440 | tf_op jit(solution)/shard_map/ppermute | solution.py:213

commit v4 on v3

--- a/solution.py
+++ b/solution.py
@@ -12,7 +12,8 @@
 SPACE = "space"
 LANES = 128
 SUBLANES = 8
-EARLY = (3, 5, 1, 7)
+FIRST = (3, 5, 2, 6)
+THEN = (4, 1, 7, 0)
 IN_VMEM = pl.BlockSpec(memory_space=pltpu.VMEM)
 IN_SMEM = pl.BlockSpec(memory_space=pltpu.SMEM)
 KERNEL = pltpu.CompilerParams(vmem_limit_bytes=16 * 2**20)
@@ -173,7 +174,7 @@
     *parts, out_ref, state_ref = refs
     chips = len(parts)
     height = parts[0].shape[0]
-    for k, part in enumerate(parts):
+    for k, part in zip(FIRST + THEN, parts):
         chip = lax.rem(chip_ref[0] - k + chips, chips)
         state_ref[pl.ds(pl.multiple_of(chip * height, height), height), :] = part[...]
     state = state_ref[...]
@@ -286,20 +287,17 @@
     gram = gram_of(
         rank, measured_slots_used, evolved, measured_data, measurement_noise_sigma
     )
-    parts = {k: shifted(pairs[k], k) for k in EARLY}
     spaces = lax.axis_size(SPACE)
+    first = [shifted(pairs[k], k) for k in FIRST]
     pieces = gram.reshape(spaces, total // spaces, total)
     pieces = jnp.sum(lax.all_to_all(pieces, SPACE, 0, 0, tiled=True), axis=0)
-    pieces, parts = lax.optimization_barrier((pieces, parts))
     pieces = jnp.sum(sent_to_all(pieces, MEMBER), axis=0)
-    pieces, pairs = lax.optimization_barrier((pieces, pairs))
+    pieces, first, pairs = lax.optimization_barrier((pieces, first, pairs))
+    then = [shifted(pairs[k], k) for k in THEN]
     gram = sent_to_all(pieces, SPACE).reshape(total, total)
-    for k in range(chips):
-        if k not in parts:
-            parts[k] = shifted(pairs[k], k)
     transform = transform_of(gram)
 
-    updated = applied(chip, transform, [parts[k] for k in range(chips)])
+    updated = applied(chip, transform, first + then)
     updated = updated.reshape(groups, own_members, own_cells)
     back = lax.all_to_all(updated, MEMBER, 0, 0, tiled=True)
     return back.swapaxes(0, 1).reshape(own_members, cells)

time: 193 us -> 180 us (0.933)
  waiting for transfers between devices: 38.1 us -> 8.86 us
  blocking collectives: 68.5 us -> 80.4 us
  starting transfers between devices: 56.5 us -> 60.6 us
    ppermute x7, waiting for transfers between devices: 29.7 us -> 2.67 us  [shifted(): lax.ppermute(array, MEMBER, [(i, (i + 2 * k) % groups) for i in range(gro...]
    all_to_all x1, blocking collectives: 14.4 us -> 23.9 us  [sent_to_all(): return lax.all_to_all(copies, axis, 0, 0, tiled=True)]
    ppermute x7, starting transfers between devices: 23.7 us -> 27.9 us  [shifted(): lax.ppermute(array, MEMBER, [(i, (i + 2 * k) % groups) for i in range(gro...]
    all_to_all x1, blocking collectives: 54.1 us -> 56.5 us  [body(): back = lax.all_to_all(updated, MEMBER, 0, 0, tiled=True)]
    all_to_all x1, waiting for transfers between devices: 2.14 us -> 0.01 us  [sent_to_all(): return lax.all_to_all(copies, axis, 0, 0, tiled=True)]
  transfers between devices with their start and end apart: 11 -> 11, of which waited for: 6 -> 3; matrix products, arithmetic and copies ran while one was open for 0% -> 0% of each run, Pallas kernels for 6% -> 6%
where the time goes in v4:
time: 180 us; the launch traced here: 179 us
  blocking collectives  80.4 us (45%)
  starting transfers between devices  60.6 us (34%)
  Pallas kernels  21.8 us (12%)
  waiting for transfers between devices  8.86 us (5%)
  local copies, waits for them, and re-layouts  6.58 us (4%)
    all_to_all x1, blocking collectives, body(): back = lax.all_to_all(updated, MEMBER, 0, 0, tiled=True)  56.5 us
    ppermute x7, starting transfers between devices, shifted(): lax.ppermute(array, MEMBER, [(i, (i + 2 * k) % groups) for i in range(gro...  27.9 us
    all_to_all x1, blocking collectives, sent_to_all(): return lax.all_to_all(copies, axis, 0, 0, tiled=True)  23.9 us
    all_to_all x1, starting transfers between devices, body(): pieces = jnp.sum(lax.all_to_all(pieces, SPACE, 0, 0, tiled=True), axis=0)  11.4 us
    pallas_call x1, Pallas kernels, transform_of(): pl.pallas_call(transform_kernel, out_shape=jax.ShapeDtypeStruct(gram.shap...  10.9 us
    all_to_all x1, starting transfers between devices, sent_to_all(): return lax.all_to_all(copies, axis, 0, 0, tiled=True)  9.08 us
    ppermute x1, starting transfers between devices, swapped(): return lax.ppermute(array, MEMBER, [(i, i ^ 1) for i in range(groups)])  8.79 us
    pallas_call x1, Pallas kernels, pick(): pl.pallas_call(pick_kernel, out_shape=jax.ShapeDtypeStruct((places.shape[...  7.32 us
  transfers between devices with their start and end apart: 11, of which 3 were waited for; matrix products, arithmetic and copies ran while one was open for 0% of the time, Pallas kernels for 6%

profile of v4, /device:TPU:1, one launch (start us, length us, event | category | flops | bytes accessed | tf_op | source)
XLA Modules:
  0.0 179.1 jit_solution(10787142902347542714)
XLA Ops:
  0.0 0.0 copy-start
  0.0 1.6 copy-done
  1.6 0.0 copy-start.2
  1.6 0.7 copy-done.2
  2.3 0.0 copy-start.1
  2.3 7.3 %shard_map.55 = f32[16,16,128]{2,1,0:T(8,128)} custom-call(s32[16,128]{1,0:T(8,128)S(1)} %copy-done.2, f32[16,32768]{1,0:T(8,128)S(1)} %copy-done), custom_call_target="tpu_custom_call" | custom-call | flops 1024 | bytes 1024 | tf_op jit(solution)/shard_map/pallas_call | solution.py:52
  9.6 0.0 copy-done.1
  9.6 0.0 copy-start.3
  9.6 0.0 copy-start.4
  9.6 0.1 shard_map.56
  9.8 8.8 %collective-permute-start = (f32[8,16,2048]{2,1,0:T(8,128)S(1)}, f32[8,16,2048]{2,1,0:T(8,128)S(1)}, u32[]{:S(2)}, u32[]{:S(2)}) collective-permute-start(f32[8,16,2048]{2,1,0:T(8,128)S(1)} %get-tuple-element.38), channel_id=1, source_target_pairs={{0,32},{32,0},{64,96},{96,64},{128,160},{160,128},{192,224},{224,1... | collective-permute-start | bytes 3145736 | tf_op jit(solution)/shard_map/ppermute | solution.py:207
  18.6 3.4 %all-to-all-start = ((f32[16,16,128]{2,1,0:T(8,128)}), f32[16,16,128]{2,1,0:T(8,128)S(1)}, u32[]{:S(2)}, u32[]{:S(2)}) async-start(f32[16,16,128]{2,1,0:T(8,128)} %shard_map.55), calls=%async_computation | async-start | bytes 262144 | tf_op jit(solution)/shard_map/all_to_all | solution.py:281
  22.6 0.0 collective-permute-done.other_ref
  22.7 0.1 shard_map.57
  22.8 0.0 copy-start.5
  22.8 0.7 copy-done.5
  23.5 0.0 copy-start.6
  23.5 0.7 copy-done.6
  24.2 0.0 copy-start.7
  24.2 0.7 copy-done.7
  24.9 6.2 %all-to-all-done = f32[16,16,128]{2,1,0:T(8,128)S(1)} async-done(((f32[16,16,128]{2,1,0:T(8,128)}), f32[16,16,128]{2,1,0:T(8,128)S(1)}, u32[]{:S(2)}, u32[]{:S(2)}) %all-to-all-start) | async-done | bytes 131104 | tf_op jit(solution)/shard_map/all_to_all | solution.py:281
  31.1 0.0 copy-done.3
  31.1 0.0 copy-done.4
  31.1 1.2 shard_map.58
  32.3 11.4 %all-to-all-start.1 = ((f32[32,8,256]{2,1,0:T(8,128)}), f32[32,8,256]{2,1,0:T(8,128)S(1)}, u32[]{:S(2)}, u32[]{:S(2)}) async-start(f32[32,8,256]{2,1,0:T(8,128)} %bitcast.4), calls=%async_computation.1 | async-start | bytes 524288 | tf_op jit(solution)/shard_map/all_to_all | solution.py:293
  43.7 2.3 %collective-permute-start.1 = (f32[32,2048]{1,0:T(8,128)}, f32[32,2048]{1,0:T(8,128)S(1)}, u32[]{:S(2)}, u32[]{:S(2)}) collective-permute-start(f32[32,2048]{1,0:T(8,128)} %copy-done.7), channel_id=1, source_target_pairs={{0,192},{32,224},{64,256},{96,288},{128,320},{160,352},{192,384},{... | collective-permute-start | bytes 786440 | tf_op jit(solution)/shard_map/ppermute | solution.py:214
  46.0 6.0 %collective-permute-start.2 = (f32[32,2048]{1,0:T(8,128)}, f32[32,2048]{1,0:T(8,128)S(1)}, u32[]{:S(2)}, u32[]{:S(2)}) collective-permute-start(f32[32,2048]{1,0:T(8,128)} %copy-done.6), channel_id=1, source_target_pairs={{0,320},{32,352},{64,384},{96,416},{128,448},{160,480},{192,0},{22... | collective-permute-start | bytes 786440 | tf_op jit(solution)/shard_map/ppermute | solution.py:214
  52.0 2.1 %collective-permute-start.3 = (f32[32,2048]{1,0:T(8,128)}, f32[32,2048]{1,0:T(8,128)S(1)}, u32[]{:S(2)}, u32[]{:S(2)}) collective-permute-start(f32[32,2048]{1,0:T(8,128)} %copy-done.5), channel_id=1, source_target_pairs={{0,128},{32,160},{64,192},{96,224},{128,256},{160,288},{192,320},{... | collective-permute-start | bytes 786440 | tf_op jit(solution)/shard_map/ppermute | solution.py:214
  54.1 5.3 %collective-permute-start.4 = (f32[32,2048]{1,0:T(8,128)S(1)}, f32[32,2048]{1,0:T(8,128)S(1)}, u32[]{:S(2)}, u32[]{:S(2)}) collective-permute-start(f32[32,2048]{1,0:T(8,128)S(1)} %get-tuple-element.51), channel_id=1, source_target_pairs={{0,384},{32,416},{64,448},{96,480},{128,0},{160,32},{192,64},{224,... | collective-permute-start | bytes 786440 | tf_op jit(solution)/shard_map/ppermute | solution.py:214
  59.4 0.0 all-to-all-done.1
  59.5 23.9 %all_to_all.25 = f32[16,8,256]{2,1,0:T(8,128)S(1)} all-to-all(f32[16,8,256]{2,1,0:T(8,128)S(1)} %broadcast_in_dim.4), channel_id=1, replica_groups=mesh['member'=16,'space'=32] {'member'}, dimensions={0} | all-to-all | bytes 262144 | tf_op jit(solution)/shard_map/all_to_all | solution.py:202
  83.4 0.0 collective-permute-done.1.refs_0_
  83.4 0.0 collective-permute-done.2.refs_1_
  83.4 0.0 collective-permute-done.3.refs_2_
  83.4 0.0 collective-permute-done.4.refs_3_
  83.4 0.7 broadcast_in_dim.5
  84.1 9.1 %all-to-all-start.3 = ((f32[32,8,256]{2,1,0:T(8,128)}), f32[32,8,256]{2,1,0:T(8,128)S(1)}, u32[]{:S(2)}, u32[]{:S(2)}) async-start(f32[32,8,256]{2,1,0:T(8,128)} %broadcast_in_dim.5), calls=%async_computation.3 | async-start | bytes 524288 | tf_op jit(solution)/shard_map/all_to_all | solution.py:202
  93.2 4.0 %collective-permute-start.5 = (f32[32,2048]{1,0:T(8,128)S(1)}, f32[32,2048]{1,0:T(8,128)S(1)}, u32[]{:S(2)}, u32[]{:S(2)}) collective-permute-start(f32[32,2048]{1,0:T(8,128)S(1)} %get-tuple-element.61), channel_id=1, source_target_pairs={{0,256},{32,288},{64,320},{96,352},{128,384},{160,416},{192,448},{... | collective-permute-start | bytes 786440 | tf_op jit(solution)/shard_map/ppermute | solution.py:214
  97.2 6.1 %collective-permute-start.6 = (f32[32,2048]{1,0:T(8,128)S(1)}, f32[32,2048]{1,0:T(8,128)S(1)}, u32[]{:S(2)}, u32[]{:S(2)}) collective-permute-start(f32[32,2048]{1,0:T(8,128)S(1)} %get-tuple-element.62), channel_id=1, source_target_pairs={{0,64},{32,96},{64,128},{96,160},{128,192},{160,224},{192,256},{22... | collective-permute-start | bytes 786440 | tf_op jit(solution)/shard_map/ppermute | solution.py:214
  103.4 2.1 %collective-permute-start.7 = (f32[32,2048]{1,0:T(8,128)S(1)}, f32[32,2048]{1,0:T(8,128)S(1)}, u32[]{:S(2)}, u32[]{:S(2)}) collective-permute-start(f32[32,2048]{1,0:T(8,128)S(1)} %get-tuple-element.63), channel_id=1, source_target_pairs={{0,448},{32,480},{64,0},{96,32},{128,64},{160,96},{192,128},{224,1... | collective-permute-start | bytes 786440 | tf_op jit(solution)/shard_map/ppermute | solution.py:214
  105.5 0.0 all-to-all-done.3
  105.5 10.9 %shard_map.59.transform_ref = f32[256,256]{1,0:T(8,128)S(1)} custom-call(f32[256,256]{1,0:T(8,128)S(1)} %bitcast.11), custom_call_target="tpu_custom_call" | custom-call | flops 1024 | bytes 1024 | tf_op jit(solution)/shard_map/pallas_call | solution.py:163
  116.4 0.0 collective-permute-done.5.refs_4_
  116.4 2.0 %collective-permute-done.6.refs_5_ = f32[32,2048]{1,0:T(8,128)S(1)} collective-permute-done((f32[32,2048]{1,0:T(8,128)S(1)}, f32[32,2048]{1,0:T(8,128)S(1)}, u32[]{:S(2)}, u32[]{:S(2)}) %collective-permute-start.6) | collective-permute-done | bytes 262176 | tf_op jit(solution)/shard_map/ppermute | solution.py:214
  118.3 0.7 collective-permute-done.7.refs_6_
  119.0 2.2 %shard_map.60 = f32[256,2048]{1,0:T(8,128)S(1)} custom-call(s32[1]{0:T(128)} %bitcast.chip_ref, f32[256,256]{1,0:T(8,128)S(1)} %shard_map.59.transform_ref, f32[32,2048]{1,0:T(8,128)S(1)} %collective-permute-done.1.refs_0_, f32[32,2048]{1,0:T(8,128)S(1)} %collective-permute-done.2.refs_1_, f32[32,2048]{1,0:T(8,128)S(1)} %collective-permute-done.3.refs_2_, ...), custom_call_target="tpu_custom_call" | custom-call | flops 1024 | bytes 1024 | tf_op jit(solution)/shard_map/pallas_call | solution.py:188
  121.2 56.5 %all_to_all.26 = f32[16,16,2048]{2,1,0:T(8,128)S(1)} all-to-all(f32[16,16,2048]{2,1,0:T(8,128)S(1)} %bitcast.10), channel_id=1, replica_groups=mesh['member'=16,'space'=32] {'member'}, dimensions={0} | all-to-all | bytes 4194304 | tf_op jit(solution)/shard_map/all_to_all | solution.py:302
  177.7 1.5 copy.8
  (3 shorter events, 0.1 us)
Async XLA Ops:
  0.0 1.6 copy-start
  1.6 0.7 copy-start.2
  2.3 7.3 %copy-start.1 = (f32[16,32768]{1,0:T(8,128)S(1)}, f32[16,32768]{1,0:T(8,128)}, u32[]{:S(2)}) copy-start(f32[16,32768]{1,0:T(8,128)} %state_ref.2) | copy-start | bytes 6291460
  9.6 21.5 %copy-start.3 = (f32[16,128]{1,0:T(8,128)S(1)}, f32[16,128]{1,0:T(8,128)}, u32[]{:S(2)}) copy-start(f32[16,128]{1,0:T(8,128)} %data_ref.1) | copy-start | bytes 24580
  9.6 21.5 %copy-start.4 = (f32[16,128]{1,0:T(8,128)S(1)}, f32[16,128]{1,0:T(8,128)}, u32[]{:S(2)}) copy-start(f32[16,128]{1,0:T(8,128)} %sigma_ref.1) | copy-start | bytes 24580
  9.8 12.9 %collective-permute-start = (f32[8,16,2048]{2,1,0:T(8,128)S(1)}, f32[8,16,2048]{2,1,0:T(8,128)S(1)}, u32[]{:S(2)}, u32[]{:S(2)}) collective-permute-start(f32[8,16,2048]{2,1,0:T(8,128)S(1)} %get-tuple-element.38), channel_id=1, source_target_pairs={{0,32},{32,0},{64,96},{96,64},{128,160},{160,128},{192,224},{224,1... | collective-permute-start | bytes 3145736 | tf_op jit(solution)/shard_map/ppermute | solution.py:207
  18.6 12.5 %all-to-all-start = ((f32[16,16,128]{2,1,0:T(8,128)}), f32[16,16,128]{2,1,0:T(8,128)S(1)}, u32[]{:S(2)}, u32[]{:S(2)}) async-start(f32[16,16,128]{2,1,0:T(8,128)} %shard_map.55), calls=%async_computation | async-start | bytes 262144 | tf_op jit(solution)/shard_map/all_to_all | solution.py:281
  22.8 0.7 copy-start.5
  23.5 0.7 copy-start.6
  24.2 0.7 copy-start.7
  32.3 27.1 %all-to-all-start.1 = ((f32[32,8,256]{2,1,0:T(8,128)}), f32[32,8,256]{2,1,0:T(8,128)S(1)}, u32[]{:S(2)}, u32[]{:S(2)}) async-start(f32[32,8,256]{2,1,0:T(8,128)} %bitcast.4), calls=%async_computation.1 | async-start | bytes 524288 | tf_op jit(solution)/shard_map/all_to_all | solution.py:293
  43.7 39.7 %collective-permute-start.1 = (f32[32,2048]{1,0:T(8,128)}, f32[32,2048]{1,0:T(8,128)S(1)}, u32[]{:S(2)}, u32[]{:S(2)}) collective-permute-start(f32[32,2048]{1,0:T(8,128)} %copy-done.7), channel_id=1, source_target_pairs={{0,192},{32,224},{64,256},{96,288},{128,320},{160,352},{192,384},{... | collective-permute-start | bytes 786440 | tf_op jit(solution)/shard_map/ppermute | solution.py:214
  46.0 37.4 %collective-permute-start.2 = (f32[32,2048]{1,0:T(8,128)}, f32[32,2048]{1,0:T(8,128)S(1)}, u32[]{:S(2)}, u32[]{:S(2)}) collective-permute-start(f32[32,2048]{1,0:T(8,128)} %copy-done.6), channel_id=1, source_target_pairs={{0,320},{32,352},{64,384},{96,416},{128,448},{160,480},{192,0},{22... | collective-permute-start | bytes 786440 | tf_op jit(solution)/shard_map/ppermute | solution.py:214
  52.0 31.4 %collective-permute-start.3 = (f32[32,2048]{1,0:T(8,128)}, f32[32,2048]{1,0:T(8,128)S(1)}, u32[]{:S(2)}, u32[]{:S(2)}) collective-permute-start(f32[32,2048]{1,0:T(8,128)} %copy-done.5), channel_id=1, source_target_pairs={{0,128},{32,160},{64,192},{96,224},{128,256},{160,288},{192,320},{... | collective-permute-start | bytes 786440 | tf_op jit(solution)/shard_map/ppermute | solution.py:214
  54.1 29.3 %collective-permute-start.4 = (f32[32,2048]{1,0:T(8,128)S(1)}, f32[32,2048]{1,0:T(8,128)S(1)}, u32[]{:S(2)}, u32[]{:S(2)}) collective-permute-start(f32[32,2048]{1,0:T(8,128)S(1)} %get-tuple-element.51), channel_id=1, source_target_pairs={{0,384},{32,416},{64,448},{96,480},{128,0},{160,32},{192,64},{224,... | collective-permute-start | bytes 786440 | tf_op jit(solution)/shard_map/ppermute | solution.py:214
  84.1 21.4 %all-to-all-start.3 = ((f32[32,8,256]{2,1,0:T(8,128)}), f32[32,8,256]{2,1,0:T(8,128)S(1)}, u32[]{:S(2)}, u32[]{:S(2)}) async-start(f32[32,8,256]{2,1,0:T(8,128)} %broadcast_in_dim.5), calls=%async_computation.3 | async-start | bytes 524288 | tf_op jit(solution)/shard_map/all_to_all | solution.py:202
  93.2 23.1 %collective-permute-start.5 = (f32[32,2048]{1,0:T(8,128)S(1)}, f32[32,2048]{1,0:T(8,128)S(1)}, u32[]{:S(2)}, u32[]{:S(2)}) collective-permute-start(f32[32,2048]{1,0:T(8,128)S(1)} %get-tuple-element.61), channel_id=1, source_target_pairs={{0,256},{32,288},{64,320},{96,352},{128,384},{160,416},{192,448},{... | collective-permute-start | bytes 786440 | tf_op jit(solution)/shard_map/ppermute | solution.py:214
  97.2 21.1 %collective-permute-start.6 = (f32[32,2048]{1,0:T(8,128)S(1)}, f32[32,2048]{1,0:T(8,128)S(1)}, u32[]{:S(2)}, u32[]{:S(2)}) collective-permute-start(f32[32,2048]{1,0:T(8,128)S(1)} %get-tuple-element.62), channel_id=1, source_target_pairs={{0,64},{32,96},{64,128},{96,160},{128,192},{160,224},{192,256},{22... | collective-permute-start | bytes 786440 | tf_op jit(solution)/shard_map/ppermute | solution.py:214
  103.4 15.6 %collective-permute-start.7 = (f32[32,2048]{1,0:T(8,128)S(1)}, f32[32,2048]{1,0:T(8,128)S(1)}, u32[]{:S(2)}, u32[]{:S(2)}) collective-permute-start(f32[32,2048]{1,0:T(8,128)S(1)} %get-tuple-element.63), channel_id=1, source_target_pairs={{0,448},{32,480},{64,0},{96,32},{128,64},{160,96},{192,128},{224,1... | collective-permute-start | bytes 786440 | tf_op jit(solution)/shard_map/ppermute | solution.py:214

commit v5 on v4

--- a/solution.py
+++ b/solution.py
@@ -12,8 +12,9 @@
 SPACE = "space"
 LANES = 128
 SUBLANES = 8
-FIRST = (3, 5, 2, 6)
-THEN = (4, 1, 7, 0)
+FIRST = (3, 5)
+SECOND = (2, 6, 1)
+THIRD = (4, 7, 0)
 IN_VMEM = pl.BlockSpec(memory_space=pltpu.VMEM)
 IN_SMEM = pl.BlockSpec(memory_space=pltpu.SMEM)
 KERNEL = pltpu.CompilerParams(vmem_limit_bytes=16 * 2**20)
@@ -174,7 +175,7 @@
     *parts, out_ref, state_ref = refs
     chips = len(parts)
     height = parts[0].shape[0]
-    for k, part in zip(FIRST + THEN, parts):
+    for k, part in zip(FIRST + SECOND + THIRD, parts):
         chip = lax.rem(chip_ref[0] - k + chips, chips)
         state_ref[pl.ds(pl.multiple_of(chip * height, height), height), :] = part[...]
     state = state_ref[...]
@@ -276,28 +277,29 @@
     rank = lax.axis_index(MEMBER).astype(jnp.int32)
     chip, core = rank // 2, lax.rem(rank, 2)
 
+    kept, sent = split(core, prior_sample, chips)
+    other = swapped(sent)
     picked = pick(measured_point_location, prior_sample)
-    state, picked = lax.optimization_barrier((prior_sample, picked))
+    picked, other = lax.optimization_barrier((picked, other))
     evolved = lax.all_to_all(picked, MEMBER, 0, 0, tiled=True).reshape(total, LANES)
-
-    kept, sent = split(core, state, chips)
-    pairs = join(chip, core, kept, swapped(sent))
-    evolved, pairs = lax.optimization_barrier((evolved, pairs))
+    pairs = join(chip, core, kept, other)
+    parts = [shifted(pairs[k], k) for k in FIRST]
+    evolved, parts, pairs = lax.optimization_barrier((evolved, parts, pairs))
 
     gram = gram_of(
         rank, measured_slots_used, evolved, measured_data, measurement_noise_sigma
     )
+    parts += [shifted(pairs[k], k) for k in SECOND]
     spaces = lax.axis_size(SPACE)
-    first = [shifted(pairs[k], k) for k in FIRST]
     pieces = gram.reshape(spaces, total // spaces, total)
     pieces = jnp.sum(lax.all_to_all(pieces, SPACE, 0, 0, tiled=True), axis=0)
     pieces = jnp.sum(sent_to_all(pieces, MEMBER), axis=0)
-    pieces, first, pairs = lax.optimization_barrier((pieces, first, pairs))
-    then = [shifted(pairs[k], k) for k in THEN]
+    pieces, parts, pairs = lax.optimization_barrier((pieces, parts, pairs))
+    parts += [shifted(pairs[k], k) for k in THIRD]
     gram = sent_to_all(pieces, SPACE).reshape(total, total)
     transform = transform_of(gram)
 
-    updated = applied(chip, transform, first + then)
+    updated = applied(chip, transform, parts)
     updated = updated.reshape(groups, own_members, own_cells)
     back = lax.all_to_all(updated, MEMBER, 0, 0, tiled=True)
     return back.swapaxes(0, 1).reshape(own_members, cells)

time: 180 us -> 183 us (1.017)
  waiting for transfers between devices: 8.86 us -> 16.1 us
  blocking collectives: 80.4 us -> 73.6 us
  starting transfers between devices: 60.6 us -> 64.5 us
  local copies, waits for them, and re-layouts: 6.58 us -> 4.51 us
    all_to_all x1, blocking collectives: 23.9 us -> 14.9 us  [sent_to_all(): return lax.all_to_all(copies, axis, 0, 0, tiled=True)]
    all_to_all x1, waiting for transfers between devices: 6.18 us -> 12.5 us  [body(): lax.all_to_all(picked, MEMBER, 0, 0, tiled=True).reshape(total, LANES)]
    ppermute x7, starting transfers between devices: 27.9 us -> 31.4 us  [shifted(): lax.ppermute(array, MEMBER, [(i, (i + 2 * k) % groups) for i in range(gro...]
    all_to_all x1, blocking collectives: 56.5 us -> 58.7 us  [body(): back = lax.all_to_all(updated, MEMBER, 0, 0, tiled=True)]
    unnamed x16 -> x12, local copies, waits for them, and re-layouts: 4.39 us -> 2.32 us
  transfers between devices with their start and end apart: 11 -> 11, of which waited for: 3 -> 3; matrix products, arithmetic and copies ran while one was open for 0% -> 0% of each run, Pallas kernels for 6% -> 10%
where the time goes in v5:
time: 183 us; the launch traced here: 182 us
  blocking collectives  73.6 us (40%)
  starting transfers between devices  64.5 us (35%)
  Pallas kernels  22.6 us (12%)
  waiting for transfers between devices  16.1 us (9%)
  local copies, waits for them, and re-layouts  4.51 us (2%)
    all_to_all x1, blocking collectives, body(): back = lax.all_to_all(updated, MEMBER, 0, 0, tiled=True)  58.7 us
    ppermute x7, starting transfers between devices, shifted(): lax.ppermute(array, MEMBER, [(i, (i + 2 * k) % groups) for i in range(gro...  31.4 us
    all_to_all x1, blocking collectives, sent_to_all(): return lax.all_to_all(copies, axis, 0, 0, tiled=True)  14.9 us
    all_to_all x1, starting transfers between devices, body(): pieces = jnp.sum(lax.all_to_all(pieces, SPACE, 0, 0, tiled=True), axis=0)  12.6 us
    all_to_all x1, waiting for transfers between devices, body(): lax.all_to_all(picked, MEMBER, 0, 0, tiled=True).reshape(total, LANES)  12.5 us
    pallas_call x1, Pallas kernels, transform_of(): pl.pallas_call(transform_kernel, out_shape=jax.ShapeDtypeStruct(gram.shap...  10.9 us
    ppermute x1, starting transfers between devices, swapped(): return lax.ppermute(array, MEMBER, [(i, i ^ 1) for i in range(groups)])  8.92 us
    all_to_all x1, starting transfers between devices, sent_to_all(): return lax.all_to_all(copies, axis, 0, 0, tiled=True)  7.69 us
  transfers between devices with their start and end apart: 11, of which 3 were waited for; matrix products, arithmetic and copies ran while one was open for 0% of the time, Pallas kernels for 10%

profile of v5, /device:TPU:1, one launch (start us, length us, event | category | flops | bytes accessed | tf_op | source)
XLA Modules:
  0.0 182.2 jit_solution(675090823410126747)
XLA Ops:
  0.0 0.0 copy-start.2
  0.0 0.0 copy-start
  0.0 1.6 copy-done
  1.6 0.0 copy-start.1
  1.6 0.1 shard_map.56
  1.7 0.0 copy-start.3
  1.8 0.0 copy-start.4
  1.8 8.9 %collective-permute-start = (f32[8,16,2048]{2,1,0:T(8,128)S(1)}, f32[8,16,2048]{2,1,0:T(8,128)S(1)}, u32[]{:S(2)}, u32[]{:S(2)}) collective-permute-start(f32[8,16,2048]{2,1,0:T(8,128)S(1)} %get-tuple-element.35), channel_id=1, source_target_pairs={{0,32},{32,0},{64,96},{96,64},{128,160},{160,128},{192,224},{224,1... | collective-permute-start | bytes 3145736 | tf_op jit(solution)/shard_map/ppermute | solution.py:208
  10.7 0.0 copy-done.2
  10.7 0.0 copy-done.1
  10.7 7.3 %shard_map.55 = f32[16,16,128]{2,1,0:T(8,128)} custom-call(s32[16,128]{1,0:T(8,128)S(1)} %copy-done.2, f32[16,32768]{1,0:T(8,128)S(1)} %copy-done.1), custom_call_target="tpu_custom_call" | custom-call | flops 1024 | bytes 1024 | tf_op jit(solution)/shard_map/pallas_call | solution.py:53
  18.1 0.0 collective-permute-done.other_ref
  18.1 0.9 shard_map.57
  19.0 0.0 copy-start.5
  19.0 0.7 copy-done.5
  19.7 1.9 %collective-permute-start.1 = (f32[32,2048]{1,0:T(8,128)}, f32[32,2048]{1,0:T(8,128)S(1)}, u32[]{:S(2)}, u32[]{:S(2)}) collective-permute-start(f32[32,2048]{1,0:T(8,128)} %get-tuple-element.39), channel_id=1, source_target_pairs={{0,192},{32,224},{64,256},{96,288},{128,320},{160,352},{192,384},{... | collective-permute-start | bytes 786440 | tf_op jit(solution)/shard_map/ppermute | solution.py:215
  21.6 6.4 %collective-permute-start.2 = (f32[32,2048]{1,0:T(8,128)}, f32[32,2048]{1,0:T(8,128)S(1)}, u32[]{:S(2)}, u32[]{:S(2)}) collective-permute-start(f32[32,2048]{1,0:T(8,128)} %get-tuple-element.40), channel_id=1, source_target_pairs={{0,320},{32,352},{64,384},{96,416},{128,448},{160,480},{192,0},{22... | collective-permute-start | bytes 786440 | tf_op jit(solution)/shard_map/ppermute | solution.py:215
  28.0 3.9 %all-to-all-start = ((f32[16,16,128]{2,1,0:T(8,128)}), f32[16,16,128]{2,1,0:T(8,128)S(1)}, u32[]{:S(2)}, u32[]{:S(2)}) async-start(f32[16,16,128]{2,1,0:T(8,128)} %shard_map.55), calls=%async_computation | async-start | bytes 262144 | tf_op jit(solution)/shard_map/all_to_all | solution.py:284
  32.5 12.5 %all-to-all-done = f32[16,16,128]{2,1,0:T(8,128)S(1)} async-done(((f32[16,16,128]{2,1,0:T(8,128)}), f32[16,16,128]{2,1,0:T(8,128)S(1)}, u32[]{:S(2)}, u32[]{:S(2)}) %all-to-all-start) | async-done | bytes 131104 | tf_op jit(solution)/shard_map/all_to_all | solution.py:284
  45.0 0.0 collective-permute-done.1.refs_0_
  45.0 0.0 collective-permute-done.2.refs_1_
  45.0 0.0 copy-done.3
  45.0 0.0 copy-done.4
  45.0 1.2 shard_map.58
  46.3 12.6 %all-to-all-start.1 = ((f32[32,8,256]{2,1,0:T(8,128)}), f32[32,8,256]{2,1,0:T(8,128)S(1)}, u32[]{:S(2)}, u32[]{:S(2)}) async-start(f32[32,8,256]{2,1,0:T(8,128)} %bitcast.4), calls=%async_computation.1 | async-start | bytes 524288 | tf_op jit(solution)/shard_map/all_to_all | solution.py:295
  58.9 6.3 %collective-permute-start.3 = (f32[32,2048]{1,0:T(8,128)}, f32[32,2048]{1,0:T(8,128)S(1)}, u32[]{:S(2)}, u32[]{:S(2)}) collective-permute-start(f32[32,2048]{1,0:T(8,128)} %copy-done.5), channel_id=1, source_target_pairs={{0,128},{32,160},{64,192},{96,224},{128,256},{160,288},{192,320},{... | collective-permute-start | bytes 786440 | tf_op jit(solution)/shard_map/ppermute | solution.py:215
  65.2 1.9 %collective-permute-start.4 = (f32[32,2048]{1,0:T(8,128)S(1)}, f32[32,2048]{1,0:T(8,128)S(1)}, u32[]{:S(2)}, u32[]{:S(2)}) collective-permute-start(f32[32,2048]{1,0:T(8,128)S(1)} %get-tuple-element.51), channel_id=1, source_target_pairs={{0,384},{32,416},{64,448},{96,480},{128,0},{160,32},{192,64},{224,... | collective-permute-start | bytes 786440 | tf_op jit(solution)/shard_map/ppermute | solution.py:215
  67.1 5.4 %collective-permute-start.5 = (f32[32,2048]{1,0:T(8,128)S(1)}, f32[32,2048]{1,0:T(8,128)S(1)}, u32[]{:S(2)}, u32[]{:S(2)}) collective-permute-start(f32[32,2048]{1,0:T(8,128)S(1)} %get-tuple-element.52), channel_id=1, source_target_pairs={{0,64},{32,96},{64,128},{96,160},{128,192},{160,224},{192,256},{22... | collective-permute-start | bytes 786440 | tf_op jit(solution)/shard_map/ppermute | solution.py:215
  72.5 0.0 all-to-all-done.1
  72.6 14.9 %all_to_all.25 = f32[16,8,256]{2,1,0:T(8,128)S(1)} all-to-all(f32[16,8,256]{2,1,0:T(8,128)S(1)} %broadcast_in_dim.4), channel_id=1, replica_groups=mesh['member'=16,'space'=32] {'member'}, dimensions={0} | all-to-all | bytes 262144 | tf_op jit(solution)/shard_map/all_to_all | solution.py:203
  87.5 0.0 collective-permute-done.3.refs_2_
  87.5 0.0 collective-permute-done.4.refs_3_
  87.5 0.0 collective-permute-done.5.refs_4_
  87.5 0.7 broadcast_in_dim.5
  88.2 7.7 %all-to-all-start.3 = ((f32[32,8,256]{2,1,0:T(8,128)}), f32[32,8,256]{2,1,0:T(8,128)S(1)}, u32[]{:S(2)}, u32[]{:S(2)}) async-start(f32[32,8,256]{2,1,0:T(8,128)} %broadcast_in_dim.5), calls=%async_computation.3 | async-start | bytes 524288 | tf_op jit(solution)/shard_map/all_to_all | solution.py:203
  95.9 7.4 %collective-permute-start.6 = (f32[32,2048]{1,0:T(8,128)S(1)}, f32[32,2048]{1,0:T(8,128)S(1)}, u32[]{:S(2)}, u32[]{:S(2)}) collective-permute-start(f32[32,2048]{1,0:T(8,128)S(1)} %get-tuple-element.62), channel_id=1, source_target_pairs={{0,256},{32,288},{64,320},{96,352},{128,384},{160,416},{192,448},{... | collective-permute-start | bytes 786440 | tf_op jit(solution)/shard_map/ppermute | solution.py:215
  103.4 2.1 %collective-permute-start.7 = (f32[32,2048]{1,0:T(8,128)S(1)}, f32[32,2048]{1,0:T(8,128)S(1)}, u32[]{:S(2)}, u32[]{:S(2)}) collective-permute-start(f32[32,2048]{1,0:T(8,128)S(1)} %get-tuple-element.63), channel_id=1, source_target_pairs={{0,448},{32,480},{64,0},{96,32},{128,64},{160,96},{192,128},{224,1... | collective-permute-start | bytes 786440 | tf_op jit(solution)/shard_map/ppermute | solution.py:215
  105.5 1.4 all-to-all-done.3
  106.9 10.9 %shard_map.59.transform_ref = f32[256,256]{1,0:T(8,128)S(1)} custom-call(f32[256,256]{1,0:T(8,128)S(1)} %bitcast.11), custom_call_target="tpu_custom_call" | custom-call | flops 1024 | bytes 1024 | tf_op jit(solution)/shard_map/pallas_call | solution.py:164
  117.8 0.0 collective-permute-done.6.refs_5_
  117.8 2.1 %collective-permute-done.7.refs_6_ = f32[32,2048]{1,0:T(8,128)S(1)} collective-permute-done((f32[32,2048]{1,0:T(8,128)S(1)}, f32[32,2048]{1,0:T(8,128)S(1)}, u32[]{:S(2)}, u32[]{:S(2)}) %collective-permute-start.7) | collective-permute-done | bytes 262176 | tf_op jit(solution)/shard_map/ppermute | solution.py:215
  119.9 2.2 %shard_map.60 = f32[256,2048]{1,0:T(8,128)S(1)} custom-call(s32[1]{0:T(128)} %bitcast.chip_ref, f32[256,256]{1,0:T(8,128)S(1)} %shard_map.59.transform_ref, f32[32,2048]{1,0:T(8,128)S(1)} %collective-permute-done.1.refs_0_, f32[32,2048]{1,0:T(8,128)S(1)} %collective-permute-done.2.refs_1_, f32[32,2048]{1,0:T(8,128)S(1)} %collective-permute-done.3.refs_2_, ...), custom_call_target="tpu_custom_call" | custom-call | flops 1024 | bytes 1024 | tf_op jit(solution)/shard_map/pallas_call | solution.py:189
  122.1 58.7 %all_to_all.26 = f32[16,16,2048]{2,1,0:T(8,128)S(1)} all-to-all(f32[16,16,2048]{2,1,0:T(8,128)S(1)} %bitcast.10), channel_id=1, replica_groups=mesh['member'=16,'space'=32] {'member'}, dimensions={0} | all-to-all | bytes 4194304 | tf_op jit(solution)/shard_map/all_to_all | solution.py:304
  180.8 1.5 copy.8
  (3 shorter events, 0.1 us)
Async XLA Ops:
  0.0 10.7 %copy-start.2 = (s32[16,128]{1,0:T(8,128)S(1)}, s32[16,128]{1,0:T(8,128)}, u32[]{:S(2)}) copy-start(s32[16,128]{1,0:T(8,128)} %places_ref.1) | copy-start | bytes 24580
  0.0 1.6 copy-start
  1.6 9.1 %copy-start.1 = (f32[16,32768]{1,0:T(8,128)S(1)}, f32[16,32768]{1,0:T(8,128)}, u32[]{:S(2)}) copy-start(f32[16,32768]{1,0:T(8,128)} %state_ref.3) | copy-start | bytes 6291460
  1.7 43.3 %copy-start.3 = (f32[16,128]{1,0:T(8,128)S(1)}, f32[16,128]{1,0:T(8,128)}, u32[]{:S(2)}) copy-start(f32[16,128]{1,0:T(8,128)} %data_ref.1) | copy-start | bytes 24580
  1.8 43.3 %copy-start.4 = (f32[16,128]{1,0:T(8,128)S(1)}, f32[16,128]{1,0:T(8,128)}, u32[]{:S(2)}) copy-start(f32[16,128]{1,0:T(8,128)} %sigma_ref.1) | copy-start | bytes 24580
  1.8 16.3 %collective-permute-start = (f32[8,16,2048]{2,1,0:T(8,128)S(1)}, f32[8,16,2048]{2,1,0:T(8,128)S(1)}, u32[]{:S(2)}, u32[]{:S(2)}) collective-permute-start(f32[8,16,2048]{2,1,0:T(8,128)S(1)} %get-tuple-element.35), channel_id=1, source_target_pairs={{0,32},{32,0},{64,96},{96,64},{128,160},{160,128},{192,224},{224,1... | collective-permute-start | bytes 3145736 | tf_op jit(solution)/shard_map/ppermute | solution.py:208
  19.0 0.7 copy-start.5
  19.7 25.3 %collective-permute-start.1 = (f32[32,2048]{1,0:T(8,128)}, f32[32,2048]{1,0:T(8,128)S(1)}, u32[]{:S(2)}, u32[]{:S(2)}) collective-permute-start(f32[32,2048]{1,0:T(8,128)} %get-tuple-element.39), channel_id=1, source_target_pairs={{0,192},{32,224},{64,256},{96,288},{128,320},{160,352},{192,384},{... | collective-permute-start | bytes 786440 | tf_op jit(solution)/shard_map/ppermute | solution.py:215
  21.6 23.4 %collective-permute-start.2 = (f32[32,2048]{1,0:T(8,128)}, f32[32,2048]{1,0:T(8,128)S(1)}, u32[]{:S(2)}, u32[]{:S(2)}) collective-permute-start(f32[32,2048]{1,0:T(8,128)} %get-tuple-element.40), channel_id=1, source_target_pairs={{0,320},{32,352},{64,384},{96,416},{128,448},{160,480},{192,0},{22... | collective-permute-start | bytes 786440 | tf_op jit(solution)/shard_map/ppermute | solution.py:215
  28.0 17.1 %all-to-all-start = ((f32[16,16,128]{2,1,0:T(8,128)}), f32[16,16,128]{2,1,0:T(8,128)S(1)}, u32[]{:S(2)}, u32[]{:S(2)}) async-start(f32[16,16,128]{2,1,0:T(8,128)} %shard_map.55), calls=%async_computation | async-start | bytes 262144 | tf_op jit(solution)/shard_map/all_to_all | solution.py:284
  46.3 26.3 %all-to-all-start.1 = ((f32[32,8,256]{2,1,0:T(8,128)}), f32[32,8,256]{2,1,0:T(8,128)S(1)}, u32[]{:S(2)}, u32[]{:S(2)}) async-start(f32[32,8,256]{2,1,0:T(8,128)} %bitcast.4), calls=%async_computation.1 | async-start | bytes 524288 | tf_op jit(solution)/shard_map/all_to_all | solution.py:295
  58.9 28.6 %collective-permute-start.3 = (f32[32,2048]{1,0:T(8,128)}, f32[32,2048]{1,0:T(8,128)S(1)}, u32[]{:S(2)}, u32[]{:S(2)}) collective-permute-start(f32[32,2048]{1,0:T(8,128)} %copy-done.5), channel_id=1, source_target_pairs={{0,128},{32,160},{64,192},{96,224},{128,256},{160,288},{192,320},{... | collective-permute-start | bytes 786440 | tf_op jit(solution)/shard_map/ppermute | solution.py:215
  65.2 22.3 %collective-permute-start.4 = (f32[32,2048]{1,0:T(8,128)S(1)}, f32[32,2048]{1,0:T(8,128)S(1)}, u32[]{:S(2)}, u32[]{:S(2)}) collective-permute-start(f32[32,2048]{1,0:T(8,128)S(1)} %get-tuple-element.51), channel_id=1, source_target_pairs={{0,384},{32,416},{64,448},{96,480},{128,0},{160,32},{192,64},{224,... | collective-permute-start | bytes 786440 | tf_op jit(solution)/shard_map/ppermute | solution.py:215
  67.1 20.4 %collective-permute-start.5 = (f32[32,2048]{1,0:T(8,128)S(1)}, f32[32,2048]{1,0:T(8,128)S(1)}, u32[]{:S(2)}, u32[]{:S(2)}) collective-permute-start(f32[32,2048]{1,0:T(8,128)S(1)} %get-tuple-element.52), channel_id=1, source_target_pairs={{0,64},{32,96},{64,128},{96,160},{128,192},{160,224},{192,256},{22... | collective-permute-start | bytes 786440 | tf_op jit(solution)/shard_map/ppermute | solution.py:215
  88.2 18.7 %all-to-all-start.3 = ((f32[32,8,256]{2,1,0:T(8,128)}), f32[32,8,256]{2,1,0:T(8,128)S(1)}, u32[]{:S(2)}, u32[]{:S(2)}) async-start(f32[32,8,256]{2,1,0:T(8,128)} %broadcast_in_dim.5), calls=%async_computation.3 | async-start | bytes 524288 | tf_op jit(solution)/shard_map/all_to_all | solution.py:203
  95.9 21.9 %collective-permute-start.6 = (f32[32,2048]{1,0:T(8,128)S(1)}, f32[32,2048]{1,0:T(8,128)S(1)}, u32[]{:S(2)}, u32[]{:S(2)}) collective-permute-start(f32[32,2048]{1,0:T(8,128)S(1)} %get-tuple-element.62), channel_id=1, source_target_pairs={{0,256},{32,288},{64,320},{96,352},{128,384},{160,416},{192,448},{... | collective-permute-start | bytes 786440 | tf_op jit(solution)/shard_map/ppermute | solution.py:215
  103.4 16.5 %collective-permute-start.7 = (f32[32,2048]{1,0:T(8,128)S(1)}, f32[32,2048]{1,0:T(8,128)S(1)}, u32[]{:S(2)}, u32[]{:S(2)}) collective-permute-start(f32[32,2048]{1,0:T(8,128)S(1)} %get-tuple-element.63), channel_id=1, source_target_pairs={{0,448},{32,480},{64,0},{96,32},{128,64},{160,96},{192,128},{224,1... | collective-permute-start | bytes 786440 | tf_op jit(solution)/shard_map/ppermute | solution.py:215

commit v6 on v4

--- a/solution.py
+++ b/solution.py
@@ -12,8 +12,8 @@
 SPACE = "space"
 LANES = 128
 SUBLANES = 8
-FIRST = (3, 5, 2, 6)
-THEN = (4, 1, 7, 0)
+FIRST = (3, 5, 2)
+THEN = (4, 6, 1, 7, 0)
 IN_VMEM = pl.BlockSpec(memory_space=pltpu.VMEM)
 IN_SMEM = pl.BlockSpec(memory_space=pltpu.SMEM)
 KERNEL = pltpu.CompilerParams(vmem_limit_bytes=16 * 2**20)

time: 180 us -> 184 us (1.022)
  waiting for transfers between devices: 8.86 us -> 14.2 us
    ppermute x7, waiting for transfers between devices: 2.67 us -> 6.18 us  [shifted(): lax.ppermute(array, MEMBER, [(i, (i + 2 * k) % groups) for i in range(gro...]
    all_to_all x1, waiting for transfers between devices: 0.01 us -> 1.87 us  [body(): pieces = jnp.sum(lax.all_to_all(pieces, SPACE, 0, 0, tiled=True), axis=0)]
  transfers between devices with their start and end apart: 11 -> 11, of which waited for: 3 -> 4; matrix products, arithmetic and copies ran while one was open for 0% -> 0% of each run, Pallas kernels for 6% -> 6%
where the time goes in v6:
time: 184 us; the launch traced here: 183 us
  blocking collectives  80 us (43%)
  starting transfers between devices  59.5 us (32%)
  Pallas kernels  21.8 us (12%)
  waiting for transfers between devices  14.2 us (8%)
  local copies, waits for them, and re-layouts  6.58 us (4%)
    all_to_all x1, blocking collectives, body(): back = lax.all_to_all(updated, MEMBER, 0, 0, tiled=True)  56 us
    ppermute x7, starting transfers between devices, shifted(): lax.ppermute(array, MEMBER, [(i, (i + 2 * k) % groups) for i in range(gro...  26.6 us
    all_to_all x1, blocking collectives, sent_to_all(): return lax.all_to_all(copies, axis, 0, 0, tiled=True)  24 us
    all_to_all x1, starting transfers between devices, body(): pieces = jnp.sum(lax.all_to_all(pieces, SPACE, 0, 0, tiled=True), axis=0)  11.4 us
    pallas_call x1, Pallas kernels, transform_of(): pl.pallas_call(transform_kernel, out_shape=jax.ShapeDtypeStruct(gram.shap...  10.9 us
    all_to_all x1, starting transfers between devices, sent_to_all(): return lax.all_to_all(copies, axis, 0, 0, tiled=True)  9.25 us
    ppermute x1, starting transfers between devices, swapped(): return lax.ppermute(array, MEMBER, [(i, i ^ 1) for i in range(groups)])  8.79 us
    pallas_call x1, Pallas kernels, pick(): pl.pallas_call(pick_kernel, out_shape=jax.ShapeDtypeStruct((places.shape[...  7.32 us
  transfers between devices with their start and end apart: 11, of which 4 were waited for; matrix products, arithmetic and copies ran while one was open for 0% of the time, Pallas kernels for 6%

profile of v6, /device:TPU:1, one launch (start us, length us, event | category | flops | bytes accessed | tf_op | source)
XLA Modules:
  0.0 183.1 jit_solution(17080397710663898487)
XLA Ops:
  0.0 0.0 copy-start
  0.0 1.6 copy-done
  1.6 0.0 copy-start.2
  1.6 0.7 copy-done.2
  2.3 0.0 copy-start.1
  2.3 7.3 %shard_map.55 = f32[16,16,128]{2,1,0:T(8,128)} custom-call(s32[16,128]{1,0:T(8,128)S(1)} %copy-done.2, f32[16,32768]{1,0:T(8,128)S(1)} %copy-done), custom_call_target="tpu_custom_call" | custom-call | flops 1024 | bytes 1024 | tf_op jit(solution)/shard_map/pallas_call | solution.py:52
  9.6 0.0 copy-done.1
  9.6 0.0 copy-start.3
  9.6 0.0 copy-start.4
  9.6 0.1 shard_map.56
  9.8 8.8 %collective-permute-start = (f32[8,16,2048]{2,1,0:T(8,128)S(1)}, f32[8,16,2048]{2,1,0:T(8,128)S(1)}, u32[]{:S(2)}, u32[]{:S(2)}) collective-permute-start(f32[8,16,2048]{2,1,0:T(8,128)S(1)} %get-tuple-element.38), channel_id=1, source_target_pairs={{0,32},{32,0},{64,96},{96,64},{128,160},{160,128},{192,224},{224,1... | collective-permute-start | bytes 3145736 | tf_op jit(solution)/shard_map/ppermute | solution.py:207
  18.6 3.4 %all-to-all-start = ((f32[16,16,128]{2,1,0:T(8,128)}), f32[16,16,128]{2,1,0:T(8,128)S(1)}, u32[]{:S(2)}, u32[]{:S(2)}) async-start(f32[16,16,128]{2,1,0:T(8,128)} %shard_map.55), calls=%async_computation | async-start | bytes 262144 | tf_op jit(solution)/shard_map/all_to_all | solution.py:281
  22.6 0.0 collective-permute-done.other_ref
  22.7 0.1 shard_map.57
  22.8 0.0 copy-start.5
  22.8 0.7 copy-done.5
  23.5 0.0 copy-start.6
  23.5 0.7 copy-done.6
  24.2 0.0 copy-start.7
  24.2 0.7 copy-done.7
  24.9 6.2 %all-to-all-done = f32[16,16,128]{2,1,0:T(8,128)S(1)} async-done(((f32[16,16,128]{2,1,0:T(8,128)}), f32[16,16,128]{2,1,0:T(8,128)S(1)}, u32[]{:S(2)}, u32[]{:S(2)}) %all-to-all-start) | async-done | bytes 131104 | tf_op jit(solution)/shard_map/all_to_all | solution.py:281
  31.1 0.0 copy-done.3
  31.1 0.0 copy-done.4
  31.1 1.2 shard_map.58
  32.3 11.4 %all-to-all-start.1 = ((f32[32,8,256]{2,1,0:T(8,128)}), f32[32,8,256]{2,1,0:T(8,128)S(1)}, u32[]{:S(2)}, u32[]{:S(2)}) async-start(f32[32,8,256]{2,1,0:T(8,128)} %bitcast.4), calls=%async_computation.1 | async-start | bytes 524288 | tf_op jit(solution)/shard_map/all_to_all | solution.py:293
  43.7 2.3 %collective-permute-start.1 = (f32[32,2048]{1,0:T(8,128)}, f32[32,2048]{1,0:T(8,128)S(1)}, u32[]{:S(2)}, u32[]{:S(2)}) collective-permute-start(f32[32,2048]{1,0:T(8,128)} %copy-done.7), channel_id=1, source_target_pairs={{0,192},{32,224},{64,256},{96,288},{128,320},{160,352},{192,384},{... | collective-permute-start | bytes 786440 | tf_op jit(solution)/shard_map/ppermute | solution.py:214
  46.0 6.0 %collective-permute-start.2 = (f32[32,2048]{1,0:T(8,128)}, f32[32,2048]{1,0:T(8,128)S(1)}, u32[]{:S(2)}, u32[]{:S(2)}) collective-permute-start(f32[32,2048]{1,0:T(8,128)} %copy-done.6), channel_id=1, source_target_pairs={{0,320},{32,352},{64,384},{96,416},{128,448},{160,480},{192,0},{22... | collective-permute-start | bytes 786440 | tf_op jit(solution)/shard_map/ppermute | solution.py:214
  52.0 2.1 %collective-permute-start.3 = (f32[32,2048]{1,0:T(8,128)}, f32[32,2048]{1,0:T(8,128)S(1)}, u32[]{:S(2)}, u32[]{:S(2)}) collective-permute-start(f32[32,2048]{1,0:T(8,128)} %copy-done.5), channel_id=1, source_target_pairs={{0,128},{32,160},{64,192},{96,224},{128,256},{160,288},{192,320},{... | collective-permute-start | bytes 786440 | tf_op jit(solution)/shard_map/ppermute | solution.py:214
  54.1 1.9 %all-to-all-done.1 = f32[32,8,256]{2,1,0:T(8,128)S(1)} async-done(((f32[32,8,256]{2,1,0:T(8,128)}), f32[32,8,256]{2,1,0:T(8,128)S(1)}, u32[]{:S(2)}, u32[]{:S(2)}) %all-to-all-start.1) | async-done | bytes 262176 | tf_op jit(solution)/shard_map/all_to_all | solution.py:293
  56.1 24.0 %all_to_all.25 = f32[16,8,256]{2,1,0:T(8,128)S(1)} all-to-all(f32[16,8,256]{2,1,0:T(8,128)S(1)} %broadcast_in_dim.4), channel_id=1, replica_groups=mesh['member'=16,'space'=32] {'member'}, dimensions={0} | all-to-all | bytes 262144 | tf_op jit(solution)/shard_map/all_to_all | solution.py:202
  80.1 0.0 collective-permute-done.1.refs_0_
  80.1 0.0 collective-permute-done.2.refs_1_
  80.1 0.0 collective-permute-done.3.refs_2_
  80.1 0.7 broadcast_in_dim.5
  80.9 9.2 %all-to-all-start.3 = ((f32[32,8,256]{2,1,0:T(8,128)}), f32[32,8,256]{2,1,0:T(8,128)S(1)}, u32[]{:S(2)}, u32[]{:S(2)}) async-start(f32[32,8,256]{2,1,0:T(8,128)} %broadcast_in_dim.5), calls=%async_computation.3 | async-start | bytes 524288 | tf_op jit(solution)/shard_map/all_to_all | solution.py:202
  90.1 4.0 %collective-permute-start.4 = (f32[32,2048]{1,0:T(8,128)S(1)}, f32[32,2048]{1,0:T(8,128)S(1)}, u32[]{:S(2)}, u32[]{:S(2)}) collective-permute-start(f32[32,2048]{1,0:T(8,128)S(1)} %get-tuple-element.60), channel_id=1, source_target_pairs={{0,256},{32,288},{64,320},{96,352},{128,384},{160,416},{192,448},{... | collective-permute-start | bytes 786440 | tf_op jit(solution)/shard_map/ppermute | solution.py:214
  94.2 5.5 %collective-permute-start.5 = (f32[32,2048]{1,0:T(8,128)S(1)}, f32[32,2048]{1,0:T(8,128)S(1)}, u32[]{:S(2)}, u32[]{:S(2)}) collective-permute-start(f32[32,2048]{1,0:T(8,128)S(1)} %get-tuple-element.61), channel_id=1, source_target_pairs={{0,384},{32,416},{64,448},{96,480},{128,0},{160,32},{192,64},{224,... | collective-permute-start | bytes 786440 | tf_op jit(solution)/shard_map/ppermute | solution.py:214
  99.7 1.9 %collective-permute-start.6 = (f32[32,2048]{1,0:T(8,128)S(1)}, f32[32,2048]{1,0:T(8,128)S(1)}, u32[]{:S(2)}, u32[]{:S(2)}) collective-permute-start(f32[32,2048]{1,0:T(8,128)S(1)} %get-tuple-element.62), channel_id=1, source_target_pairs={{0,64},{32,96},{64,128},{96,160},{128,192},{160,224},{192,256},{22... | collective-permute-start | bytes 786440 | tf_op jit(solution)/shard_map/ppermute | solution.py:214
  101.6 4.8 %collective-permute-start.7 = (f32[32,2048]{1,0:T(8,128)S(1)}, f32[32,2048]{1,0:T(8,128)S(1)}, u32[]{:S(2)}, u32[]{:S(2)}) collective-permute-start(f32[32,2048]{1,0:T(8,128)S(1)} %get-tuple-element.63), channel_id=1, source_target_pairs={{0,448},{32,480},{64,0},{96,32},{128,64},{160,96},{192,128},{224,1... | collective-permute-start | bytes 786440 | tf_op jit(solution)/shard_map/ppermute | solution.py:214
  106.4 0.0 all-to-all-done.3
  106.4 10.9 %shard_map.59.transform_ref = f32[256,256]{1,0:T(8,128)S(1)} custom-call(f32[256,256]{1,0:T(8,128)S(1)} %bitcast.11), custom_call_target="tpu_custom_call" | custom-call | flops 1024 | bytes 1024 | tf_op jit(solution)/shard_map/pallas_call | solution.py:163
  117.3 0.0 collective-permute-done.4.refs_3_
  117.3 1.9 %collective-permute-done.5.refs_4_ = f32[32,2048]{1,0:T(8,128)S(1)} collective-permute-done((f32[32,2048]{1,0:T(8,128)S(1)}, f32[32,2048]{1,0:T(8,128)S(1)}, u32[]{:S(2)}, u32[]{:S(2)}) %collective-permute-start.5) | collective-permute-done | bytes 262176 | tf_op jit(solution)/shard_map/ppermute | solution.py:214
  119.1 0.0 collective-permute-done.6.refs_5_
  119.1 4.3 %collective-permute-done.7.refs_6_ = f32[32,2048]{1,0:T(8,128)S(1)} collective-permute-done((f32[32,2048]{1,0:T(8,128)S(1)}, f32[32,2048]{1,0:T(8,128)S(1)}, u32[]{:S(2)}, u32[]{:S(2)}) %collective-permute-start.7) | collective-permute-done | bytes 262176 | tf_op jit(solution)/shard_map/ppermute | solution.py:214
  123.4 2.1 %shard_map.60 = f32[256,2048]{1,0:T(8,128)S(1)} custom-call(s32[1]{0:T(128)} %bitcast.chip_ref, f32[256,256]{1,0:T(8,128)S(1)} %shard_map.59.transform_ref, f32[32,2048]{1,0:T(8,128)S(1)} %collective-permute-done.1.refs_0_, f32[32,2048]{1,0:T(8,128)S(1)} %collective-permute-done.2.refs_1_, f32[32,2048]{1,0:T(8,128)S(1)} %collective-permute-done.3.refs_2_, ...), custom_call_target="tpu_custom_call" | custom-call | flops 1024 | bytes 1024 | tf_op jit(solution)/shard_map/pallas_call | solution.py:188
  125.6 56.0 %all_to_all.26 = f32[16,16,2048]{2,1,0:T(8,128)S(1)} all-to-all(f32[16,16,2048]{2,1,0:T(8,128)S(1)} %bitcast.10), channel_id=1, replica_groups=mesh['member'=16,'space'=32] {'member'}, dimensions={0} | all-to-all | bytes 4194304 | tf_op jit(solution)/shard_map/all_to_all | solution.py:302
  181.6 1.5 copy.8
  (3 shorter events, 0.1 us)
Async XLA Ops:
  0.0 1.6 copy-start
  1.6 0.7 copy-start.2
  2.3 7.3 %copy-start.1 = (f32[16,32768]{1,0:T(8,128)S(1)}, f32[16,32768]{1,0:T(8,128)}, u32[]{:S(2)}) copy-start(f32[16,32768]{1,0:T(8,128)} %state_ref.2) | copy-start | bytes 6291460
  9.6 21.5 %copy-start.3 = (f32[16,128]{1,0:T(8,128)S(1)}, f32[16,128]{1,0:T(8,128)}, u32[]{:S(2)}) copy-start(f32[16,128]{1,0:T(8,128)} %data_ref.1) | copy-start | bytes 24580
  9.6 21.5 %copy-start.4 = (f32[16,128]{1,0:T(8,128)S(1)}, f32[16,128]{1,0:T(8,128)}, u32[]{:S(2)}) copy-start(f32[16,128]{1,0:T(8,128)} %sigma_ref.1) | copy-start | bytes 24580
  9.8 12.9 %collective-permute-start = (f32[8,16,2048]{2,1,0:T(8,128)S(1)}, f32[8,16,2048]{2,1,0:T(8,128)S(1)}, u32[]{:S(2)}, u32[]{:S(2)}) collective-permute-start(f32[8,16,2048]{2,1,0:T(8,128)S(1)} %get-tuple-element.38), channel_id=1, source_target_pairs={{0,32},{32,0},{64,96},{96,64},{128,160},{160,128},{192,224},{224,1... | collective-permute-start | bytes 3145736 | tf_op jit(solution)/shard_map/ppermute | solution.py:207
  18.6 12.5 %all-to-all-start = ((f32[16,16,128]{2,1,0:T(8,128)}), f32[16,16,128]{2,1,0:T(8,128)S(1)}, u32[]{:S(2)}, u32[]{:S(2)}) async-start(f32[16,16,128]{2,1,0:T(8,128)} %shard_map.55), calls=%async_computation | async-start | bytes 262144 | tf_op jit(solution)/shard_map/all_to_all | solution.py:281
  22.8 0.7 copy-start.5
  23.5 0.7 copy-start.6
  24.2 0.7 copy-start.7
  32.3 23.7 %all-to-all-start.1 = ((f32[32,8,256]{2,1,0:T(8,128)}), f32[32,8,256]{2,1,0:T(8,128)S(1)}, u32[]{:S(2)}, u32[]{:S(2)}) async-start(f32[32,8,256]{2,1,0:T(8,128)} %bitcast.4), calls=%async_computation.1 | async-start | bytes 524288 | tf_op jit(solution)/shard_map/all_to_all | solution.py:293
  43.7 36.4 %collective-permute-start.1 = (f32[32,2048]{1,0:T(8,128)}, f32[32,2048]{1,0:T(8,128)S(1)}, u32[]{:S(2)}, u32[]{:S(2)}) collective-permute-start(f32[32,2048]{1,0:T(8,128)} %copy-done.7), channel_id=1, source_target_pairs={{0,192},{32,224},{64,256},{96,288},{128,320},{160,352},{192,384},{... | collective-permute-start | bytes 786440 | tf_op jit(solution)/shard_map/ppermute | solution.py:214
  46.0 34.1 %collective-permute-start.2 = (f32[32,2048]{1,0:T(8,128)}, f32[32,2048]{1,0:T(8,128)S(1)}, u32[]{:S(2)}, u32[]{:S(2)}) collective-permute-start(f32[32,2048]{1,0:T(8,128)} %copy-done.6), channel_id=1, source_target_pairs={{0,320},{32,352},{64,384},{96,416},{128,448},{160,480},{192,0},{22... | collective-permute-start | bytes 786440 | tf_op jit(solution)/shard_map/ppermute | solution.py:214
  52.0 28.1 %collective-permute-start.3 = (f32[32,2048]{1,0:T(8,128)}, f32[32,2048]{1,0:T(8,128)S(1)}, u32[]{:S(2)}, u32[]{:S(2)}) collective-permute-start(f32[32,2048]{1,0:T(8,128)} %copy-done.5), channel_id=1, source_target_pairs={{0,128},{32,160},{64,192},{96,224},{128,256},{160,288},{192,320},{... | collective-permute-start | bytes 786440 | tf_op jit(solution)/shard_map/ppermute | solution.py:214
  80.9 25.5 %all-to-all-start.3 = ((f32[32,8,256]{2,1,0:T(8,128)}), f32[32,8,256]{2,1,0:T(8,128)S(1)}, u32[]{:S(2)}, u32[]{:S(2)}) async-start(f32[32,8,256]{2,1,0:T(8,128)} %broadcast_in_dim.5), calls=%async_computation.3 | async-start | bytes 524288 | tf_op jit(solution)/shard_map/all_to_all | solution.py:202
  90.1 27.2 %collective-permute-start.4 = (f32[32,2048]{1,0:T(8,128)S(1)}, f32[32,2048]{1,0:T(8,128)S(1)}, u32[]{:S(2)}, u32[]{:S(2)}) collective-permute-start(f32[32,2048]{1,0:T(8,128)S(1)} %get-tuple-element.60), channel_id=1, source_target_pairs={{0,256},{32,288},{64,320},{96,352},{128,384},{160,416},{192,448},{... | collective-permute-start | bytes 786440 | tf_op jit(solution)/shard_map/ppermute | solution.py:214
  94.2 25.0 %collective-permute-start.5 = (f32[32,2048]{1,0:T(8,128)S(1)}, f32[32,2048]{1,0:T(8,128)S(1)}, u32[]{:S(2)}, u32[]{:S(2)}) collective-permute-start(f32[32,2048]{1,0:T(8,128)S(1)} %get-tuple-element.61), channel_id=1, source_target_pairs={{0,384},{32,416},{64,448},{96,480},{128,0},{160,32},{192,64},{224,... | collective-permute-start | bytes 786440 | tf_op jit(solution)/shard_map/ppermute | solution.py:214
  99.7 19.4 %collective-permute-start.6 = (f32[32,2048]{1,0:T(8,128)S(1)}, f32[32,2048]{1,0:T(8,128)S(1)}, u32[]{:S(2)}, u32[]{:S(2)}) collective-permute-start(f32[32,2048]{1,0:T(8,128)S(1)} %get-tuple-element.62), channel_id=1, source_target_pairs={{0,64},{32,96},{64,128},{96,160},{128,192},{160,224},{192,256},{22... | collective-permute-start | bytes 786440 | tf_op jit(solution)/shard_map/ppermute | solution.py:214
  101.6 21.8 %collective-permute-start.7 = (f32[32,2048]{1,0:T(8,128)S(1)}, f32[32,2048]{1,0:T(8,128)S(1)}, u32[]{:S(2)}, u32[]{:S(2)}) collective-permute-start(f32[32,2048]{1,0:T(8,128)S(1)} %get-tuple-element.63), channel_id=1, source_target_pairs={{0,448},{32,480},{64,0},{96,32},{128,64},{160,96},{192,128},{224,1... | collective-permute-start | bytes 786440 | tf_op jit(solution)/shard_map/ppermute | solution.py:214

commit v7 on v6

--- a/solution.py
+++ b/solution.py
@@ -12,8 +12,8 @@
 SPACE = "space"
 LANES = 128
 SUBLANES = 8
-FIRST = (3, 5, 2)
-THEN = (4, 6, 1, 7, 0)
+FIRST = (2, 6, 1)
+THEN = (3, 5, 4, 7, 0)
 IN_VMEM = pl.BlockSpec(memory_space=pltpu.VMEM)
 IN_SMEM = pl.BlockSpec(memory_space=pltpu.SMEM)
 KERNEL = pltpu.CompilerParams(vmem_limit_bytes=16 * 2**20)

time: 184 us -> 182 us (0.989)
  waiting for transfers between devices: 14.2 us -> 25.7 us
  blocking collectives: 80 us -> 70.3 us
  starting transfers between devices: 59.5 us -> 56.2 us
    all_to_all x1, blocking collectives: 24 us -> 12.9 us  [sent_to_all(): return lax.all_to_all(copies, axis, 0, 0, tiled=True)]
    ppermute x7, waiting for transfers between devices: 6.18 us -> 16.6 us  [shifted(): lax.ppermute(array, MEMBER, [(i, (i + 2 * k) % groups) for i in range(gro...]
    ppermute x7, starting transfers between devices: 26.6 us -> 23.3 us  [shifted(): lax.ppermute(array, MEMBER, [(i, (i + 2 * k) % groups) for i in range(gro...]
where the time goes in v7:
time: 182 us
  blocking collectives  70.3 us (39%)
  starting transfers between devices  56.2 us (31%)
  waiting for transfers between devices  25.7 us (14%)
  Pallas kernels  21.8 us (12%)
  local copies, waits for them, and re-layouts  6.58 us (4%)
    all_to_all x1, blocking collectives, body(): back = lax.all_to_all(updated, MEMBER, 0, 0, tiled=True)  57.4 us
    ppermute x7, starting transfers between devices, shifted(): lax.ppermute(array, MEMBER, [(i, (i + 2 * k) % groups) for i in range(gro...  23.3 us
    ppermute x7, waiting for transfers between devices, shifted(): lax.ppermute(array, MEMBER, [(i, (i + 2 * k) % groups) for i in range(gro...  16.6 us
    all_to_all x1, blocking collectives, sent_to_all(): return lax.all_to_all(copies, axis, 0, 0, tiled=True)  12.9 us
    all_to_all x1, starting transfers between devices, body(): pieces = jnp.sum(lax.all_to_all(pieces, SPACE, 0, 0, tiled=True), axis=0)  11.4 us
    pallas_call x1, Pallas kernels, transform_of(): pl.pallas_call(transform_kernel, out_shape=jax.ShapeDtypeStruct(gram.shap...  10.9 us
    all_to_all x1, starting transfers between devices, sent_to_all(): return lax.all_to_all(copies, axis, 0, 0, tiled=True)  9.36 us
    ppermute x1, starting transfers between devices, swapped(): return lax.ppermute(array, MEMBER, [(i, i ^ 1) for i in range(groups)])  8.79 us
  transfers between devices with their start and end apart: 11, of which 4 were waited for; matrix products, arithmetic and copies ran while one was open for 0% of the time, Pallas kernels for 6%

profile of v7, /device:TPU:1, one launch (start us, length us, event | category | flops | bytes accessed | tf_op | source)
XLA Modules:
  0.0 181.5 jit_solution(3918135509120847130)
XLA Ops:
  0.0 0.0 copy-start
  0.0 1.6 copy-done
  1.6 0.0 copy-start.2
  1.6 0.7 copy-done.2
  2.3 0.0 copy-start.1
  2.3 7.3 %shard_map.55 = f32[16,16,128]{2,1,0:T(8,128)} custom-call(s32[16,128]{1,0:T(8,128)S(1)} %copy-done.2, f32[16,32768]{1,0:T(8,128)S(1)} %copy-done), custom_call_target="tpu_custom_call" | custom-call | flops 1024 | bytes 1024 | tf_op jit(solution)/shard_map/pallas_call | solution.py:52
  9.6 0.0 copy-done.1
  9.6 0.0 copy-start.3
  9.6 0.0 copy-start.4
  9.6 0.1 shard_map.56
  9.8 8.8 %collective-permute-start = (f32[8,16,2048]{2,1,0:T(8,128)S(1)}, f32[8,16,2048]{2,1,0:T(8,128)S(1)}, u32[]{:S(2)}, u32[]{:S(2)}) collective-permute-start(f32[8,16,2048]{2,1,0:T(8,128)S(1)} %get-tuple-element.38), channel_id=1, source_target_pairs={{0,32},{32,0},{64,96},{96,64},{128,160},{160,128},{192,224},{224,1... | collective-permute-start | bytes 3145736 | tf_op jit(solution)/shard_map/ppermute | solution.py:207
  18.6 3.4 %all-to-all-start = ((f32[16,16,128]{2,1,0:T(8,128)}), f32[16,16,128]{2,1,0:T(8,128)S(1)}, u32[]{:S(2)}, u32[]{:S(2)}) async-start(f32[16,16,128]{2,1,0:T(8,128)} %shard_map.55), calls=%async_computation | async-start | bytes 262144 | tf_op jit(solution)/shard_map/all_to_all | solution.py:281
  22.6 0.0 collective-permute-done.other_ref
  22.7 0.1 shard_map.57
  22.8 0.0 copy-start.5
  22.8 0.7 copy-done.5
  23.5 0.0 copy-start.6
  23.5 0.7 copy-done.6
  24.2 0.0 copy-start.7
  24.2 0.7 copy-done.7
  24.9 6.2 %all-to-all-done = f32[16,16,128]{2,1,0:T(8,128)S(1)} async-done(((f32[16,16,128]{2,1,0:T(8,128)}), f32[16,16,128]{2,1,0:T(8,128)S(1)}, u32[]{:S(2)}, u32[]{:S(2)}) %all-to-all-start) | async-done | bytes 131104 | tf_op jit(solution)/shard_map/all_to_all | solution.py:281
  31.1 0.0 copy-done.3
  31.1 0.0 copy-done.4
  31.1 1.2 shard_map.58
  32.3 11.4 %all-to-all-start.1 = ((f32[32,8,256]{2,1,0:T(8,128)}), f32[32,8,256]{2,1,0:T(8,128)S(1)}, u32[]{:S(2)}, u32[]{:S(2)}) async-start(f32[32,8,256]{2,1,0:T(8,128)} %bitcast.4), calls=%async_computation.1 | async-start | bytes 524288 | tf_op jit(solution)/shard_map/all_to_all | solution.py:293
  43.7 2.1 %collective-permute-start.1 = (f32[32,2048]{1,0:T(8,128)}, f32[32,2048]{1,0:T(8,128)S(1)}, u32[]{:S(2)}, u32[]{:S(2)}) collective-permute-start(f32[32,2048]{1,0:T(8,128)} %copy-done.7), channel_id=1, source_target_pairs={{0,128},{32,160},{64,192},{96,224},{128,256},{160,288},{192,320},{... | collective-permute-start | bytes 786440 | tf_op jit(solution)/shard_map/ppermute | solution.py:214
  45.8 5.3 %collective-permute-start.2 = (f32[32,2048]{1,0:T(8,128)}, f32[32,2048]{1,0:T(8,128)S(1)}, u32[]{:S(2)}, u32[]{:S(2)}) collective-permute-start(f32[32,2048]{1,0:T(8,128)} %copy-done.6), channel_id=1, source_target_pairs={{0,384},{32,416},{64,448},{96,480},{128,0},{160,32},{192,64},{224,... | collective-permute-start | bytes 786440 | tf_op jit(solution)/shard_map/ppermute | solution.py:214
  51.1 2.0 %collective-permute-start.3 = (f32[32,2048]{1,0:T(8,128)}, f32[32,2048]{1,0:T(8,128)S(1)}, u32[]{:S(2)}, u32[]{:S(2)}) collective-permute-start(f32[32,2048]{1,0:T(8,128)} %copy-done.5), channel_id=1, source_target_pairs={{0,64},{32,96},{64,128},{96,160},{128,192},{160,224},{192,256},{22... | collective-permute-start | bytes 786440 | tf_op jit(solution)/shard_map/ppermute | solution.py:214
  53.1 2.9 %all-to-all-done.1 = f32[32,8,256]{2,1,0:T(8,128)S(1)} async-done(((f32[32,8,256]{2,1,0:T(8,128)}), f32[32,8,256]{2,1,0:T(8,128)S(1)}, u32[]{:S(2)}, u32[]{:S(2)}) %all-to-all-start.1) | async-done | bytes 262176 | tf_op jit(solution)/shard_map/all_to_all | solution.py:293
  56.0 12.9 %all_to_all.25 = f32[16,8,256]{2,1,0:T(8,128)S(1)} all-to-all(f32[16,8,256]{2,1,0:T(8,128)S(1)} %broadcast_in_dim.4), channel_id=1, replica_groups=mesh['member'=16,'space'=32] {'member'}, dimensions={0} | all-to-all | bytes 262144 | tf_op jit(solution)/shard_map/all_to_all | solution.py:202
  69.0 0.0 collective-permute-done.1.refs_0_
  69.0 0.0 collective-permute-done.2.refs_1_
  69.0 0.0 collective-permute-done.3.refs_2_
  69.0 0.7 broadcast_in_dim.5
  69.8 9.4 %all-to-all-start.3 = ((f32[32,8,256]{2,1,0:T(8,128)}), f32[32,8,256]{2,1,0:T(8,128)S(1)}, u32[]{:S(2)}, u32[]{:S(2)}) async-start(f32[32,8,256]{2,1,0:T(8,128)} %broadcast_in_dim.5), calls=%async_computation.3 | async-start | bytes 524288 | tf_op jit(solution)/shard_map/all_to_all | solution.py:202
  79.1 2.1 %collective-permute-start.4 = (f32[32,2048]{1,0:T(8,128)S(1)}, f32[32,2048]{1,0:T(8,128)S(1)}, u32[]{:S(2)}, u32[]{:S(2)}) collective-permute-start(f32[32,2048]{1,0:T(8,128)S(1)} %get-tuple-element.60), channel_id=1, source_target_pairs={{0,192},{32,224},{64,256},{96,288},{128,320},{160,352},{192,384},{... | collective-permute-start | bytes 786440 | tf_op jit(solution)/shard_map/ppermute | solution.py:214
  81.2 6.2 %collective-permute-start.5 = (f32[32,2048]{1,0:T(8,128)S(1)}, f32[32,2048]{1,0:T(8,128)S(1)}, u32[]{:S(2)}, u32[]{:S(2)}) collective-permute-start(f32[32,2048]{1,0:T(8,128)S(1)} %get-tuple-element.61), channel_id=1, source_target_pairs={{0,320},{32,352},{64,384},{96,416},{128,448},{160,480},{192,0},{22... | collective-permute-start | bytes 786440 | tf_op jit(solution)/shard_map/ppermute | solution.py:214
  87.4 3.5 %collective-permute-start.6 = (f32[32,2048]{1,0:T(8,128)S(1)}, f32[32,2048]{1,0:T(8,128)S(1)}, u32[]{:S(2)}, u32[]{:S(2)}) collective-permute-start(f32[32,2048]{1,0:T(8,128)S(1)} %get-tuple-element.62), channel_id=1, source_target_pairs={{0,256},{32,288},{64,320},{96,352},{128,384},{160,416},{192,448},{... | collective-permute-start | bytes 786440 | tf_op jit(solution)/shard_map/ppermute | solution.py:214
  91.0 2.1 %collective-permute-start.7 = (f32[32,2048]{1,0:T(8,128)S(1)}, f32[32,2048]{1,0:T(8,128)S(1)}, u32[]{:S(2)}, u32[]{:S(2)}) collective-permute-start(f32[32,2048]{1,0:T(8,128)S(1)} %get-tuple-element.63), channel_id=1, source_target_pairs={{0,448},{32,480},{64,0},{96,32},{128,64},{160,96},{192,128},{224,1... | collective-permute-start | bytes 786440 | tf_op jit(solution)/shard_map/ppermute | solution.py:214
  93.1 0.0 all-to-all-done.3
  93.1 10.9 %shard_map.59.transform_ref = f32[256,256]{1,0:T(8,128)S(1)} custom-call(f32[256,256]{1,0:T(8,128)S(1)} %bitcast.11), custom_call_target="tpu_custom_call" | custom-call | flops 1024 | bytes 1024 | tf_op jit(solution)/shard_map/pallas_call | solution.py:163
  103.9 4.3 %collective-permute-done.4.refs_3_ = f32[32,2048]{1,0:T(8,128)S(1)} collective-permute-done((f32[32,2048]{1,0:T(8,128)S(1)}, f32[32,2048]{1,0:T(8,128)S(1)}, u32[]{:S(2)}, u32[]{:S(2)}) %collective-permute-start.4) | collective-permute-done | bytes 262176 | tf_op jit(solution)/shard_map/ppermute | solution.py:214
  108.3 0.0 collective-permute-done.5.refs_4_
  108.3 0.0 collective-permute-done.6.refs_5_
  108.3 12.2 %collective-permute-done.7.refs_6_ = f32[32,2048]{1,0:T(8,128)S(1)} collective-permute-done((f32[32,2048]{1,0:T(8,128)S(1)}, f32[32,2048]{1,0:T(8,128)S(1)}, u32[]{:S(2)}, u32[]{:S(2)}) %collective-permute-start.7) | collective-permute-done | bytes 262176 | tf_op jit(solution)/shard_map/ppermute | solution.py:214
  120.5 2.2 %shard_map.60 = f32[256,2048]{1,0:T(8,128)S(1)} custom-call(s32[1]{0:T(128)} %bitcast.chip_ref, f32[256,256]{1,0:T(8,128)S(1)} %shard_map.59.transform_ref, f32[32,2048]{1,0:T(8,128)S(1)} %collective-permute-done.1.refs_0_, f32[32,2048]{1,0:T(8,128)S(1)} %collective-permute-done.2.refs_1_, f32[32,2048]{1,0:T(8,128)S(1)} %collective-permute-done.3.refs_2_, ...), custom_call_target="tpu_custom_call" | custom-call | flops 1024 | bytes 1024 | tf_op jit(solution)/shard_map/pallas_call | solution.py:188
  122.7 57.4 %all_to_all.26 = f32[16,16,2048]{2,1,0:T(8,128)S(1)} all-to-all(f32[16,16,2048]{2,1,0:T(8,128)S(1)} %bitcast.10), channel_id=1, replica_groups=mesh['member'=16,'space'=32] {'member'}, dimensions={0} | all-to-all | bytes 4194304 | tf_op jit(solution)/shard_map/all_to_all | solution.py:302
  180.1 1.5 copy.8
  (3 shorter events, 0.1 us)
Async XLA Ops:
  0.0 1.6 copy-start
  1.6 0.7 copy-start.2
  2.3 7.3 %copy-start.1 = (f32[16,32768]{1,0:T(8,128)S(1)}, f32[16,32768]{1,0:T(8,128)}, u32[]{:S(2)}) copy-start(f32[16,32768]{1,0:T(8,128)} %state_ref.2) | copy-start | bytes 6291460
  9.6 21.5 %copy-start.3 = (f32[16,128]{1,0:T(8,128)S(1)}, f32[16,128]{1,0:T(8,128)}, u32[]{:S(2)}) copy-start(f32[16,128]{1,0:T(8,128)} %data_ref.1) | copy-start | bytes 24580
  9.6 21.5 %copy-start.4 = (f32[16,128]{1,0:T(8,128)S(1)}, f32[16,128]{1,0:T(8,128)}, u32[]{:S(2)}) copy-start(f32[16,128]{1,0:T(8,128)} %sigma_ref.1) | copy-start | bytes 24580
  9.8 12.9 %collective-permute-start = (f32[8,16,2048]{2,1,0:T(8,128)S(1)}, f32[8,16,2048]{2,1,0:T(8,128)S(1)}, u32[]{:S(2)}, u32[]{:S(2)}) collective-permute-start(f32[8,16,2048]{2,1,0:T(8,128)S(1)} %get-tuple-element.38), channel_id=1, source_target_pairs={{0,32},{32,0},{64,96},{96,64},{128,160},{160,128},{192,224},{224,1... | collective-permute-start | bytes 3145736 | tf_op jit(solution)/shard_map/ppermute | solution.py:207
  18.6 12.5 %all-to-all-start = ((f32[16,16,128]{2,1,0:T(8,128)}), f32[16,16,128]{2,1,0:T(8,128)S(1)}, u32[]{:S(2)}, u32[]{:S(2)}) async-start(f32[16,16,128]{2,1,0:T(8,128)} %shard_map.55), calls=%async_computation | async-start | bytes 262144 | tf_op jit(solution)/shard_map/all_to_all | solution.py:281
  22.8 0.7 copy-start.5
  23.5 0.7 copy-start.6
  24.2 0.7 copy-start.7
  32.3 23.7 %all-to-all-start.1 = ((f32[32,8,256]{2,1,0:T(8,128)}), f32[32,8,256]{2,1,0:T(8,128)S(1)}, u32[]{:S(2)}, u32[]{:S(2)}) async-start(f32[32,8,256]{2,1,0:T(8,128)} %bitcast.4), calls=%async_computation.1 | async-start | bytes 524288 | tf_op jit(solution)/shard_map/all_to_all | solution.py:293
  43.7 25.3 %collective-permute-start.1 = (f32[32,2048]{1,0:T(8,128)}, f32[32,2048]{1,0:T(8,128)S(1)}, u32[]{:S(2)}, u32[]{:S(2)}) collective-permute-start(f32[32,2048]{1,0:T(8,128)} %copy-done.7), channel_id=1, source_target_pairs={{0,128},{32,160},{64,192},{96,224},{128,256},{160,288},{192,320},{... | collective-permute-start | bytes 786440 | tf_op jit(solution)/shard_map/ppermute | solution.py:214
  45.8 23.2 %collective-permute-start.2 = (f32[32,2048]{1,0:T(8,128)}, f32[32,2048]{1,0:T(8,128)S(1)}, u32[]{:S(2)}, u32[]{:S(2)}) collective-permute-start(f32[32,2048]{1,0:T(8,128)} %copy-done.6), channel_id=1, source_target_pairs={{0,384},{32,416},{64,448},{96,480},{128,0},{160,32},{192,64},{224,... | collective-permute-start | bytes 786440 | tf_op jit(solution)/shard_map/ppermute | solution.py:214
  51.1 17.9 %collective-permute-start.3 = (f32[32,2048]{1,0:T(8,128)}, f32[32,2048]{1,0:T(8,128)S(1)}, u32[]{:S(2)}, u32[]{:S(2)}) collective-permute-start(f32[32,2048]{1,0:T(8,128)} %copy-done.5), channel_id=1, source_target_pairs={{0,64},{32,96},{64,128},{96,160},{128,192},{160,224},{192,256},{22... | collective-permute-start | bytes 786440 | tf_op jit(solution)/shard_map/ppermute | solution.py:214
  69.8 23.3 %all-to-all-start.3 = ((f32[32,8,256]{2,1,0:T(8,128)}), f32[32,8,256]{2,1,0:T(8,128)S(1)}, u32[]{:S(2)}, u32[]{:S(2)}) async-start(f32[32,8,256]{2,1,0:T(8,128)} %broadcast_in_dim.5), calls=%async_computation.3 | async-start | bytes 524288 | tf_op jit(solution)/shard_map/all_to_all | solution.py:202
  79.1 29.2 %collective-permute-start.4 = (f32[32,2048]{1,0:T(8,128)S(1)}, f32[32,2048]{1,0:T(8,128)S(1)}, u32[]{:S(2)}, u32[]{:S(2)}) collective-permute-start(f32[32,2048]{1,0:T(8,128)S(1)} %get-tuple-element.60), channel_id=1, source_target_pairs={{0,192},{32,224},{64,256},{96,288},{128,320},{160,352},{192,384},{... | collective-permute-start | bytes 786440 | tf_op jit(solution)/shard_map/ppermute | solution.py:214
  81.2 27.1 %collective-permute-start.5 = (f32[32,2048]{1,0:T(8,128)S(1)}, f32[32,2048]{1,0:T(8,128)S(1)}, u32[]{:S(2)}, u32[]{:S(2)}) collective-permute-start(f32[32,2048]{1,0:T(8,128)S(1)} %get-tuple-element.61), channel_id=1, source_target_pairs={{0,320},{32,352},{64,384},{96,416},{128,448},{160,480},{192,0},{22... | collective-permute-start | bytes 786440 | tf_op jit(solution)/shard_map/ppermute | solution.py:214
  87.4 20.9 %collective-permute-start.6 = (f32[32,2048]{1,0:T(8,128)S(1)}, f32[32,2048]{1,0:T(8,128)S(1)}, u32[]{:S(2)}, u32[]{:S(2)}) collective-permute-start(f32[32,2048]{1,0:T(8,128)S(1)} %get-tuple-element.62), channel_id=1, source_target_pairs={{0,256},{32,288},{64,320},{96,352},{128,384},{160,416},{192,448},{... | collective-permute-start | bytes 786440 | tf_op jit(solution)/shard_map/ppermute | solution.py:214
  91.0 29.5 %collective-permute-start.7 = (f32[32,2048]{1,0:T(8,128)S(1)}, f32[32,2048]{1,0:T(8,128)S(1)}, u32[]{:S(2)}, u32[]{:S(2)}) collective-permute-start(f32[32,2048]{1,0:T(8,128)S(1)} %get-tuple-element.63), channel_id=1, source_target_pairs={{0,448},{32,480},{64,0},{96,32},{128,64},{160,96},{192,128},{224,1... | collective-permute-start | bytes 786440 | tf_op jit(solution)/shard_map/ppermute | solution.py:214

commit v8 on v7

--- a/solution.py
+++ b/solution.py
@@ -12,8 +12,9 @@
 SPACE = "space"
 LANES = 128
 SUBLANES = 8
-FIRST = (2, 6, 1)
-THEN = (3, 5, 4, 7, 0)
+FIRST = (1, 7)
+SECOND = (3, 5)
+THIRD = (4, 2, 6, 0)
 IN_VMEM = pl.BlockSpec(memory_space=pltpu.VMEM)
 IN_SMEM = pl.BlockSpec(memory_space=pltpu.SMEM)
 KERNEL = pltpu.CompilerParams(vmem_limit_bytes=16 * 2**20)
@@ -174,7 +175,7 @@
     *parts, out_ref, state_ref = refs
     chips = len(parts)
     height = parts[0].shape[0]
-    for k, part in zip(FIRST + THEN, parts):
+    for k, part in zip(FIRST + SECOND + THIRD, parts):
         chip = lax.rem(chip_ref[0] - k + chips, chips)
         state_ref[pl.ds(pl.multiple_of(chip * height, height), height), :] = part[...]
     state = state_ref[...]
@@ -287,17 +288,18 @@
     gram = gram_of(
         rank, measured_slots_used, evolved, measured_data, measurement_noise_sigma
     )
-    spaces = lax.axis_size(SPACE)
-    first = [shifted(pairs[k], k) for k in FIRST]
-    pieces = gram.reshape(spaces, total // spaces, total)
-    pieces = jnp.sum(lax.all_to_all(pieces, SPACE, 0, 0, tiled=True), axis=0)
-    pieces = jnp.sum(sent_to_all(pieces, MEMBER), axis=0)
-    pieces, first, pairs = lax.optimization_barrier((pieces, first, pairs))
-    then = [shifted(pairs[k], k) for k in THEN]
-    gram = sent_to_all(pieces, SPACE).reshape(total, total)
+    parts = [shifted(pairs[k], k) for k in FIRST]
+    pieces = gram.reshape(groups, own_members, total)
+    pieces = jnp.sum(lax.all_to_all(pieces, MEMBER, 0, 0, tiled=True), axis=0)
+    pieces, parts, pairs = lax.optimization_barrier((pieces, parts, pairs))
+    parts += [shifted(pairs[k], k) for k in SECOND]
+    pieces = jnp.sum(sent_to_all(pieces, SPACE), axis=0)
+    pieces, parts, pairs = lax.optimization_barrier((pieces, parts, pairs))
+    parts += [shifted(pairs[k], k) for k in THIRD]
+    gram = sent_to_all(pieces, MEMBER).reshape(total, total)
     transform = transform_of(gram)
 
-    updated = applied(chip, transform, first + then)
+    updated = applied(chip, transform, parts)
     updated = updated.reshape(groups, own_members, own_cells)
     back = lax.all_to_all(updated, MEMBER, 0, 0, tiled=True)
     return back.swapaxes(0, 1).reshape(own_members, cells)

time: 182 us -> 188 us (1.033)
  blocking collectives: 70.3 us -> 55 us
  waiting for transfers between devices: 25.7 us -> 36.6 us
  starting transfers between devices: 56.2 us -> 65.3 us
    all_to_all x1 -> x0, blocking collectives: 12.9 us -> none  [sent_to_all(): return lax.all_to_all(copies, axis, 0, 0, tiled=True)]
    all_to_all x1 -> x2, starting transfers between devices: 9.36 us -> 20.1 us  [sent_to_all(): return lax.all_to_all(copies, axis, 0, 0, tiled=True)]
    all_to_all x1, starting transfers between devices: 11.4 us -> 3.43 us  [body(): pieces = jnp.sum(lax.all_to_all(pieces, MEMBER, 0, 0, tiled=True), axis=0)]
    all_to_all x1 -> x2, waiting for transfers between devices: 0.01 us -> 7.14 us  [sent_to_all(): return lax.all_to_all(copies, axis, 0, 0, tiled=True)]
    ppermute x7, starting transfers between devices: 23.3 us -> 29.6 us  [shifted(): lax.ppermute(array, MEMBER, [(i, (i + 2 * k) % groups) for i in range(gro...]
    all_to_all x1, blocking collectives: 57.4 us -> 55 us  [body(): back = lax.all_to_all(updated, MEMBER, 0, 0, tiled=True)]
    ppermute x7, waiting for transfers between devices: 16.6 us -> 18.6 us  [shifted(): lax.ppermute(array, MEMBER, [(i, (i + 2 * k) % groups) for i in range(gro...]
    unnamed x16 -> x18, local copies, waits for them, and re-layouts: 4.39 us -> 4.38 us
  transfers between devices with their start and end apart: 11 -> 12, of which waited for: 4 -> 7; matrix products, arithmetic and copies ran while one was open for 0% -> 0% of each run, Pallas kernels for 6% -> 6%
where the time goes in v8:
time: 188 us; the launch traced here: 187 us
  starting transfers between devices  65.3 us (35%)
  blocking collectives  55 us (29%)
  waiting for transfers between devices  36.6 us (19%)
  Pallas kernels  21.8 us (12%)
  local copies, waits for them, and re-layouts  7.43 us (4%)
    all_to_all x1, blocking collectives, body(): back = lax.all_to_all(updated, MEMBER, 0, 0, tiled=True)  55 us
    ppermute x7, starting transfers between devices, shifted(): lax.ppermute(array, MEMBER, [(i, (i + 2 * k) % groups) for i in range(gro...  29.6 us
    all_to_all x2, starting transfers between devices, sent_to_all(): return lax.all_to_all(copies, axis, 0, 0, tiled=True)  20.1 us
    ppermute x7, waiting for transfers between devices, shifted(): lax.ppermute(array, MEMBER, [(i, (i + 2 * k) % groups) for i in range(gro...  18.6 us
    pallas_call x1, Pallas kernels, transform_of(): pl.pallas_call(transform_kernel, out_shape=jax.ShapeDtypeStruct(gram.shap...  10.9 us
    ppermute x1, starting transfers between devices, swapped(): return lax.ppermute(array, MEMBER, [(i, i ^ 1) for i in range(groups)])  8.79 us
    pallas_call x1, Pallas kernels, pick(): pl.pallas_call(pick_kernel, out_shape=jax.ShapeDtypeStruct((places.shape[...  7.31 us
    all_to_all x2, waiting for transfers between devices, sent_to_all(): return lax.all_to_all(copies, axis, 0, 0, tiled=True)  7.14 us
  transfers between devices with their start and end apart: 12, of which 7 were waited for; matrix products, arithmetic and copies ran while one was open for 0% of the time, Pallas kernels for 6%

profile of v8, /device:TPU:1, one launch (start us, length us, event | category | flops | bytes accessed | tf_op | source)
XLA Modules:
  0.0 187.1 jit_solution(3267860776249761267)
XLA Ops:
  0.0 0.0 copy-start
  0.0 1.6 copy-done
  1.6 0.0 copy-start.2
  1.6 0.7 copy-done.2
  2.3 0.0 copy-start.1
  2.3 7.3 %shard_map.55 = f32[16,16,128]{2,1,0:T(8,128)} custom-call(s32[16,128]{1,0:T(8,128)S(1)} %copy-done.2, f32[16,32768]{1,0:T(8,128)S(1)} %copy-done), custom_call_target="tpu_custom_call" | custom-call | flops 1024 | bytes 1024 | tf_op jit(solution)/shard_map/pallas_call | solution.py:53
  9.6 0.0 copy-done.1
  9.6 0.0 copy-start.3
  9.6 0.1 shard_map.56
  9.8 8.8 %collective-permute-start = (f32[8,16,2048]{2,1,0:T(8,128)S(1)}, f32[8,16,2048]{2,1,0:T(8,128)S(1)}, u32[]{:S(2)}, u32[]{:S(2)}) collective-permute-start(f32[8,16,2048]{2,1,0:T(8,128)S(1)} %get-tuple-element.47), channel_id=1, source_target_pairs={{0,32},{32,0},{64,96},{96,64},{128,160},{160,128},{192,224},{224,1... | collective-permute-start | bytes 3145736 | tf_op jit(solution)/shard_map/ppermute | solution.py:208
  18.5 3.4 %all-to-all-start = ((f32[16,16,128]{2,1,0:T(8,128)}), f32[16,16,128]{2,1,0:T(8,128)S(1)}, u32[]{:S(2)}, u32[]{:S(2)}) async-start(f32[16,16,128]{2,1,0:T(8,128)} %shard_map.55), calls=%async_computation | async-start | bytes 262144 | tf_op jit(solution)/shard_map/all_to_all | solution.py:282
  22.6 0.0 collective-permute-done.other_ref
  22.7 0.1 shard_map.57
  22.8 0.0 copy-start.5
  22.8 0.7 copy-done.5
  23.5 0.7 copy-done.7
  24.2 0.7 copy-done.8
  24.9 6.2 %all-to-all-done = f32[16,16,128]{2,1,0:T(8,128)S(1)} async-done(((f32[16,16,128]{2,1,0:T(8,128)}), f32[16,16,128]{2,1,0:T(8,128)S(1)}, u32[]{:S(2)}, u32[]{:S(2)}) %all-to-all-start) | async-done | bytes 131104 | tf_op jit(solution)/shard_map/all_to_all | solution.py:282
  31.1 0.0 copy-done.3
  31.1 0.0 copy-done.4
  31.1 1.2 shard_map.58
  32.3 3.4 %all-to-all-start.1 = ((f32[16,16,256]{2,1,0:T(8,128)}), f32[16,16,256]{2,1,0:T(8,128)S(1)}, u32[]{:S(2)}, u32[]{:S(2)}) async-start(f32[16,16,256]{2,1,0:T(8,128)} %bitcast.4), calls=%async_computation.1 | async-start | bytes 524288 | tf_op jit(solution)/shard_map/all_to_all | solution.py:293
  35.7 2.9 %collective-permute-start.1 = (f32[32,2048]{1,0:T(8,128)}, f32[32,2048]{1,0:T(8,128)S(1)}, u32[]{:S(2)}, u32[]{:S(2)}) collective-permute-start(f32[32,2048]{1,0:T(8,128)} %copy-done.8), channel_id=1, source_target_pairs={{0,64},{32,96},{64,128},{96,160},{128,192},{160,224},{192,256},{22... | collective-permute-start | bytes 786440 | tf_op jit(solution)/shard_map/ppermute | solution.py:215
  38.6 3.6 %collective-permute-start.2 = (f32[32,2048]{1,0:T(8,128)}, f32[32,2048]{1,0:T(8,128)S(1)}, u32[]{:S(2)}, u32[]{:S(2)}) collective-permute-start(f32[32,2048]{1,0:T(8,128)} %copy-done.7), channel_id=1, source_target_pairs={{0,448},{32,480},{64,0},{96,32},{128,64},{160,96},{192,128},{224,1... | collective-permute-start | bytes 786440 | tf_op jit(solution)/shard_map/ppermute | solution.py:215
  42.3 4.8 %all-to-all-done.1 = f32[16,16,256]{2,1,0:T(8,128)S(1)} async-done(((f32[16,16,256]{2,1,0:T(8,128)}), f32[16,16,256]{2,1,0:T(8,128)S(1)}, u32[]{:S(2)}, u32[]{:S(2)}) %all-to-all-start.1) | async-done | bytes 262176 | tf_op jit(solution)/shard_map/all_to_all | solution.py:293
  47.0 3.2 %collective-permute-done.1.refs_0_ = f32[32,2048]{1,0:T(8,128)S(1)} collective-permute-done((f32[32,2048]{1,0:T(8,128)}, f32[32,2048]{1,0:T(8,128)S(1)}, u32[]{:S(2)}, u32[]{:S(2)}) %collective-permute-start.1) | collective-permute-done | bytes 262176 | tf_op jit(solution)/shard_map/ppermute | solution.py:215
  50.2 0.0 collective-permute-done.2.refs_1_
  50.2 0.9 broadcast_in_dim.4
  51.1 11.4 %all-to-all-start.2 = ((f32[32,16,256]{2,1,0:T(8,128)}), f32[32,16,256]{2,1,0:T(8,128)S(1)}, u32[]{:S(2)}, u32[]{:S(2)}) async-start(f32[32,16,256]{2,1,0:T(8,128)} %broadcast_in_dim.4), calls=%async_computation.2 | async-start | bytes 1048576 | tf_op jit(solution)/shard_map/all_to_all | solution.py:203
  62.5 0.0 copy-done.6
  62.5 5.1 %collective-permute-start.3 = (f32[32,2048]{1,0:T(8,128)S(1)}, f32[32,2048]{1,0:T(8,128)S(1)}, u32[]{:S(2)}, u32[]{:S(2)}) collective-permute-start(f32[32,2048]{1,0:T(8,128)S(1)} %copy-done.6), channel_id=1, source_target_pairs={{0,192},{32,224},{64,256},{96,288},{128,320},{160,352},{192,384},{... | collective-permute-start | bytes 786440 | tf_op jit(solution)/shard_map/ppermute | solution.py:215
  67.5 3.2 %collective-permute-start.4 = (f32[32,2048]{1,0:T(8,128)S(1)}, f32[32,2048]{1,0:T(8,128)S(1)}, u32[]{:S(2)}, u32[]{:S(2)}) collective-permute-start(f32[32,2048]{1,0:T(8,128)S(1)} %get-tuple-element.69), channel_id=1, source_target_pairs={{0,320},{32,352},{64,384},{96,416},{128,448},{160,480},{192,0},{22... | collective-permute-start | bytes 786440 | tf_op jit(solution)/shard_map/ppermute | solution.py:215
  70.8 7.1 %all-to-all-done.2 = f32[32,16,256]{2,1,0:T(8,128)S(1)} async-done(((f32[32,16,256]{2,1,0:T(8,128)}), f32[32,16,256]{2,1,0:T(8,128)S(1)}, u32[]{:S(2)}, u32[]{:S(2)}) %all-to-all-start.2) | async-done | bytes 524320 | tf_op jit(solution)/shard_map/all_to_all | solution.py:203
  77.9 8.2 %collective-permute-done.3.refs_2_ = f32[32,2048]{1,0:T(8,128)S(1)} collective-permute-done((f32[32,2048]{1,0:T(8,128)S(1)}, f32[32,2048]{1,0:T(8,128)S(1)}, u32[]{:S(2)}, u32[]{:S(2)}) %collective-permute-start.3) | collective-permute-done | bytes 262176 | tf_op jit(solution)/shard_map/ppermute | solution.py:215
  86.1 0.0 collective-permute-done.4.refs_3_
  86.1 0.7 broadcast_in_dim.5
  86.8 8.7 %all-to-all-start.3 = ((f32[16,16,256]{2,1,0:T(8,128)}), f32[16,16,256]{2,1,0:T(8,128)S(1)}, u32[]{:S(2)}, u32[]{:S(2)}) async-start(f32[16,16,256]{2,1,0:T(8,128)} %broadcast_in_dim.5), calls=%async_computation.3 | async-start | bytes 524288 | tf_op jit(solution)/shard_map/all_to_all | solution.py:203
  95.6 7.2 %collective-permute-start.5 = (f32[32,2048]{1,0:T(8,128)S(1)}, f32[32,2048]{1,0:T(8,128)S(1)}, u32[]{:S(2)}, u32[]{:S(2)}) collective-permute-start(f32[32,2048]{1,0:T(8,128)S(1)} %get-tuple-element.79), channel_id=1, source_target_pairs={{0,256},{32,288},{64,320},{96,352},{128,384},{160,416},{192,448},{... | collective-permute-start | bytes 786440 | tf_op jit(solution)/shard_map/ppermute | solution.py:215
  102.8 2.2 %collective-permute-start.6 = (f32[32,2048]{1,0:T(8,128)S(1)}, f32[32,2048]{1,0:T(8,128)S(1)}, u32[]{:S(2)}, u32[]{:S(2)}) collective-permute-start(f32[32,2048]{1,0:T(8,128)S(1)} %get-tuple-element.80), channel_id=1, source_target_pairs={{0,128},{32,160},{64,192},{96,224},{128,256},{160,288},{192,320},{... | collective-permute-start | bytes 786440 | tf_op jit(solution)/shard_map/ppermute | solution.py:215
  105.0 5.4 %collective-permute-start.7 = (f32[32,2048]{1,0:T(8,128)S(1)}, f32[32,2048]{1,0:T(8,128)S(1)}, u32[]{:S(2)}, u32[]{:S(2)}) collective-permute-start(f32[32,2048]{1,0:T(8,128)S(1)} %get-tuple-element.81), channel_id=1, source_target_pairs={{0,384},{32,416},{64,448},{96,480},{128,0},{160,32},{192,64},{224,... | collective-permute-start | bytes 786440 | tf_op jit(solution)/shard_map/ppermute | solution.py:215
  110.4 0.0 all-to-all-done.3
  110.4 10.9 %shard_map.59.transform_ref = f32[256,256]{1,0:T(8,128)S(1)} custom-call(f32[256,256]{1,0:T(8,128)S(1)} %bitcast.11), custom_call_target="tpu_custom_call" | custom-call | flops 1024 | bytes 1024 | tf_op jit(solution)/shard_map/pallas_call | solution.py:164
  121.2 0.0 collective-permute-done.5.refs_4_
  121.2 1.8 collective-permute-done.6.refs_5_
  123.0 5.4 %collective-permute-done.7.refs_6_ = f32[32,2048]{1,0:T(8,128)S(1)} collective-permute-done((f32[32,2048]{1,0:T(8,128)S(1)}, f32[32,2048]{1,0:T(8,128)S(1)}, u32[]{:S(2)}, u32[]{:S(2)}) %collective-permute-start.7) | collective-permute-done | bytes 262176 | tf_op jit(solution)/shard_map/ppermute | solution.py:215
  128.4 2.2 %shard_map.60 = f32[256,2048]{1,0:T(8,128)S(1)} custom-call(s32[1]{0:T(128)} %bitcast.chip_ref, f32[256,256]{1,0:T(8,128)S(1)} %shard_map.59.transform_ref, f32[32,2048]{1,0:T(8,128)S(1)} %collective-permute-done.1.refs_0_, f32[32,2048]{1,0:T(8,128)S(1)} %collective-permute-done.2.refs_1_, f32[32,2048]{1,0:T(8,128)S(1)} %collective-permute-done.3.refs_2_, ...), custom_call_target="tpu_custom_call" | custom-call | flops 1024 | bytes 1024 | tf_op jit(solution)/shard_map/pallas_call | solution.py:189
  130.6 55.0 %all_to_all.25 = f32[16,16,2048]{2,1,0:T(8,128)S(1)} all-to-all(f32[16,16,2048]{2,1,0:T(8,128)S(1)} %bitcast.10), channel_id=1, replica_groups=mesh['member'=16,'space'=32] {'member'}, dimensions={0} | all-to-all | bytes 4194304 | tf_op jit(solution)/shard_map/all_to_all | solution.py:304
  185.6 1.5 copy.8
  (6 shorter events, 0.1 us)
Async XLA Ops:
  0.0 1.6 copy-start
  1.6 0.7 copy-start.2
  2.3 7.3 %copy-start.1 = (f32[16,32768]{1,0:T(8,128)S(1)}, f32[16,32768]{1,0:T(8,128)}, u32[]{:S(2)}) copy-start(f32[16,32768]{1,0:T(8,128)} %state_ref.2) | copy-start | bytes 6291460
  9.6 21.5 %copy-start.3 = (f32[16,128]{1,0:T(8,128)S(1)}, f32[16,128]{1,0:T(8,128)}, u32[]{:S(2)}) copy-start(f32[16,128]{1,0:T(8,128)} %data_ref.1) | copy-start | bytes 24580
  9.6 21.5 %copy-start.4 = (f32[16,128]{1,0:T(8,128)S(1)}, f32[16,128]{1,0:T(8,128)}, u32[]{:S(2)}) copy-start(f32[16,128]{1,0:T(8,128)} %sigma_ref.1) | copy-start | bytes 24580
  9.8 12.9 %collective-permute-start = (f32[8,16,2048]{2,1,0:T(8,128)S(1)}, f32[8,16,2048]{2,1,0:T(8,128)S(1)}, u32[]{:S(2)}, u32[]{:S(2)}) collective-permute-start(f32[8,16,2048]{2,1,0:T(8,128)S(1)} %get-tuple-element.47), channel_id=1, source_target_pairs={{0,32},{32,0},{64,96},{96,64},{128,160},{160,128},{192,224},{224,1... | collective-permute-start | bytes 3145736 | tf_op jit(solution)/shard_map/ppermute | solution.py:208
  18.5 12.5 %all-to-all-start = ((f32[16,16,128]{2,1,0:T(8,128)}), f32[16,16,128]{2,1,0:T(8,128)S(1)}, u32[]{:S(2)}, u32[]{:S(2)}) async-start(f32[16,16,128]{2,1,0:T(8,128)} %shard_map.55), calls=%async_computation | async-start | bytes 262144 | tf_op jit(solution)/shard_map/all_to_all | solution.py:282
  22.8 0.7 copy-start.5
  23.5 0.7 copy-start.7
  24.2 0.7 copy-start.8
  31.1 31.4 %copy-start.6 = (f32[32,2048]{1,0:T(8,128)S(1)}, f32[32,2048]{1,0:T(8,128)}, u32[]{:S(2)}) copy-start(f32[32,2048]{1,0:T(8,128)} %copy-done.5) | copy-start | bytes 786436
  32.3 14.7 %all-to-all-start.1 = ((f32[16,16,256]{2,1,0:T(8,128)}), f32[16,16,256]{2,1,0:T(8,128)S(1)}, u32[]{:S(2)}, u32[]{:S(2)}) async-start(f32[16,16,256]{2,1,0:T(8,128)} %bitcast.4), calls=%async_computation.1 | async-start | bytes 524288 | tf_op jit(solution)/shard_map/all_to_all | solution.py:293
  35.7 14.5 %collective-permute-start.1 = (f32[32,2048]{1,0:T(8,128)}, f32[32,2048]{1,0:T(8,128)S(1)}, u32[]{:S(2)}, u32[]{:S(2)}) collective-permute-start(f32[32,2048]{1,0:T(8,128)} %copy-done.8), channel_id=1, source_target_pairs={{0,64},{32,96},{64,128},{96,160},{128,192},{160,224},{192,256},{22... | collective-permute-start | bytes 786440 | tf_op jit(solution)/shard_map/ppermute | solution.py:215
  38.6 11.6 %collective-permute-start.2 = (f32[32,2048]{1,0:T(8,128)}, f32[32,2048]{1,0:T(8,128)S(1)}, u32[]{:S(2)}, u32[]{:S(2)}) collective-permute-start(f32[32,2048]{1,0:T(8,128)} %copy-done.7), channel_id=1, source_target_pairs={{0,448},{32,480},{64,0},{96,32},{128,64},{160,96},{192,128},{224,1... | collective-permute-start | bytes 786440 | tf_op jit(solution)/shard_map/ppermute | solution.py:215
  51.1 26.8 %all-to-all-start.2 = ((f32[32,16,256]{2,1,0:T(8,128)}), f32[32,16,256]{2,1,0:T(8,128)S(1)}, u32[]{:S(2)}, u32[]{:S(2)}) async-start(f32[32,16,256]{2,1,0:T(8,128)} %broadcast_in_dim.4), calls=%async_computation.2 | async-start | bytes 1048576 | tf_op jit(solution)/shard_map/all_to_all | solution.py:203
  62.5 23.6 %collective-permute-start.3 = (f32[32,2048]{1,0:T(8,128)S(1)}, f32[32,2048]{1,0:T(8,128)S(1)}, u32[]{:S(2)}, u32[]{:S(2)}) collective-permute-start(f32[32,2048]{1,0:T(8,128)S(1)} %copy-done.6), channel_id=1, source_target_pairs={{0,192},{32,224},{64,256},{96,288},{128,320},{160,352},{192,384},{... | collective-permute-start | bytes 786440 | tf_op jit(solution)/shard_map/ppermute | solution.py:215
  67.5 18.6 %collective-permute-start.4 = (f32[32,2048]{1,0:T(8,128)S(1)}, f32[32,2048]{1,0:T(8,128)S(1)}, u32[]{:S(2)}, u32[]{:S(2)}) collective-permute-start(f32[32,2048]{1,0:T(8,128)S(1)} %get-tuple-element.69), channel_id=1, source_target_pairs={{0,320},{32,352},{64,384},{96,416},{128,448},{160,480},{192,0},{22... | collective-permute-start | bytes 786440 | tf_op jit(solution)/shard_map/ppermute | solution.py:215
  86.8 23.5 %all-to-all-start.3 = ((f32[16,16,256]{2,1,0:T(8,128)}), f32[16,16,256]{2,1,0:T(8,128)S(1)}, u32[]{:S(2)}, u32[]{:S(2)}) async-start(f32[16,16,256]{2,1,0:T(8,128)} %broadcast_in_dim.5), calls=%async_computation.3 | async-start | bytes 524288 | tf_op jit(solution)/shard_map/all_to_all | solution.py:203
  95.6 25.7 %collective-permute-start.5 = (f32[32,2048]{1,0:T(8,128)S(1)}, f32[32,2048]{1,0:T(8,128)S(1)}, u32[]{:S(2)}, u32[]{:S(2)}) collective-permute-start(f32[32,2048]{1,0:T(8,128)S(1)} %get-tuple-element.79), channel_id=1, source_target_pairs={{0,256},{32,288},{64,320},{96,352},{128,384},{160,416},{192,448},{... | collective-permute-start | bytes 786440 | tf_op jit(solution)/shard_map/ppermute | solution.py:215
  102.8 20.3 %collective-permute-start.6 = (f32[32,2048]{1,0:T(8,128)S(1)}, f32[32,2048]{1,0:T(8,128)S(1)}, u32[]{:S(2)}, u32[]{:S(2)}) collective-permute-start(f32[32,2048]{1,0:T(8,128)S(1)} %get-tuple-element.80), channel_id=1, source_target_pairs={{0,128},{32,160},{64,192},{96,224},{128,256},{160,288},{192,320},{... | collective-permute-start | bytes 786440 | tf_op jit(solution)/shard_map/ppermute | solution.py:215
  105.0 23.5 %collective-permute-start.7 = (f32[32,2048]{1,0:T(8,128)S(1)}, f32[32,2048]{1,0:T(8,128)S(1)}, u32[]{:S(2)}, u32[]{:S(2)}) collective-permute-start(f32[32,2048]{1,0:T(8,128)S(1)} %get-tuple-element.81), channel_id=1, source_target_pairs={{0,384},{32,416},{64,448},{96,480},{128,0},{160,32},{192,64},{224,... | collective-permute-start | bytes 786440 | tf_op jit(solution)/shard_map/ppermute | solution.py:215

commit v9 on v4

--- a/solution.py
+++ b/solution.py
@@ -12,11 +12,13 @@
 SPACE = "space"
 LANES = 128
 SUBLANES = 8
+SOON = (1,7)
 FIRST = (3, 5, 2, 6)
-THEN = (4, 1, 7, 0)
+THEN = (4, 0)
 IN_VMEM = pl.BlockSpec(memory_space=pltpu.VMEM)
 IN_SMEM = pl.BlockSpec(memory_space=pltpu.SMEM)
 KERNEL = pltpu.CompilerParams(vmem_limit_bytes=16 * 2**20)
+LARGE = pl.CostEstimate(flops=2**34, bytes_accessed=2**26, transcendentals=0)
 SMALL = pl.CostEstimate(flops=1024, bytes_accessed=1024, transcendentals=0)
 
 
@@ -85,7 +87,7 @@
         in_specs=[IN_SMEM, IN_SMEM, IN_VMEM, IN_VMEM, IN_VMEM],
         out_specs=IN_VMEM,
         compiler_params=KERNEL,
-        cost_estimate=SMALL,
+        cost_estimate=LARGE,
     )(rank.reshape(1), used, evolved, data, sigma)
 
 
@@ -174,7 +176,7 @@
     *parts, out_ref, state_ref = refs
     chips = len(parts)
     height = parts[0].shape[0]
-    for k, part in zip(FIRST + THEN, parts):
+    for k, part in zip(SOON + FIRST + THEN, parts):
         chip = lax.rem(chip_ref[0] - k + chips, chips)
         state_ref[pl.ds(pl.multiple_of(chip * height, height), height), :] = part[...]
     state = state_ref[...]
@@ -282,12 +284,14 @@
 
     kept, sent = split(core, state, chips)
     pairs = join(chip, core, kept, swapped(sent))
+    soon = [shifted(pairs[k], k) for k in SOON]
     evolved, pairs = lax.optimization_barrier((evolved, pairs))
 
     gram = gram_of(
         rank, measured_slots_used, evolved, measured_data, measurement_noise_sigma
     )
     spaces = lax.axis_size(SPACE)
+    gram, soon = lax.optimization_barrier((gram, soon))
     first = [shifted(pairs[k], k) for k in FIRST]
     pieces = gram.reshape(spaces, total // spaces, total)
     pieces = jnp.sum(lax.all_to_all(pieces, SPACE, 0, 0, tiled=True), axis=0)
@@ -297,7 +301,7 @@
     gram = sent_to_all(pieces, SPACE).reshape(total, total)
     transform = transform_of(gram)
 
-    updated = applied(chip, transform, first + then)
+    updated = applied(chip, transform, soon + first + then)
     updated = updated.reshape(groups, own_members, own_cells)
     back = lax.all_to_all(updated, MEMBER, 0, 0, tiled=True)
     return back.swapaxes(0, 1).reshape(own_members, cells)

time: 180 us -> 186 us (1.033)
  waiting for transfers between devices: 8.86 us -> 14.9 us
  blocking collectives: 80.4 us -> 82.4 us
    all_to_all x1, waiting for transfers between devices: 0.01 us -> 10.1 us  [sent_to_all(): return lax.all_to_all(copies, axis, 0, 0, tiled=True)]
    all_to_all x1, waiting for transfers between devices: 6.18 us -> 0.27 us  [body(): lax.all_to_all(picked, MEMBER, 0, 0, tiled=True).reshape(total, LANES)]
    all_to_all x1, blocking collectives: 23.9 us -> 27.2 us  [sent_to_all(): return lax.all_to_all(copies, axis, 0, 0, tiled=True)]
    ppermute x7, starting transfers between devices: 27.9 us -> 26 us  [shifted(): lax.ppermute(array, MEMBER, [(i, (i + 2 * k) % groups) for i in range(gro...]
    unnamed x16 -> x14, local copies, waits for them, and re-layouts: 4.39 us -> 3 us
  transfers between devices with their start and end apart: 11 -> 11, of which waited for: 3 -> 4; matrix products, arithmetic and copies ran while one was open for 0% -> 0% of each run, Pallas kernels for 6% -> 7%
where the time goes in v9:
time: 186 us; the launch traced here: 185 us
  blocking collectives  82.4 us (44%)
  starting transfers between devices  58.8 us (32%)
  Pallas kernels  22.6 us (12%)
  waiting for transfers between devices  14.9 us (8%)
  local copies, waits for them, and re-layouts  5.2 us (3%)
    all_to_all x1, blocking collectives, body(): back = lax.all_to_all(updated, MEMBER, 0, 0, tiled=True)  55.2 us
    all_to_all x1, blocking collectives, sent_to_all(): return lax.all_to_all(copies, axis, 0, 0, tiled=True)  27.2 us
    ppermute x7, starting transfers between devices, shifted(): lax.ppermute(array, MEMBER, [(i, (i + 2 * k) % groups) for i in range(gro...  26 us
    all_to_all x1, starting transfers between devices, body(): pieces = jnp.sum(lax.all_to_all(pieces, SPACE, 0, 0, tiled=True), axis=0)  11.4 us
    pallas_call x1, Pallas kernels, transform_of(): pl.pallas_call(transform_kernel, out_shape=jax.ShapeDtypeStruct(gram.shap...  10.9 us
    all_to_all x1, waiting for transfers between devices, sent_to_all(): return lax.all_to_all(copies, axis, 0, 0, tiled=True)  10.1 us
    all_to_all x1, starting transfers between devices, sent_to_all(): return lax.all_to_all(copies, axis, 0, 0, tiled=True)  9.21 us
    ppermute x1, starting transfers between devices, swapped(): return lax.ppermute(array, MEMBER, [(i, i ^ 1) for i in range(groups)])  8.79 us
  transfers between devices with their start and end apart: 11, of which 4 were waited for; matrix products, arithmetic and copies ran while one was open for 0% of the time, Pallas kernels for 7%

profile of v9, /device:TPU:1, one launch (start us, length us, event | category | flops | bytes accessed | tf_op | source)
XLA Modules:
  0.0 184.8 jit_solution(877764118975441340)
XLA Ops:
  0.0 0.0 copy-start
  0.0 1.6 copy-done
  1.6 0.0 copy-start.2
  1.6 0.7 copy-done.2
  2.3 0.0 copy-start.1
  2.3 7.3 %shard_map.55 = f32[16,16,128]{2,1,0:T(8,128)} custom-call(s32[16,128]{1,0:T(8,128)S(1)} %copy-done.2, f32[16,32768]{1,0:T(8,128)S(1)} %copy-done), custom_call_target="tpu_custom_call" | custom-call | flops 1024 | bytes 1024 | tf_op jit(solution)/shard_map/pallas_call | solution.py:54
  9.6 0.0 copy-done.1
  9.6 0.0 copy-start.5
  9.6 0.0 copy-start.6
  9.6 0.1 shard_map.56
  9.8 8.8 %collective-permute-start = (f32[8,16,2048]{2,1,0:T(8,128)S(1)}, f32[8,16,2048]{2,1,0:T(8,128)S(1)}, u32[]{:S(2)}, u32[]{:S(2)}) collective-permute-start(f32[8,16,2048]{2,1,0:T(8,128)S(1)} %get-tuple-element.37), channel_id=1, source_target_pairs={{0,32},{32,0},{64,96},{96,64},{128,160},{160,128},{192,224},{224,1... | collective-permute-start | bytes 3145736 | tf_op jit(solution)/shard_map/ppermute | solution.py:209
  18.6 3.4 %all-to-all-start = ((f32[16,16,128]{2,1,0:T(8,128)}), f32[16,16,128]{2,1,0:T(8,128)S(1)}, u32[]{:S(2)}, u32[]{:S(2)}) async-start(f32[16,16,128]{2,1,0:T(8,128)} %shard_map.55), calls=%async_computation | async-start | bytes 262144 | tf_op jit(solution)/shard_map/all_to_all | solution.py:283
  22.7 0.0 collective-permute-done.other_ref
  22.7 0.9 shard_map.57
  23.6 0.0 copy-start.3
  23.6 0.7 copy-done.3
  24.3 3.2 %collective-permute-start.1 = (f32[32,2048]{1,0:T(8,128)}, f32[32,2048]{1,0:T(8,128)S(1)}, u32[]{:S(2)}, u32[]{:S(2)}) collective-permute-start(f32[32,2048]{1,0:T(8,128)} %get-tuple-element.39), channel_id=1, source_target_pairs={{0,64},{32,96},{64,128},{96,160},{128,192},{160,224},{192,256},{22... | collective-permute-start | bytes 786440 | tf_op jit(solution)/shard_map/ppermute | solution.py:216
  27.5 3.3 %collective-permute-start.2 = (f32[32,2048]{1,0:T(8,128)}, f32[32,2048]{1,0:T(8,128)S(1)}, u32[]{:S(2)}, u32[]{:S(2)}) collective-permute-start(f32[32,2048]{1,0:T(8,128)} %get-tuple-element.45), channel_id=1, source_target_pairs={{0,448},{32,480},{64,0},{96,32},{128,64},{160,96},{192,128},{224,1... | collective-permute-start | bytes 786440 | tf_op jit(solution)/shard_map/ppermute | solution.py:216
  30.8 0.3 all-to-all-done
  31.1 0.0 copy-done.5
  31.1 0.0 copy-done.6
  31.1 0.0 copy-start.4
  31.1 1.2 shard_map.58
  32.3 3.3 %collective-permute-done.1.refs_0_ = f32[32,2048]{1,0:T(8,128)S(1)} collective-permute-done((f32[32,2048]{1,0:T(8,128)}, f32[32,2048]{1,0:T(8,128)S(1)}, u32[]{:S(2)}, u32[]{:S(2)}) %collective-permute-start.1) | collective-permute-done | bytes 262176 | tf_op jit(solution)/shard_map/ppermute | solution.py:216
  35.6 1.2 collective-permute-done.2.refs_1_
  36.8 11.4 %all-to-all-start.1 = ((f32[32,8,256]{2,1,0:T(8,128)}), f32[32,8,256]{2,1,0:T(8,128)S(1)}, u32[]{:S(2)}, u32[]{:S(2)}) async-start(f32[32,8,256]{2,1,0:T(8,128)} %bitcast.4), calls=%async_computation.1 | async-start | bytes 524288 | tf_op jit(solution)/shard_map/all_to_all | solution.py:297
  48.2 0.0 copy-done.4
  48.2 7.3 %collective-permute-start.3 = (f32[32,2048]{1,0:T(8,128)S(1)}, f32[32,2048]{1,0:T(8,128)S(1)}, u32[]{:S(2)}, u32[]{:S(2)}) collective-permute-start(f32[32,2048]{1,0:T(8,128)S(1)} %copy-done.4), channel_id=1, source_target_pairs={{0,192},{32,224},{64,256},{96,288},{128,320},{160,352},{192,384},{... | collective-permute-start | bytes 786440 | tf_op jit(solution)/shard_map/ppermute | solution.py:216
  55.6 1.9 %collective-permute-start.4 = (f32[32,2048]{1,0:T(8,128)S(1)}, f32[32,2048]{1,0:T(8,128)S(1)}, u32[]{:S(2)}, u32[]{:S(2)}) collective-permute-start(f32[32,2048]{1,0:T(8,128)S(1)} %get-tuple-element.49), channel_id=1, source_target_pairs={{0,320},{32,352},{64,384},{96,416},{128,448},{160,480},{192,0},{22... | collective-permute-start | bytes 786440 | tf_op jit(solution)/shard_map/ppermute | solution.py:216
  57.5 4.3 %collective-permute-start.5 = (f32[32,2048]{1,0:T(8,128)S(1)}, f32[32,2048]{1,0:T(8,128)S(1)}, u32[]{:S(2)}, u32[]{:S(2)}) collective-permute-start(f32[32,2048]{1,0:T(8,128)S(1)} %get-tuple-element.50), channel_id=1, source_target_pairs={{0,128},{32,160},{64,192},{96,224},{128,256},{160,288},{192,320},{... | collective-permute-start | bytes 786440 | tf_op jit(solution)/shard_map/ppermute | solution.py:216
  61.8 3.1 %collective-permute-start.6 = (f32[32,2048]{1,0:T(8,128)S(1)}, f32[32,2048]{1,0:T(8,128)S(1)}, u32[]{:S(2)}, u32[]{:S(2)}) collective-permute-start(f32[32,2048]{1,0:T(8,128)S(1)} %get-tuple-element.51), channel_id=1, source_target_pairs={{0,384},{32,416},{64,448},{96,480},{128,0},{160,32},{192,64},{224,... | collective-permute-start | bytes 786440 | tf_op jit(solution)/shard_map/ppermute | solution.py:216
  64.9 0.0 all-to-all-done.1
  65.0 27.2 %all_to_all.25 = f32[16,8,256]{2,1,0:T(8,128)S(1)} all-to-all(f32[16,8,256]{2,1,0:T(8,128)S(1)} %broadcast_in_dim.4), channel_id=1, replica_groups=mesh['member'=16,'space'=32] {'member'}, dimensions={0} | all-to-all | bytes 262144 | tf_op jit(solution)/shard_map/all_to_all | solution.py:204
  92.2 0.0 collective-permute-done.3.refs_2_
  92.2 0.0 collective-permute-done.4.refs_3_
  92.2 0.0 collective-permute-done.5.refs_4_
  92.2 0.0 collective-permute-done.6.refs_5_
  92.2 0.7 broadcast_in_dim.5
  92.9 9.2 %all-to-all-start.3 = ((f32[32,8,256]{2,1,0:T(8,128)}), f32[32,8,256]{2,1,0:T(8,128)S(1)}, u32[]{:S(2)}, u32[]{:S(2)}) async-start(f32[32,8,256]{2,1,0:T(8,128)} %broadcast_in_dim.5), calls=%async_computation.3 | async-start | bytes 524288 | tf_op jit(solution)/shard_map/all_to_all | solution.py:204
  102.2 2.8 %collective-permute-start.7 = (f32[32,2048]{1,0:T(8,128)S(1)}, f32[32,2048]{1,0:T(8,128)S(1)}, u32[]{:S(2)}, u32[]{:S(2)}) collective-permute-start(f32[32,2048]{1,0:T(8,128)S(1)} %get-tuple-element.61), channel_id=1, source_target_pairs={{0,256},{32,288},{64,320},{96,352},{128,384},{160,416},{192,448},{... | collective-permute-start | bytes 786440 | tf_op jit(solution)/shard_map/ppermute | solution.py:216
  105.0 10.1 %all-to-all-done.3 = f32[32,8,256]{2,1,0:T(8,128)S(1)} async-done(((f32[32,8,256]{2,1,0:T(8,128)}), f32[32,8,256]{2,1,0:T(8,128)S(1)}, u32[]{:S(2)}, u32[]{:S(2)}) %all-to-all-start.3) | async-done | bytes 262176 | tf_op jit(solution)/shard_map/all_to_all | solution.py:204
  115.1 10.9 %shard_map.59.transform_ref = f32[256,256]{1,0:T(8,128)S(1)} custom-call(f32[256,256]{1,0:T(8,128)S(1)} %bitcast.11), custom_call_target="tpu_custom_call" | custom-call | flops 1024 | bytes 1024 | tf_op jit(solution)/shard_map/pallas_call | solution.py:165
  125.9 0.0 collective-permute-done.7.refs_6_
  125.9 2.2 %shard_map.60 = f32[256,2048]{1,0:T(8,128)S(1)} custom-call(s32[1]{0:T(128)} %bitcast.chip_ref, f32[256,256]{1,0:T(8,128)S(1)} %shard_map.59.transform_ref, f32[32,2048]{1,0:T(8,128)S(1)} %collective-permute-done.1.refs_0_, f32[32,2048]{1,0:T(8,128)S(1)} %collective-permute-done.2.refs_1_, f32[32,2048]{1,0:T(8,128)S(1)} %collective-permute-done.3.refs_2_, ...), custom_call_target="tpu_custom_call" | custom-call | flops 1024 | bytes 1024 | tf_op jit(solution)/shard_map/pallas_call | solution.py:190
  128.1 55.2 %all_to_all.26 = f32[16,16,2048]{2,1,0:T(8,128)S(1)} all-to-all(f32[16,16,2048]{2,1,0:T(8,128)S(1)} %bitcast.10), channel_id=1, replica_groups=mesh['member'=16,'space'=32] {'member'}, dimensions={0} | all-to-all | bytes 4194304 | tf_op jit(solution)/shard_map/all_to_all | solution.py:306
  183.3 1.5 copy.8
  (3 shorter events, 0.1 us)
Async XLA Ops:
  0.0 1.6 copy-start
  1.6 0.7 copy-start.2
  2.3 7.3 %copy-start.1 = (f32[16,32768]{1,0:T(8,128)S(1)}, f32[16,32768]{1,0:T(8,128)}, u32[]{:S(2)}) copy-start(f32[16,32768]{1,0:T(8,128)} %state_ref.2) | copy-start | bytes 6291460
  9.6 21.5 %copy-start.5 = (f32[16,128]{1,0:T(8,128)S(1)}, f32[16,128]{1,0:T(8,128)}, u32[]{:S(2)}) copy-start(f32[16,128]{1,0:T(8,128)} %data_ref.1) | copy-start | bytes 24580
  9.6 21.5 %copy-start.6 = (f32[16,128]{1,0:T(8,128)S(1)}, f32[16,128]{1,0:T(8,128)}, u32[]{:S(2)}) copy-start(f32[16,128]{1,0:T(8,128)} %sigma_ref.1) | copy-start | bytes 24580
  9.8 12.9 %collective-permute-start = (f32[8,16,2048]{2,1,0:T(8,128)S(1)}, f32[8,16,2048]{2,1,0:T(8,128)S(1)}, u32[]{:S(2)}, u32[]{:S(2)}) collective-permute-start(f32[8,16,2048]{2,1,0:T(8,128)S(1)} %get-tuple-element.37), channel_id=1, source_target_pairs={{0,32},{32,0},{64,96},{96,64},{128,160},{160,128},{192,224},{224,1... | collective-permute-start | bytes 3145736 | tf_op jit(solution)/shard_map/ppermute | solution.py:209
  18.6 12.5 %all-to-all-start = ((f32[16,16,128]{2,1,0:T(8,128)}), f32[16,16,128]{2,1,0:T(8,128)S(1)}, u32[]{:S(2)}, u32[]{:S(2)}) async-start(f32[16,16,128]{2,1,0:T(8,128)} %shard_map.55), calls=%async_computation | async-start | bytes 262144 | tf_op jit(solution)/shard_map/all_to_all | solution.py:283
  23.6 0.7 copy-start.3
  24.3 11.3 %collective-permute-start.1 = (f32[32,2048]{1,0:T(8,128)}, f32[32,2048]{1,0:T(8,128)S(1)}, u32[]{:S(2)}, u32[]{:S(2)}) collective-permute-start(f32[32,2048]{1,0:T(8,128)} %get-tuple-element.39), channel_id=1, source_target_pairs={{0,64},{32,96},{64,128},{96,160},{128,192},{160,224},{192,256},{22... | collective-permute-start | bytes 786440 | tf_op jit(solution)/shard_map/ppermute | solution.py:216
  27.5 9.3 %collective-permute-start.2 = (f32[32,2048]{1,0:T(8,128)}, f32[32,2048]{1,0:T(8,128)S(1)}, u32[]{:S(2)}, u32[]{:S(2)}) collective-permute-start(f32[32,2048]{1,0:T(8,128)} %get-tuple-element.45), channel_id=1, source_target_pairs={{0,448},{32,480},{64,0},{96,32},{128,64},{160,96},{192,128},{224,1... | collective-permute-start | bytes 786440 | tf_op jit(solution)/shard_map/ppermute | solution.py:216
  31.1 17.1 %copy-start.4 = (f32[32,2048]{1,0:T(8,128)S(1)}, f32[32,2048]{1,0:T(8,128)}, u32[]{:S(2)}) copy-start(f32[32,2048]{1,0:T(8,128)} %copy-done.3) | copy-start | bytes 786436
  36.8 28.1 %all-to-all-start.1 = ((f32[32,8,256]{2,1,0:T(8,128)}), f32[32,8,256]{2,1,0:T(8,128)S(1)}, u32[]{:S(2)}, u32[]{:S(2)}) async-start(f32[32,8,256]{2,1,0:T(8,128)} %bitcast.4), calls=%async_computation.1 | async-start | bytes 524288 | tf_op jit(solution)/shard_map/all_to_all | solution.py:297
  48.2 43.9 %collective-permute-start.3 = (f32[32,2048]{1,0:T(8,128)S(1)}, f32[32,2048]{1,0:T(8,128)S(1)}, u32[]{:S(2)}, u32[]{:S(2)}) collective-permute-start(f32[32,2048]{1,0:T(8,128)S(1)} %copy-done.4), channel_id=1, source_target_pairs={{0,192},{32,224},{64,256},{96,288},{128,320},{160,352},{192,384},{... | collective-permute-start | bytes 786440 | tf_op jit(solution)/shard_map/ppermute | solution.py:216
  55.6 36.6 %collective-permute-start.4 = (f32[32,2048]{1,0:T(8,128)S(1)}, f32[32,2048]{1,0:T(8,128)S(1)}, u32[]{:S(2)}, u32[]{:S(2)}) collective-permute-start(f32[32,2048]{1,0:T(8,128)S(1)} %get-tuple-element.49), channel_id=1, source_target_pairs={{0,320},{32,352},{64,384},{96,416},{128,448},{160,480},{192,0},{22... | collective-permute-start | bytes 786440 | tf_op jit(solution)/shard_map/ppermute | solution.py:216
  57.5 34.7 %collective-permute-start.5 = (f32[32,2048]{1,0:T(8,128)S(1)}, f32[32,2048]{1,0:T(8,128)S(1)}, u32[]{:S(2)}, u32[]{:S(2)}) collective-permute-start(f32[32,2048]{1,0:T(8,128)S(1)} %get-tuple-element.50), channel_id=1, source_target_pairs={{0,128},{32,160},{64,192},{96,224},{128,256},{160,288},{192,320},{... | collective-permute-start | bytes 786440 | tf_op jit(solution)/shard_map/ppermute | solution.py:216
  61.8 30.4 %collective-permute-start.6 = (f32[32,2048]{1,0:T(8,128)S(1)}, f32[32,2048]{1,0:T(8,128)S(1)}, u32[]{:S(2)}, u32[]{:S(2)}) collective-permute-start(f32[32,2048]{1,0:T(8,128)S(1)} %get-tuple-element.51), channel_id=1, source_target_pairs={{0,384},{32,416},{64,448},{96,480},{128,0},{160,32},{192,64},{224,... | collective-permute-start | bytes 786440 | tf_op jit(solution)/shard_map/ppermute | solution.py:216
  92.9 22.1 %all-to-all-start.3 = ((f32[32,8,256]{2,1,0:T(8,128)}), f32[32,8,256]{2,1,0:T(8,128)S(1)}, u32[]{:S(2)}, u32[]{:S(2)}) async-start(f32[32,8,256]{2,1,0:T(8,128)} %broadcast_in_dim.5), calls=%async_computation.3 | async-start | bytes 524288 | tf_op jit(solution)/shard_map/all_to_all | solution.py:204
  102.2 23.8 %collective-permute-start.7 = (f32[32,2048]{1,0:T(8,128)S(1)}, f32[32,2048]{1,0:T(8,128)S(1)}, u32[]{:S(2)}, u32[]{:S(2)}) collective-permute-start(f32[32,2048]{1,0:T(8,128)S(1)} %get-tuple-element.61), channel_id=1, source_target_pairs={{0,256},{32,288},{64,320},{96,352},{128,384},{160,416},{192,448},{... | collective-permute-start | bytes 786440 | tf_op jit(solution)/shard_map/ppermute | solution.py:216

commit v10 on v4

--- a/solution.py
+++ b/solution.py
@@ -17,6 +17,7 @@
 IN_VMEM = pl.BlockSpec(memory_space=pltpu.VMEM)
 IN_SMEM = pl.BlockSpec(memory_space=pltpu.SMEM)
 KERNEL = pltpu.CompilerParams(vmem_limit_bytes=16 * 2**20)
+LARGE = pl.CostEstimate(flops=2**34, bytes_accessed=2**26, transcendentals=0)
 SMALL = pl.CostEstimate(flops=1024, bytes_accessed=1024, transcendentals=0)
 
 
@@ -30,18 +31,19 @@
     )
 
 
-def pick_kernel(places_ref, state_ref, out_ref):
+def pick_kernel(places_ref, lanes_ref, state_ref, out_ref):
     rows, members = out_ref.shape[:2]
     lane = lax.broadcasted_iota(jnp.int32, (members, LANES), 1)
 
     def one_row(row, carry):
+        within = lanes_ref[pl.ds(row, 1), :] & (LANES - 1)
+        within = jnp.broadcast_to(within, (members, LANES))
         total = jnp.zeros((members, LANES), jnp.float32)
         for slot in range(LANES):
-            place = places_ref[row, slot]
-            tile = pl.multiple_of((place >> 7) << 7, LANES)
+            tile = pl.multiple_of((places_ref[row, slot] >> 7) << 7, LANES)
             cells = state_ref[:, pl.ds(tile, LANES)]
-            turned = pltpu.roll(cells, (slot - place) & (LANES - 1), 1)
-            total = jnp.where(lane == slot, turned, total)
+            found = jnp.take_along_axis(cells, within, axis=1)
+            total = jnp.where(lane == slot, found, total)
         out_ref[row] = total
         return carry
 
@@ -52,11 +54,11 @@
     return pl.pallas_call(
         pick_kernel,
         out_shape=jax.ShapeDtypeStruct((places.shape[0], state.shape[0], LANES), jnp.float32),
-        in_specs=[IN_SMEM, IN_VMEM],
-        out_specs=IN_VMEM,
-        compiler_params=KERNEL,
-        cost_estimate=SMALL,
-    )(places, state)
+        in_specs=[IN_SMEM, IN_VMEM, IN_VMEM],
+        out_specs=IN_VMEM,
+        compiler_params=KERNEL,
+        cost_estimate=SMALL,
+    )(places, places, state)
 
 
 def gram_kernel(rank_ref, used_ref, evolved_ref, data_ref, sigma_ref, out_ref):
@@ -85,7 +87,7 @@
         in_specs=[IN_SMEM, IN_SMEM, IN_VMEM, IN_VMEM, IN_VMEM],
         out_specs=IN_VMEM,
         compiler_params=KERNEL,
-        cost_estimate=SMALL,
+        cost_estimate=LARGE,
     )(rank.reshape(1), used, evolved, data, sigma)
 
 
@@ -196,9 +198,23 @@
     )(chip.reshape(1), transform, *parts)
 
 
-def sent_to_all(array, axis):
-    size = lax.axis_size(axis)
-    copies = jnp.broadcast_to(array[None], (size, *array.shape))
+def spread_kernel(parts_ref, out_ref):
+    total = parts_ref[0]
+    for part in range(1, parts_ref.shape[0]):
+        total = total + parts_ref[part]
+    for copy in range(out_ref.shape[0]):
+        out_ref[copy] = total
+
+
+def sum_sent_to_all(parts, axis):
+    copies = pl.pallas_call(
+        spread_kernel,
+        out_shape=jax.ShapeDtypeStruct((lax.axis_size(axis), *parts.shape[1:]), jnp.float32),
+        in_specs=[IN_VMEM],
+        out_specs=IN_VMEM,
+        compiler_params=KERNEL,
+        cost_estimate=SMALL,
+    )(parts)
     return lax.all_to_all(copies, axis, 0, 0, tiled=True)
 
 
@@ -282,7 +298,6 @@
 
     kept, sent = split(core, state, chips)
     pairs = join(chip, core, kept, swapped(sent))
-    evolved, pairs = lax.optimization_barrier((evolved, pairs))
 
     gram = gram_of(
         rank, measured_slots_used, evolved, measured_data, measurement_noise_sigma
@@ -290,11 +305,11 @@
     spaces = lax.axis_size(SPACE)
     first = [shifted(pairs[k], k) for k in FIRST]
     pieces = gram.reshape(spaces, total // spaces, total)
-    pieces = jnp.sum(lax.all_to_all(pieces, SPACE, 0, 0, tiled=True), axis=0)
-    pieces = jnp.sum(sent_to_all(pieces, MEMBER), axis=0)
+    pieces = lax.all_to_all(pieces, SPACE, 0, 0, tiled=True)
+    pieces = sum_sent_to_all(pieces, MEMBER)
     pieces, first, pairs = lax.optimization_barrier((pieces, first, pairs))
     then = [shifted(pairs[k], k) for k in THEN]
-    gram = sent_to_all(pieces, SPACE).reshape(total, total)
+    gram = sum_sent_to_all(pieces, SPACE).reshape(total, total)
     transform = transform_of(gram)
 
     updated = applied(chip, transform, first + then)

time: 180 us -> 178 us (0.989)
  local copies, waits for them, and re-layouts: 6.58 us -> 3.76 us
  Pallas kernels: 21.8 us -> 24 us
    all_to_all x1, starting transfers between devices: 3.42 us -> 10.2 us  [body(): lax.all_to_all(picked, MEMBER, 0, 0, tiled=True).reshape(total, LANES)]
    ppermute x1, starting transfers between devices: 8.79 us -> 2.13 us  [swapped(): return lax.ppermute(array, MEMBER, [(i, i ^ 1) for i in range(groups)])]
    unnamed x16 -> x12, local copies, waits for them, and re-layouts: 4.39 us -> 2.3 us
  transfers between devices with their start and end apart: 11 -> 11, of which waited for: 3 -> 3; matrix products, arithmetic and copies ran while one was open for 0% -> 0% of each run, Pallas kernels for 6% -> 8%
where the time goes in v10:
time: 178 us
  blocking collectives  80.2 us (45%)
  starting transfers between devices  60.6 us (34%)
  Pallas kernels  24 us (13%)
  waiting for transfers between devices  8.2 us (5%)
  local copies, waits for them, and re-layouts  3.76 us (2%)
    all_to_all x1, blocking collectives, body(): back = lax.all_to_all(updated, MEMBER, 0, 0, tiled=True)  56.3 us
    ppermute x7, starting transfers between devices, shifted(): lax.ppermute(array, MEMBER, [(i, (i + 2 * k) % groups) for i in range(gro...  27.9 us
    all_to_all x1, blocking collectives, sum_sent_to_all(): return lax.all_to_all(copies, axis, 0, 0, tiled=True)  23.9 us
    all_to_all x1, starting transfers between devices, body(): pieces = lax.all_to_all(pieces, SPACE, 0, 0, tiled=True)  11.3 us
    pallas_call x1, Pallas kernels, transform_of(): pl.pallas_call(transform_kernel, out_shape=jax.ShapeDtypeStruct(gram.shap...  10.9 us
    all_to_all x1, starting transfers between devices, body(): lax.all_to_all(picked, MEMBER, 0, 0, tiled=True).reshape(total, LANES)  10.2 us
    all_to_all x1, starting transfers between devices, sum_sent_to_all(): return lax.all_to_all(copies, axis, 0, 0, tiled=True)  9.08 us
    pallas_call x1, Pallas kernels, pick(): pl.pallas_call(pick_kernel, out_shape=jax.ShapeDtypeStruct((places.shape[...  6.84 us
  transfers between devices with their start and end apart: 11, of which 3 were waited for; matrix products, arithmetic and copies ran while one was open for 0% of the time, Pallas kernels for 8%

profile of v10, /device:TPU:1, one launch (start us, length us, event | category | flops | bytes accessed | tf_op | source)
XLA Modules:
  0.0 177.5 jit_solution(5542929666026648044)
XLA Ops:
  0.0 0.0 copy-start
  0.0 1.6 copy-done
  1.6 0.0 copy-start.2
  1.6 0.7 copy-done.2
  2.3 0.0 copy-start.1
  2.3 0.0 copy-start.4
  2.3 0.0 copy-start.5
  2.3 6.8 %shard_map.55 = f32[16,16,128]{2,1,0:T(8,128)} custom-call(s32[16,128]{1,0:T(8,128)S(1)} %copy-done.2, s32[16,128]{1,0:T(8,128)S(1)} %copy-done.2, f32[16,32768]{1,0:T(8,128)S(1)} %copy-done), custom_call_target="tpu_custom_call" | custom-call | flops 1024 | bytes 1024 | tf_op jit(solution)/shard_map/pallas_call | solution.py:54
  9.1 10.2 %all-to-all-start = ((f32[16,16,128]{2,1,0:T(8,128)}), f32[16,16,128]{2,1,0:T(8,128)S(1)}, u32[]{:S(2)}, u32[]{:S(2)}) async-start(f32[16,16,128]{2,1,0:T(8,128)} %shard_map.55), calls=%async_computation | async-start | bytes 262144 | tf_op jit(solution)/shard_map/all_to_all | solution.py:297
  19.3 0.0 copy-done.1
  19.3 1.1 shard_map.58
  20.4 2.1 %collective-permute-start = (f32[8,16,2048]{2,1,0:T(8,128)}, f32[8,16,2048]{2,1,0:T(8,128)S(1)}, u32[]{:S(2)}, u32[]{:S(2)}) collective-permute-start(f32[8,16,2048]{2,1,0:T(8,128)} %get-tuple-element.29), channel_id=1, source_target_pairs={{0,32},{32,0},{64,96},{96,64},{128,160},{160,128},{192,224},{224,1... | collective-permute-start | bytes 3145736 | tf_op jit(solution)/shard_map/ppermute | solution.py:223
  23.2 5.3 %all-to-all-done = f32[16,16,128]{2,1,0:T(8,128)S(1)} async-done(((f32[16,16,128]{2,1,0:T(8,128)}), f32[16,16,128]{2,1,0:T(8,128)S(1)}, u32[]{:S(2)}, u32[]{:S(2)}) %all-to-all-start) | async-done | bytes 131104 | tf_op jit(solution)/shard_map/all_to_all | solution.py:297
  28.5 0.0 copy-done.4
  28.5 0.0 copy-done.5
  28.5 1.2 shard_map.56
  29.7 11.3 %all-to-all-start.1 = ((f32[32,8,256]{2,1,0:T(8,128)}), f32[32,8,256]{2,1,0:T(8,128)S(1)}, u32[]{:S(2)}, u32[]{:S(2)}) async-start(f32[32,8,256]{2,1,0:T(8,128)} %bitcast.3), calls=%async_computation.1 | async-start | bytes 524288 | tf_op jit(solution)/shard_map/all_to_all | solution.py:308
  41.1 0.0 collective-permute-done.other_ref
  41.1 1.1 shard_map.59
  42.1 0.0 copy-start.3
  42.1 2.3 %collective-permute-start.1 = (f32[32,2048]{1,0:T(8,128)}, f32[32,2048]{1,0:T(8,128)S(1)}, u32[]{:S(2)}, u32[]{:S(2)}) collective-permute-start(f32[32,2048]{1,0:T(8,128)} %get-tuple-element.30), channel_id=1, source_target_pairs={{0,192},{32,224},{64,256},{96,288},{128,320},{160,352},{192,384},{... | collective-permute-start | bytes 786440 | tf_op jit(solution)/shard_map/ppermute | solution.py:230
  44.4 6.0 %collective-permute-start.2 = (f32[32,2048]{1,0:T(8,128)}, f32[32,2048]{1,0:T(8,128)S(1)}, u32[]{:S(2)}, u32[]{:S(2)}) collective-permute-start(f32[32,2048]{1,0:T(8,128)} %get-tuple-element.31), channel_id=1, source_target_pairs={{0,320},{32,352},{64,384},{96,416},{128,448},{160,480},{192,0},{22... | collective-permute-start | bytes 786440 | tf_op jit(solution)/shard_map/ppermute | solution.py:230
  50.4 2.1 %collective-permute-start.3 = (f32[32,2048]{1,0:T(8,128)}, f32[32,2048]{1,0:T(8,128)S(1)}, u32[]{:S(2)}, u32[]{:S(2)}) collective-permute-start(f32[32,2048]{1,0:T(8,128)} %get-tuple-element.32), channel_id=1, source_target_pairs={{0,128},{32,160},{64,192},{96,224},{128,256},{160,288},{192,320},{... | collective-permute-start | bytes 786440 | tf_op jit(solution)/shard_map/ppermute | solution.py:230
  52.5 5.3 %collective-permute-start.4 = (f32[32,2048]{1,0:T(8,128)S(1)}, f32[32,2048]{1,0:T(8,128)S(1)}, u32[]{:S(2)}, u32[]{:S(2)}) collective-permute-start(f32[32,2048]{1,0:T(8,128)S(1)} %get-tuple-element.33), channel_id=1, source_target_pairs={{0,384},{32,416},{64,448},{96,480},{128,0},{160,32},{192,64},{224,... | collective-permute-start | bytes 786440 | tf_op jit(solution)/shard_map/ppermute | solution.py:230
  57.8 0.0 all-to-all-done.1.parts_ref
  57.9 23.9 %all_to_all.25.parts_ref = f32[16,8,256]{2,1,0:T(8,128)S(1)} all-to-all(f32[16,8,256]{2,1,0:T(8,128)S(1)} %shard_map.57), channel_id=1, replica_groups=mesh['member'=16,'space'=32] {'member'}, dimensions={0} | all-to-all | bytes 262144 | tf_op jit(solution)/shard_map/all_to_all | solution.py:218
  81.8 0.0 collective-permute-done.1.refs_0_
  81.8 0.0 collective-permute-done.2.refs_1_
  81.8 0.0 collective-permute-done.3.refs_2_
  81.8 0.0 collective-permute-done.4.refs_3_
  81.8 0.7 shard_map.60
  82.5 0.0 copy-done.3
  82.5 9.1 %all-to-all-start.3 = ((f32[32,8,256]{2,1,0:T(8,128)}), f32[32,8,256]{2,1,0:T(8,128)S(1)}, u32[]{:S(2)}, u32[]{:S(2)}) async-start(f32[32,8,256]{2,1,0:T(8,128)} %shard_map.60), calls=%async_computation.3 | async-start | bytes 524288 | tf_op jit(solution)/shard_map/all_to_all | solution.py:218
  91.6 4.0 %collective-permute-start.5 = (f32[32,2048]{1,0:T(8,128)}, f32[32,2048]{1,0:T(8,128)S(1)}, u32[]{:S(2)}, u32[]{:S(2)}) collective-permute-start(f32[32,2048]{1,0:T(8,128)} %get-tuple-element.43), channel_id=1, source_target_pairs={{0,256},{32,288},{64,320},{96,352},{128,384},{160,416},{192,448},{... | collective-permute-start | bytes 786440 | tf_op jit(solution)/shard_map/ppermute | solution.py:230
  95.6 6.1 %collective-permute-start.6 = (f32[32,2048]{1,0:T(8,128)}, f32[32,2048]{1,0:T(8,128)S(1)}, u32[]{:S(2)}, u32[]{:S(2)}) collective-permute-start(f32[32,2048]{1,0:T(8,128)} %copy-done.3), channel_id=1, source_target_pairs={{0,64},{32,96},{64,128},{96,160},{128,192},{160,224},{192,256},{22... | collective-permute-start | bytes 786440 | tf_op jit(solution)/shard_map/ppermute | solution.py:230
  101.8 2.1 %collective-permute-start.7 = (f32[32,2048]{1,0:T(8,128)S(1)}, f32[32,2048]{1,0:T(8,128)S(1)}, u32[]{:S(2)}, u32[]{:S(2)}) collective-permute-start(f32[32,2048]{1,0:T(8,128)S(1)} %get-tuple-element.45), channel_id=1, source_target_pairs={{0,448},{32,480},{64,0},{96,32},{128,64},{160,96},{192,128},{224,1... | collective-permute-start | bytes 786440 | tf_op jit(solution)/shard_map/ppermute | solution.py:230
  103.9 0.0 all-to-all-done.3
  103.9 10.9 %shard_map.61.transform_ref = f32[256,256]{1,0:T(8,128)S(1)} custom-call(f32[256,256]{1,0:T(8,128)S(1)} %bitcast.11), custom_call_target="tpu_custom_call" | custom-call | flops 1024 | bytes 1024 | tf_op jit(solution)/shard_map/pallas_call | solution.py:165
  114.7 0.0 collective-permute-done.5.refs_4_
  114.7 2.2 %collective-permute-done.6.refs_5_ = f32[32,2048]{1,0:T(8,128)S(1)} collective-permute-done((f32[32,2048]{1,0:T(8,128)}, f32[32,2048]{1,0:T(8,128)S(1)}, u32[]{:S(2)}, u32[]{:S(2)}) %collective-permute-start.6) | collective-permute-done | bytes 262176 | tf_op jit(solution)/shard_map/ppermute | solution.py:230
  116.9 0.7 collective-permute-done.7.refs_6_
  117.6 2.1 %shard_map.62 = f32[256,2048]{1,0:T(8,128)S(1)} custom-call(s32[1]{0:T(128)} %bitcast.chip_ref, f32[256,256]{1,0:T(8,128)S(1)} %shard_map.61.transform_ref, f32[32,2048]{1,0:T(8,128)S(1)} %collective-permute-done.1.refs_0_, f32[32,2048]{1,0:T(8,128)S(1)} %collective-permute-done.2.refs_1_, f32[32,2048]{1,0:T(8,128)S(1)} %collective-permute-done.3.refs_2_, ...), custom_call_target="tpu_custom_call" | custom-call | flops 1024 | bytes 1024 | tf_op jit(solution)/shard_map/pallas_call | solution.py:190
  119.8 56.3 %all_to_all.26 = f32[16,16,2048]{2,1,0:T(8,128)S(1)} all-to-all(f32[16,16,2048]{2,1,0:T(8,128)S(1)} %bitcast.10), channel_id=1, replica_groups=mesh['member'=16,'space'=32] {'member'}, dimensions={0} | all-to-all | bytes 4194304 | tf_op jit(solution)/shard_map/all_to_all | solution.py:317
  176.1 1.5 copy.7
  (1 shorter events, 0.0 us)
Async XLA Ops:
  0.0 1.6 copy-start
  1.6 0.7 copy-start.2
  2.3 17.0 %copy-start.1 = (f32[16,32768]{1,0:T(8,128)S(1)}, f32[16,32768]{1,0:T(8,128)}, u32[]{:S(2)}) copy-start(f32[16,32768]{1,0:T(8,128)} %state_ref.2) | copy-start | bytes 6291460
  2.3 26.2 %copy-start.4 = (f32[16,128]{1,0:T(8,128)S(1)}, f32[16,128]{1,0:T(8,128)}, u32[]{:S(2)}) copy-start(f32[16,128]{1,0:T(8,128)} %data_ref.1) | copy-start | bytes 24580
  2.3 26.2 %copy-start.5 = (f32[16,128]{1,0:T(8,128)S(1)}, f32[16,128]{1,0:T(8,128)}, u32[]{:S(2)}) copy-start(f32[16,128]{1,0:T(8,128)} %sigma_ref.1) | copy-start | bytes 24580
  9.1 19.4 %all-to-all-start = ((f32[16,16,128]{2,1,0:T(8,128)}), f32[16,16,128]{2,1,0:T(8,128)S(1)}, u32[]{:S(2)}, u32[]{:S(2)}) async-start(f32[16,16,128]{2,1,0:T(8,128)} %shard_map.55), calls=%async_computation | async-start | bytes 262144 | tf_op jit(solution)/shard_map/all_to_all | solution.py:297
  20.4 20.6 %collective-permute-start = (f32[8,16,2048]{2,1,0:T(8,128)}, f32[8,16,2048]{2,1,0:T(8,128)S(1)}, u32[]{:S(2)}, u32[]{:S(2)}) collective-permute-start(f32[8,16,2048]{2,1,0:T(8,128)} %get-tuple-element.29), channel_id=1, source_target_pairs={{0,32},{32,0},{64,96},{96,64},{128,160},{160,128},{192,224},{224,1... | collective-permute-start | bytes 3145736 | tf_op jit(solution)/shard_map/ppermute | solution.py:223
  29.7 28.1 %all-to-all-start.1 = ((f32[32,8,256]{2,1,0:T(8,128)}), f32[32,8,256]{2,1,0:T(8,128)S(1)}, u32[]{:S(2)}, u32[]{:S(2)}) async-start(f32[32,8,256]{2,1,0:T(8,128)} %bitcast.3), calls=%async_computation.1 | async-start | bytes 524288 | tf_op jit(solution)/shard_map/all_to_all | solution.py:308
  42.1 40.4 %copy-start.3 = (f32[32,2048]{1,0:T(8,128)}, f32[32,2048]{1,0:T(8,128)S(1)}, u32[]{:S(2)}) copy-start(f32[32,2048]{1,0:T(8,128)S(1)} %get-tuple-element.44) | copy-start | bytes 786436
  42.1 39.6 %collective-permute-start.1 = (f32[32,2048]{1,0:T(8,128)}, f32[32,2048]{1,0:T(8,128)S(1)}, u32[]{:S(2)}, u32[]{:S(2)}) collective-permute-start(f32[32,2048]{1,0:T(8,128)} %get-tuple-element.30), channel_id=1, source_target_pairs={{0,192},{32,224},{64,256},{96,288},{128,320},{160,352},{192,384},{... | collective-permute-start | bytes 786440 | tf_op jit(solution)/shard_map/ppermute | solution.py:230
  44.4 37.4 %collective-permute-start.2 = (f32[32,2048]{1,0:T(8,128)}, f32[32,2048]{1,0:T(8,128)S(1)}, u32[]{:S(2)}, u32[]{:S(2)}) collective-permute-start(f32[32,2048]{1,0:T(8,128)} %get-tuple-element.31), channel_id=1, source_target_pairs={{0,320},{32,352},{64,384},{96,416},{128,448},{160,480},{192,0},{22... | collective-permute-start | bytes 786440 | tf_op jit(solution)/shard_map/ppermute | solution.py:230
  50.4 31.3 %collective-permute-start.3 = (f32[32,2048]{1,0:T(8,128)}, f32[32,2048]{1,0:T(8,128)S(1)}, u32[]{:S(2)}, u32[]{:S(2)}) collective-permute-start(f32[32,2048]{1,0:T(8,128)} %get-tuple-element.32), channel_id=1, source_target_pairs={{0,128},{32,160},{64,192},{96,224},{128,256},{160,288},{192,320},{... | collective-permute-start | bytes 786440 | tf_op jit(solution)/shard_map/ppermute | solution.py:230
  52.5 29.2 %collective-permute-start.4 = (f32[32,2048]{1,0:T(8,128)S(1)}, f32[32,2048]{1,0:T(8,128)S(1)}, u32[]{:S(2)}, u32[]{:S(2)}) collective-permute-start(f32[32,2048]{1,0:T(8,128)S(1)} %get-tuple-element.33), channel_id=1, source_target_pairs={{0,384},{32,416},{64,448},{96,480},{128,0},{160,32},{192,64},{224,... | collective-permute-start | bytes 786440 | tf_op jit(solution)/shard_map/ppermute | solution.py:230
  82.5 21.4 %all-to-all-start.3 = ((f32[32,8,256]{2,1,0:T(8,128)}), f32[32,8,256]{2,1,0:T(8,128)S(1)}, u32[]{:S(2)}, u32[]{:S(2)}) async-start(f32[32,8,256]{2,1,0:T(8,128)} %shard_map.60), calls=%async_computation.3 | async-start | bytes 524288 | tf_op jit(solution)/shard_map/all_to_all | solution.py:218
  91.6 23.1 %collective-permute-start.5 = (f32[32,2048]{1,0:T(8,128)}, f32[32,2048]{1,0:T(8,128)S(1)}, u32[]{:S(2)}, u32[]{:S(2)}) collective-permute-start(f32[32,2048]{1,0:T(8,128)} %get-tuple-element.43), channel_id=1, source_target_pairs={{0,256},{32,288},{64,320},{96,352},{128,384},{160,416},{192,448},{... | collective-permute-start | bytes 786440 | tf_op jit(solution)/shard_map/ppermute | solution.py:230
  95.6 21.3 %collective-permute-start.6 = (f32[32,2048]{1,0:T(8,128)}, f32[32,2048]{1,0:T(8,128)S(1)}, u32[]{:S(2)}, u32[]{:S(2)}) collective-permute-start(f32[32,2048]{1,0:T(8,128)} %copy-done.3), channel_id=1, source_target_pairs={{0,64},{32,96},{64,128},{96,160},{128,192},{160,224},{192,256},{22... | collective-permute-start | bytes 786440 | tf_op jit(solution)/shard_map/ppermute | solution.py:230
  101.8 15.8 %collective-permute-start.7 = (f32[32,2048]{1,0:T(8,128)S(1)}, f32[32,2048]{1,0:T(8,128)S(1)}, u32[]{:S(2)}, u32[]{:S(2)}) collective-permute-start(f32[32,2048]{1,0:T(8,128)S(1)} %get-tuple-element.45), channel_id=1, source_target_pairs={{0,448},{32,480},{64,0},{96,32},{128,64},{160,96},{192,128},{224,1... | collective-permute-start | bytes 786440 | tf_op jit(solution)/shard_map/ppermute | solution.py:230

commit v11 on v10

--- a/solution.py
+++ b/solution.py
@@ -12,8 +12,8 @@
 SPACE = "space"
 LANES = 128
 SUBLANES = 8
-FIRST = (3, 5, 2, 6)
-THEN = (4, 1, 7, 0)
+FIRST = (2, 6, 1, 7)
+THEN = (3, 5, 4, 0)
 IN_VMEM = pl.BlockSpec(memory_space=pltpu.VMEM)
 IN_SMEM = pl.BlockSpec(memory_space=pltpu.SMEM)
 KERNEL = pltpu.CompilerParams(vmem_limit_bytes=16 * 2**20)

time: 178 us -> 181 us (1.017)
  waiting for transfers between devices: 8.2 us -> 13 us
    all_to_all x1, blocking collectives: 23.9 us -> 14 us  [sum_sent_to_all(): return lax.all_to_all(copies, axis, 0, 0, tiled=True)]
    all_to_all x1, blocking collectives: 56.3 us -> 64.9 us  [body(): back = lax.all_to_all(updated, MEMBER, 0, 0, tiled=True)]
    ppermute x7, waiting for transfers between devices: 2.88 us -> 7.7 us  [shifted(): lax.ppermute(array, MEMBER, [(i, (i + 2 * k) % groups) for i in range(gro...]
where the time goes in v11:
time: 181 us; the launch traced here: 180 us
  blocking collectives  78.9 us (44%)
  starting transfers between devices  58.9 us (33%)
  Pallas kernels  23.9 us (13%)
  waiting for transfers between devices  13 us (7%)
  local copies, waits for them, and re-layouts  4.45 us (2%)
    all_to_all x1, blocking collectives, body(): back = lax.all_to_all(updated, MEMBER, 0, 0, tiled=True)  64.9 us
    ppermute x7, starting transfers between devices, shifted(): lax.ppermute(array, MEMBER, [(i, (i + 2 * k) % groups) for i in range(gro...  26.1 us
    all_to_all x1, blocking collectives, sum_sent_to_all(): return lax.all_to_all(copies, axis, 0, 0, tiled=True)  14 us
    all_to_all x1, starting transfers between devices, body(): pieces = lax.all_to_all(pieces, SPACE, 0, 0, tiled=True)  11.3 us
    pallas_call x1, Pallas kernels, transform_of(): pl.pallas_call(transform_kernel, out_shape=jax.ShapeDtypeStruct(gram.shap...  10.9 us
    all_to_all x1, starting transfers between devices, body(): lax.all_to_all(picked, MEMBER, 0, 0, tiled=True).reshape(total, LANES)  10.2 us
    all_to_all x1, starting transfers between devices, sum_sent_to_all(): return lax.all_to_all(copies, axis, 0, 0, tiled=True)  9.21 us
    ppermute x7, waiting for transfers between devices, shifted(): lax.ppermute(array, MEMBER, [(i, (i + 2 * k) % groups) for i in range(gro...  7.7 us
  transfers between devices with their start and end apart: 11, of which 3 were waited for; matrix products, arithmetic and copies ran while one was open for 0% of the time, Pallas kernels for 8%

profile of v11, /device:TPU:1, one launch (start us, length us, event | category | flops | bytes accessed | tf_op | source)
XLA Modules:
  0.0 180.1 jit_solution(6148819483316756070)
XLA Ops:
  0.0 0.0 copy-start
  0.0 1.6 copy-done
  1.6 0.0 copy-start.2
  1.6 0.7 copy-done.2
  2.3 0.0 copy-start.1
  2.3 0.0 copy-start.4
  2.3 0.0 copy-start.5
  2.3 6.8 %shard_map.55 = f32[16,16,128]{2,1,0:T(8,128)} custom-call(s32[16,128]{1,0:T(8,128)S(1)} %copy-done.2, s32[16,128]{1,0:T(8,128)S(1)} %copy-done.2, f32[16,32768]{1,0:T(8,128)S(1)} %copy-done), custom_call_target="tpu_custom_call" | custom-call | flops 1024 | bytes 1024 | tf_op jit(solution)/shard_map/pallas_call | solution.py:54
  9.1 10.2 %all-to-all-start = ((f32[16,16,128]{2,1,0:T(8,128)}), f32[16,16,128]{2,1,0:T(8,128)S(1)}, u32[]{:S(2)}, u32[]{:S(2)}) async-start(f32[16,16,128]{2,1,0:T(8,128)} %shard_map.55), calls=%async_computation | async-start | bytes 262144 | tf_op jit(solution)/shard_map/all_to_all | solution.py:297
  19.3 0.0 copy-done.1
  19.3 1.1 shard_map.58
  20.4 2.1 %collective-permute-start = (f32[8,16,2048]{2,1,0:T(8,128)}, f32[8,16,2048]{2,1,0:T(8,128)S(1)}, u32[]{:S(2)}, u32[]{:S(2)}) collective-permute-start(f32[8,16,2048]{2,1,0:T(8,128)} %get-tuple-element.29), channel_id=1, source_target_pairs={{0,32},{32,0},{64,96},{96,64},{128,160},{160,128},{192,224},{224,1... | collective-permute-start | bytes 3145736 | tf_op jit(solution)/shard_map/ppermute | solution.py:223
  23.2 5.3 %all-to-all-done = f32[16,16,128]{2,1,0:T(8,128)S(1)} async-done(((f32[16,16,128]{2,1,0:T(8,128)}), f32[16,16,128]{2,1,0:T(8,128)S(1)}, u32[]{:S(2)}, u32[]{:S(2)}) %all-to-all-start) | async-done | bytes 131104 | tf_op jit(solution)/shard_map/all_to_all | solution.py:297
  28.5 0.0 copy-done.4
  28.5 0.0 copy-done.5
  28.5 1.2 shard_map.56
  29.7 11.3 %all-to-all-start.1 = ((f32[32,8,256]{2,1,0:T(8,128)}), f32[32,8,256]{2,1,0:T(8,128)S(1)}, u32[]{:S(2)}, u32[]{:S(2)}) async-start(f32[32,8,256]{2,1,0:T(8,128)} %bitcast.3), calls=%async_computation.1 | async-start | bytes 524288 | tf_op jit(solution)/shard_map/all_to_all | solution.py:308
  41.1 0.0 collective-permute-done.other_ref
  41.1 1.0 shard_map.59
  42.0 0.0 copy-start.3
  42.0 0.7 copy-done.3
  42.7 2.1 %collective-permute-start.1 = (f32[32,2048]{1,0:T(8,128)}, f32[32,2048]{1,0:T(8,128)S(1)}, u32[]{:S(2)}, u32[]{:S(2)}) collective-permute-start(f32[32,2048]{1,0:T(8,128)} %get-tuple-element.30), channel_id=1, source_target_pairs={{0,128},{32,160},{64,192},{96,224},{128,256},{160,288},{192,320},{... | collective-permute-start | bytes 786440 | tf_op jit(solution)/shard_map/ppermute | solution.py:230
  44.8 5.3 %collective-permute-start.2 = (f32[32,2048]{1,0:T(8,128)}, f32[32,2048]{1,0:T(8,128)S(1)}, u32[]{:S(2)}, u32[]{:S(2)}) collective-permute-start(f32[32,2048]{1,0:T(8,128)} %get-tuple-element.31), channel_id=1, source_target_pairs={{0,384},{32,416},{64,448},{96,480},{128,0},{160,32},{192,64},{224,... | collective-permute-start | bytes 786440 | tf_op jit(solution)/shard_map/ppermute | solution.py:230
  50.1 2.0 %collective-permute-start.3 = (f32[32,2048]{1,0:T(8,128)S(1)}, f32[32,2048]{1,0:T(8,128)S(1)}, u32[]{:S(2)}, u32[]{:S(2)}) collective-permute-start(f32[32,2048]{1,0:T(8,128)S(1)} %get-tuple-element.32), channel_id=1, source_target_pairs={{0,64},{32,96},{64,128},{96,160},{128,192},{160,224},{192,256},{22... | collective-permute-start | bytes 786440 | tf_op jit(solution)/shard_map/ppermute | solution.py:230
  52.1 4.5 %collective-permute-start.4 = (f32[32,2048]{1,0:T(8,128)S(1)}, f32[32,2048]{1,0:T(8,128)S(1)}, u32[]{:S(2)}, u32[]{:S(2)}) collective-permute-start(f32[32,2048]{1,0:T(8,128)S(1)} %get-tuple-element.33), channel_id=1, source_target_pairs={{0,448},{32,480},{64,0},{96,32},{128,64},{160,96},{192,128},{224,1... | collective-permute-start | bytes 786440 | tf_op jit(solution)/shard_map/ppermute | solution.py:230
  56.6 0.0 all-to-all-done.1.parts_ref
  56.7 14.0 %all_to_all.25.parts_ref = f32[16,8,256]{2,1,0:T(8,128)S(1)} all-to-all(f32[16,8,256]{2,1,0:T(8,128)S(1)} %shard_map.57), channel_id=1, replica_groups=mesh['member'=16,'space'=32] {'member'}, dimensions={0} | all-to-all | bytes 262144 | tf_op jit(solution)/shard_map/all_to_all | solution.py:218
  70.7 0.0 collective-permute-done.1.refs_0_
  70.7 0.0 collective-permute-done.2.refs_1_
  70.7 0.0 collective-permute-done.3.refs_2_
  70.7 0.0 collective-permute-done.4.refs_3_
  70.8 0.7 shard_map.60
  71.5 9.2 %all-to-all-start.3 = ((f32[32,8,256]{2,1,0:T(8,128)}), f32[32,8,256]{2,1,0:T(8,128)S(1)}, u32[]{:S(2)}, u32[]{:S(2)}) async-start(f32[32,8,256]{2,1,0:T(8,128)} %shard_map.60), calls=%async_computation.3 | async-start | bytes 524288 | tf_op jit(solution)/shard_map/all_to_all | solution.py:218
  80.7 3.7 %collective-permute-start.5 = (f32[32,2048]{1,0:T(8,128)}, f32[32,2048]{1,0:T(8,128)S(1)}, u32[]{:S(2)}, u32[]{:S(2)}) collective-permute-start(f32[32,2048]{1,0:T(8,128)} %get-tuple-element.43), channel_id=1, source_target_pairs={{0,192},{32,224},{64,256},{96,288},{128,320},{160,352},{192,384},{... | collective-permute-start | bytes 786440 | tf_op jit(solution)/shard_map/ppermute | solution.py:230
  84.4 4.6 %collective-permute-start.6 = (f32[32,2048]{1,0:T(8,128)}, f32[32,2048]{1,0:T(8,128)S(1)}, u32[]{:S(2)}, u32[]{:S(2)}) collective-permute-start(f32[32,2048]{1,0:T(8,128)} %copy-done.3), channel_id=1, source_target_pairs={{0,320},{32,352},{64,384},{96,416},{128,448},{160,480},{192,0},{22... | collective-permute-start | bytes 786440 | tf_op jit(solution)/shard_map/ppermute | solution.py:230
  89.0 4.0 %collective-permute-start.7 = (f32[32,2048]{1,0:T(8,128)S(1)}, f32[32,2048]{1,0:T(8,128)S(1)}, u32[]{:S(2)}, u32[]{:S(2)}) collective-permute-start(f32[32,2048]{1,0:T(8,128)S(1)} %get-tuple-element.45), channel_id=1, source_target_pairs={{0,256},{32,288},{64,320},{96,352},{128,384},{160,416},{192,448},{... | collective-permute-start | bytes 786440 | tf_op jit(solution)/shard_map/ppermute | solution.py:230
  93.0 0.0 all-to-all-done.3
  93.0 10.9 %shard_map.61.transform_ref = f32[256,256]{1,0:T(8,128)S(1)} custom-call(f32[256,256]{1,0:T(8,128)S(1)} %bitcast.11), custom_call_target="tpu_custom_call" | custom-call | flops 1024 | bytes 1024 | tf_op jit(solution)/shard_map/pallas_call | solution.py:165
  103.9 0.0 collective-permute-done.5.refs_4_
  103.9 2.4 %collective-permute-done.6.refs_5_ = f32[32,2048]{1,0:T(8,128)S(1)} collective-permute-done((f32[32,2048]{1,0:T(8,128)}, f32[32,2048]{1,0:T(8,128)S(1)}, u32[]{:S(2)}, u32[]{:S(2)}) %collective-permute-start.6) | collective-permute-done | bytes 262176 | tf_op jit(solution)/shard_map/ppermute | solution.py:230
  106.3 5.3 %collective-permute-done.7.refs_6_ = f32[32,2048]{1,0:T(8,128)S(1)} collective-permute-done((f32[32,2048]{1,0:T(8,128)S(1)}, f32[32,2048]{1,0:T(8,128)S(1)}, u32[]{:S(2)}, u32[]{:S(2)}) %collective-permute-start.7) | collective-permute-done | bytes 262176 | tf_op jit(solution)/shard_map/ppermute | solution.py:230
  111.6 2.1 %shard_map.62 = f32[256,2048]{1,0:T(8,128)S(1)} custom-call(s32[1]{0:T(128)} %bitcast.chip_ref, f32[256,256]{1,0:T(8,128)S(1)} %shard_map.61.transform_ref, f32[32,2048]{1,0:T(8,128)S(1)} %collective-permute-done.1.refs_0_, f32[32,2048]{1,0:T(8,128)S(1)} %collective-permute-done.2.refs_1_, f32[32,2048]{1,0:T(8,128)S(1)} %collective-permute-done.3.refs_2_, ...), custom_call_target="tpu_custom_call" | custom-call | flops 1024 | bytes 1024 | tf_op jit(solution)/shard_map/pallas_call | solution.py:190
  113.7 64.9 %all_to_all.26 = f32[16,16,2048]{2,1,0:T(8,128)S(1)} all-to-all(f32[16,16,2048]{2,1,0:T(8,128)S(1)} %bitcast.10), channel_id=1, replica_groups=mesh['member'=16,'space'=32] {'member'}, dimensions={0} | all-to-all | bytes 4194304 | tf_op jit(solution)/shard_map/all_to_all | solution.py:317
  178.6 1.5 copy.7
  (1 shorter events, 0.0 us)
Async XLA Ops:
  0.0 1.6 copy-start
  1.6 0.7 copy-start.2
  2.3 17.0 %copy-start.1 = (f32[16,32768]{1,0:T(8,128)S(1)}, f32[16,32768]{1,0:T(8,128)}, u32[]{:S(2)}) copy-start(f32[16,32768]{1,0:T(8,128)} %state_ref.2) | copy-start | bytes 6291460
  2.3 26.2 %copy-start.4 = (f32[16,128]{1,0:T(8,128)S(1)}, f32[16,128]{1,0:T(8,128)}, u32[]{:S(2)}) copy-start(f32[16,128]{1,0:T(8,128)} %data_ref.1) | copy-start | bytes 24580
  2.3 26.2 %copy-start.5 = (f32[16,128]{1,0:T(8,128)S(1)}, f32[16,128]{1,0:T(8,128)}, u32[]{:S(2)}) copy-start(f32[16,128]{1,0:T(8,128)} %sigma_ref.1) | copy-start | bytes 24580
  9.1 19.4 %all-to-all-start = ((f32[16,16,128]{2,1,0:T(8,128)}), f32[16,16,128]{2,1,0:T(8,128)S(1)}, u32[]{:S(2)}, u32[]{:S(2)}) async-start(f32[16,16,128]{2,1,0:T(8,128)} %shard_map.55), calls=%async_computation | async-start | bytes 262144 | tf_op jit(solution)/shard_map/all_to_all | solution.py:297
  20.4 20.6 %collective-permute-start = (f32[8,16,2048]{2,1,0:T(8,128)}, f32[8,16,2048]{2,1,0:T(8,128)S(1)}, u32[]{:S(2)}, u32[]{:S(2)}) collective-permute-start(f32[8,16,2048]{2,1,0:T(8,128)} %get-tuple-element.29), channel_id=1, source_target_pairs={{0,32},{32,0},{64,96},{96,64},{128,160},{160,128},{192,224},{224,1... | collective-permute-start | bytes 3145736 | tf_op jit(solution)/shard_map/ppermute | solution.py:223
  29.7 26.9 %all-to-all-start.1 = ((f32[32,8,256]{2,1,0:T(8,128)}), f32[32,8,256]{2,1,0:T(8,128)S(1)}, u32[]{:S(2)}, u32[]{:S(2)}) async-start(f32[32,8,256]{2,1,0:T(8,128)} %bitcast.3), calls=%async_computation.1 | async-start | bytes 524288 | tf_op jit(solution)/shard_map/all_to_all | solution.py:308
  42.0 0.7 copy-start.3
  42.7 28.0 %collective-permute-start.1 = (f32[32,2048]{1,0:T(8,128)}, f32[32,2048]{1,0:T(8,128)S(1)}, u32[]{:S(2)}, u32[]{:S(2)}) collective-permute-start(f32[32,2048]{1,0:T(8,128)} %get-tuple-element.30), channel_id=1, source_target_pairs={{0,128},{32,160},{64,192},{96,224},{128,256},{160,288},{192,320},{... | collective-permute-start | bytes 786440 | tf_op jit(solution)/shard_map/ppermute | solution.py:230
  44.8 25.9 %collective-permute-start.2 = (f32[32,2048]{1,0:T(8,128)}, f32[32,2048]{1,0:T(8,128)S(1)}, u32[]{:S(2)}, u32[]{:S(2)}) collective-permute-start(f32[32,2048]{1,0:T(8,128)} %get-tuple-element.31), channel_id=1, source_target_pairs={{0,384},{32,416},{64,448},{96,480},{128,0},{160,32},{192,64},{224,... | collective-permute-start | bytes 786440 | tf_op jit(solution)/shard_map/ppermute | solution.py:230
  50.1 20.6 %collective-permute-start.3 = (f32[32,2048]{1,0:T(8,128)S(1)}, f32[32,2048]{1,0:T(8,128)S(1)}, u32[]{:S(2)}, u32[]{:S(2)}) collective-permute-start(f32[32,2048]{1,0:T(8,128)S(1)} %get-tuple-element.32), channel_id=1, source_target_pairs={{0,64},{32,96},{64,128},{96,160},{128,192},{160,224},{192,256},{22... | collective-permute-start | bytes 786440 | tf_op jit(solution)/shard_map/ppermute | solution.py:230
  52.1 18.6 %collective-permute-start.4 = (f32[32,2048]{1,0:T(8,128)S(1)}, f32[32,2048]{1,0:T(8,128)S(1)}, u32[]{:S(2)}, u32[]{:S(2)}) collective-permute-start(f32[32,2048]{1,0:T(8,128)S(1)} %get-tuple-element.33), channel_id=1, source_target_pairs={{0,448},{32,480},{64,0},{96,32},{128,64},{160,96},{192,128},{224,1... | collective-permute-start | bytes 786440 | tf_op jit(solution)/shard_map/ppermute | solution.py:230
  71.5 21.5 %all-to-all-start.3 = ((f32[32,8,256]{2,1,0:T(8,128)}), f32[32,8,256]{2,1,0:T(8,128)S(1)}, u32[]{:S(2)}, u32[]{:S(2)}) async-start(f32[32,8,256]{2,1,0:T(8,128)} %shard_map.60), calls=%async_computation.3 | async-start | bytes 524288 | tf_op jit(solution)/shard_map/all_to_all | solution.py:218
  80.7 23.1 %collective-permute-start.5 = (f32[32,2048]{1,0:T(8,128)}, f32[32,2048]{1,0:T(8,128)S(1)}, u32[]{:S(2)}, u32[]{:S(2)}) collective-permute-start(f32[32,2048]{1,0:T(8,128)} %get-tuple-element.43), channel_id=1, source_target_pairs={{0,192},{32,224},{64,256},{96,288},{128,320},{160,352},{192,384},{... | collective-permute-start | bytes 786440 | tf_op jit(solution)/shard_map/ppermute | solution.py:230
  84.4 21.9 %collective-permute-start.6 = (f32[32,2048]{1,0:T(8,128)}, f32[32,2048]{1,0:T(8,128)S(1)}, u32[]{:S(2)}, u32[]{:S(2)}) collective-permute-start(f32[32,2048]{1,0:T(8,128)} %copy-done.3), channel_id=1, source_target_pairs={{0,320},{32,352},{64,384},{96,416},{128,448},{160,480},{192,0},{22... | collective-permute-start | bytes 786440 | tf_op jit(solution)/shard_map/ppermute | solution.py:230
  89.0 22.5 %collective-permute-start.7 = (f32[32,2048]{1,0:T(8,128)S(1)}, f32[32,2048]{1,0:T(8,128)S(1)}, u32[]{:S(2)}, u32[]{:S(2)}) collective-permute-start(f32[32,2048]{1,0:T(8,128)S(1)} %get-tuple-element.45), channel_id=1, source_target_pairs={{0,256},{32,288},{64,320},{96,352},{128,384},{160,416},{192,448},{... | collective-permute-start | bytes 786440 | tf_op jit(solution)/shard_map/ppermute | solution.py:230
